TPU v7x, 512 devices: a whole 4x4x16 slice. The times are simulated.
512 devices in a mesh: dp: 8 (over x, core), space: 64 (over z, y).
Axes of the slice: x: 4, y: 4, z: 16, core: 2. Of those that a mesh axis runs over, the one named last changes fastest.
Arguments:
- features: bfloat16 [8, 8192, 256], P('dp', 'space'), may hold values from -6 to 6
- fractional: float32 [8, 3, 8192], P('dp', None, 'space'), may hold values from 0 to 1, as said below
- counts: int32 [8, 64], P('dp', 'space'), may hold values from 64 to 128, as said below
- neighbor_index: int32 [8, 8192, 32], P('dp', 'space'), may hold values from 0 to 191, as said below
- neighbor_count: int32 [8, 8192], P('dp', 'space'), may hold values from 8 to 32, as said below
- send_list: int32 [8, 64, 2, 32], P('dp', 'space'), may hold values from 0 to 127, as said below
- distances: float32 [8, 8192, 32], P('dp', 'space'), may hold values from 0.5 to 5
- wave_index: int32 [3, 512], replicated, may hold values from -4 to 4, as said below
- w_message: bfloat16 [256, 256], replicated, may hold values from -0.375 to 0.375
- w_filter: bfloat16 [20, 256], replicated, may hold values from -1.25 to 1.25
- w_charge: bfloat16 [256, 256], replicated, may hold values from -0.375 to 0.375
- w_kspace: bfloat16 [20, 256], replicated, may hold values from -1.25 to 1.25
- cotangent: bfloat16 [8, 8192, 256], P('dp', 'space'), may hold values from -6 to 6
Outputs:
- updated: bfloat16 [8, 8192, 256], P('dp', 'space')
- grad_features: float32 [8, 8192, 256], P('dp', 'space')
- grad_message: float32 [256, 256], replicated
- grad_charge: float32 [256, 256], replicated
- grad_filter: float32 [20, 256], replicated
- grad_kspace: float32 [20, 256], replicated
Inputs may be any that keep to these rules, and one draw needn't show every extreme that they name: `counts`: in every slab one domain holds exactly 128 live atoms and another exactly 64. `send_list`: entries of a domain's lists are rows of that domain below its count. `neighbor_index`: entries below 128 are below the domain's count. `neighbor_count`: the first atom row of every domain uses all 32 slots. `fractional`: the first coordinate of domain d's rows lies in [d / 64, (d + 1) / 64]. `wave_index`: no wave vector is zero.
All inputs are finite; a program needn't handle non-finite values.
Results may differ from a plain program's by a relative error of at most 0.0069.
Values may be sent and summed in bfloat16 or wider, within the bound.
No kernel may reach another device: no remote copies, remote signals or barrier semaphores. Data moves between devices by JAX's collectives and lax.ppermute only.
A program may use at most 64 MiB of HBM per device.

v0:
```python
import math

import jax
import jax.numpy as jnp
from jax import lax
from jax.sharding import PartitionSpec as P

cutoff_radius = 5.0
kspace_limit = 8.0 * math.pi * math.sqrt(3.0)
ewald_scale_factor = 4.0
two_pi = 2.0 * math.pi


def passed_along(value, axis, steps):
    count = lax.axis_size(axis)
    pairs = [(source, (source + steps) % count) for source in range(count)]
    return lax.ppermute(value, axis, pairs)


def smooth_basis(values, count_bins, width):
    centers = width * jnp.arange(count_bins).astype(jnp.float32) / (count_bins - 1)
    spacing = width / (count_bins - 1)
    scaled = (values[None, :] - centers[:, None]) / spacing
    return jnp.exp(-0.5 * scaled * scaled)


def radial_basis(lengths, count_bins):
    envelope = 0.5 * (jnp.cos(math.pi * lengths / cutoff_radius) + 1.0)
    return (smooth_basis(lengths, count_bins, cutoff_radius) * envelope[None, :]).astype(
        jnp.bfloat16
    )


def contract_rows(left, right):
    return lax.dot_general(
        left, right, (((0,), (0,)), ((), ())), preferred_element_type=jnp.float32
    )


def trig_tables(coords, wave_index):
    wave_float = wave_index.astype(jnp.float32)
    phase_angle = (
        coords[0][:, None] * wave_float[0][None, :] + coords[1][:, None] * wave_float[1][None, :]
    )
    phase_angle = (phase_angle + coords[2][:, None] * wave_float[2][None, :]) * two_pi
    return (jnp.cos(phase_angle).astype(jnp.bfloat16), jnp.sin(phase_angle).astype(jnp.bfloat16))


def kspace_filter(wave_index, w_kspace):
    wave_float = wave_index.astype(jnp.float32)
    squares = (
        wave_float[0] * wave_float[0]
        + wave_float[1] * wave_float[1]
        + wave_float[2] * wave_float[2]
    )
    wave_norm = two_pi * jnp.sqrt(squares)
    wave_basis = smooth_basis(wave_norm, w_kspace.shape[0], kspace_limit).astype(jnp.bfloat16)
    return (wave_basis, contract_rows(wave_basis, w_kspace))


def silu_derivative(values):
    sigma_values = jax.nn.sigmoid(values)
    return sigma_values * (1.0 + values * (1.0 - sigma_values))


def body(
    features,
    fractional,
    counts,
    neighbor_index,
    neighbor_count,
    send_list,
    distances,
    wave_index,
    w_message,
    w_filter,
    w_charge,
    w_kspace,
    cotangent,
):
    own_features = features[0]
    atoms_here, channels = own_features.shape
    slots_per = neighbor_index.shape[2]
    ghost_rows = send_list.shape[3]
    count_bins = w_filter.shape[0]
    wave_total = wave_index.shape[1]
    domains_here = lax.axis_size("space")
    ewald_coefficient = ewald_scale_factor / math.sqrt(atoms_here * domains_here * wave_total)
    live_rows = (jnp.arange(atoms_here) < counts[0, 0]).astype(jnp.float32)[:, None]
    slot_live = live_rows * (jnp.arange(slots_per)[None, :] < neighbor_count[0][:, None]).astype(
        jnp.float32
    )
    hidden_pre = jnp.dot(own_features, w_message, preferred_element_type=jnp.float32)
    activated = jax.nn.silu(hidden_pre).astype(jnp.bfloat16)
    lists_down = send_list[0, 0, 0]
    lists_up = send_list[0, 0, 1]
    from_lower = passed_along(activated[lists_up], "space", 1)
    from_upper = passed_along(activated[lists_down], "space", -1)
    extended = jnp.concatenate([activated, from_lower, from_upper], axis=0)
    block_rows = min(64, atoms_here)
    count_blocks = atoms_here // block_rows
    index_blocks = neighbor_index[0].reshape(count_blocks, block_rows * slots_per)
    live_blocks = slot_live.reshape(count_blocks, block_rows * slots_per)
    length_blocks = distances[0].reshape(count_blocks, block_rows * slots_per)
    charge = (
        live_rows * jnp.dot(own_features, w_charge, preferred_element_type=jnp.float32)
    ).astype(jnp.bfloat16)
    cosines, sines = trig_tables(fractional[0], wave_index)
    wave_basis, wave_filter = kspace_filter(wave_index, w_kspace)
    factor_cos, sine_factor = lax.psum(
        (contract_rows(cosines, charge), contract_rows(sines, charge)), "space"
    )
    weight_cos = (ewald_coefficient * wave_filter * factor_cos).astype(jnp.bfloat16)
    weight_sin = (ewald_coefficient * wave_filter * sine_factor).astype(jnp.bfloat16)

    def forward_block(pieces):
        index_piece, live_piece, length_piece = pieces
        edge_weights = contract_rows(radial_basis(length_piece, count_bins), w_filter)
        gathered = extended[index_piece].astype(jnp.float32)
        summed = (live_piece[:, None] * edge_weights * gathered).reshape(
            block_rows, slots_per, channels
        )
        return jnp.sum(summed, axis=1)

    messages = lax.map(forward_block, (index_blocks, live_blocks, length_blocks)).reshape(
        atoms_here, channels
    )
    ewald = jnp.dot(cosines, weight_cos, preferred_element_type=jnp.float32) + jnp.dot(
        sines, weight_sin, preferred_element_type=jnp.float32
    )
    updated = (own_features.astype(jnp.float32) + live_rows * (messages + ewald)).astype(
        jnp.bfloat16
    )
    own_cot = cotangent[0]
    masked = jnp.where(live_rows > 0.0, own_cot, jnp.zeros_like(own_cot))
    adjoint_cos, adjoint_sin = lax.psum(
        (contract_rows(cosines, masked), contract_rows(sines, masked)), "space"
    )
    filter_grad = ewald_coefficient * (factor_cos * adjoint_cos + sine_factor * adjoint_sin)
    kspace_term = jnp.dot(
        wave_basis.astype(jnp.float32),
        filter_grad,
        precision=lax.Precision.HIGHEST,
        preferred_element_type=jnp.float32,
    )
    pushed_cos = (ewald_coefficient * wave_filter * adjoint_cos).astype(jnp.bfloat16)
    pushed_sin = (ewald_coefficient * wave_filter * adjoint_sin).astype(jnp.bfloat16)
    charge_grad = (
        live_rows
        * (
            jnp.dot(cosines, pushed_cos, preferred_element_type=jnp.float32)
            + jnp.dot(sines, pushed_sin, preferred_element_type=jnp.float32)
        )
    ).astype(jnp.bfloat16)
    charge_term = contract_rows(own_features, charge_grad)
    cot_blocks = masked.reshape(count_blocks, block_rows, channels)

    def backward_block(running, pieces):
        ext_grad, filter_term = running
        index_piece, live_piece, length_piece, cot_piece = pieces
        basis = radial_basis(length_piece, count_bins)
        edge_weights = contract_rows(basis, w_filter)
        gathered = extended[index_piece].astype(jnp.float32)
        edge_cot = jnp.broadcast_to(cot_piece[:, None, :], (block_rows, slots_per, channels))
        weighted = live_piece[:, None] * edge_cot.reshape(block_rows * slots_per, channels).astype(
            jnp.float32
        )
        edge_grad = (weighted * gathered).astype(jnp.bfloat16)
        filter_term = filter_term + jnp.dot(basis, edge_grad, preferred_element_type=jnp.float32)
        ext_grad = ext_grad.at[index_piece].add(weighted * edge_weights)
        return ((ext_grad, filter_term), None)

    initial = (
        jnp.zeros((atoms_here + 2 * ghost_rows, channels), jnp.float32),
        jnp.zeros((count_bins, channels), jnp.float32),
    )
    (ext_grad, filter_term), unused = lax.scan(
        backward_block, initial, (index_blocks, live_blocks, length_blocks, cot_blocks)
    )
    back_upper = passed_along(
        ext_grad[atoms_here : atoms_here + ghost_rows].astype(jnp.bfloat16), "space", -1
    ).astype(jnp.float32)
    back_lower = passed_along(
        ext_grad[atoms_here + ghost_rows :].astype(jnp.bfloat16), "space", 1
    ).astype(jnp.float32)
    act_grad = ext_grad[:atoms_here].at[lists_up].add(back_upper).at[lists_down].add(back_lower)
    pre_grad = (act_grad * silu_derivative(hidden_pre)).astype(jnp.bfloat16)
    message_term = contract_rows(own_features, pre_grad)
    back_dims = (((1,), (1,)), ((), ()))
    grad_features = (
        own_cot.astype(jnp.float32)
        + lax.dot_general(pre_grad, w_message, back_dims, preferred_element_type=jnp.float32)
        + lax.dot_general(charge_grad, w_charge, back_dims, preferred_element_type=jnp.float32)
    )
    grad_kspace = lax.psum(kspace_term, "dp")
    grad_message, grad_charge, grad_filter = lax.psum(
        (message_term, charge_term, filter_term), ("dp", "space")
    )
    return (updated[None], grad_features[None], grad_message, grad_charge, grad_filter, grad_kspace)


def solution(mesh):
    placed = (
        P("dp", "space", None),
        P("dp", None, "space"),
        P("dp", "space"),
        P("dp", "space", None),
        P("dp", "space"),
        P("dp", "space", None, None),
        P("dp", "space", None),
        P(),
        P(),
        P(),
        P(),
        P(),
        P("dp", "space", None),
    )
    return jax.shard_map(
        body,
        mesh=mesh,
        in_specs=placed,
        out_specs=(P("dp", "space", None), P("dp", "space", None), P(), P(), P(), P()),
        check_vma=False,
    )
```

profile of v0, /device:TPU:1, one launch (start us, length us, event | category | flops | bytes accessed | tf_op | source)
XLA Modules:
  0.0 806.2 jit_solution(4355718209116518734)
XLA Ops:
  7.2 0.8 fusion.56
  8.0 0.6 copy-done.29
  8.6 1.0 multiply_convert_fusion.11
  9.6 0.6 gather_fusion.2
  10.2 4.0 collective-permute-start
  14.3 0.6 gather_fusion.3
  14.9 12.3 %collective-permute-start.1 = (bf16[32,256]{1,0:T(8,128)(2,1)S(1)}, bf16[32,256]{1,0:T(8,128)(2,1)S(1)}, u32[]{:S(2)}, u32[]{:S(2)}) collective-permute-start(bf16[32,256]{1,0:T(8,128)(2,1)S(1)} %gather_fusion.3), channel_id=1, source_target_pairs={{0,63},{1,0},{2,1},{3,2},{4,3},{5,4},{6,5},{7,6},{8,7},{9,8},{10,9... | collective-permute-start | bytes 49160 | tf_op jit(solution)/shard_map/ppermute | solution.py:17
  27.9 0.7 slice_bitcast_fusion.2
  28.6 0.7 convert_element_type.144
  29.4 1.1 fusion.30
  30.5 2.0 fusion.66
  32.5 2.0 fusion.65
  34.5 2.0 fusion.52
  36.5 2.0 fusion.53
  38.7 0.5 broadcast.288
  39.2 0.6 reduce.3
  41.4 41.7 %while.28 = (s32[]{:T(128)}, f32[192,256]{1,0:T(8,128)S(1)}, f32[20,256]{1,0:T(8,128)S(1)}, s32[2,2048]{1,0:T(2,128)S(1)}, f32[2,2048]{1,0:T(2,128)S(1)}, /*inde...) while((s32[]{:T(128)}, f32[192,256]{1,0:T(8,128)S(1)}, ...), condition=%wide.region_7.8_spmd.clone, body=%wide.region_5.7_spmd.clone.sunk | while | flops 45621288 | bytes 18172284 | solution.py:177
  41.7 7.5 gather_fusion.1
  49.6 0.4 convolution_add_fusion.6
  50.0 0.6 convolution_multiply_fusion.5
  50.6 11.7 %scatter_fusion = f32[192,256]{1,0:T(8,128)S(1)} fusion(f32[192,256]{1,0:T(8,128)S(1)} %get-tuple-element.461, s32[2048]{0:T(1024)S(1)} %bitcast.121, f32[2048,256]{1,0:T(8,128)S(1)} %convolution_multiply_fusion.5), kind=kCustom, calls=%fused_computation.4.clone.clone.1 | custom fusion | flops 524288 | bytes 6299648 | tf_op jit(solution)/shard_map/while/body/eval_jaxpr/scatter-add | solution.py:170
  62.6 7.5 gather_fusion.1
  70.4 0.4 convolution_add_fusion.6
  70.9 0.6 convolution_multiply_fusion.5
  71.4 11.7 %scatter_fusion = f32[192,256]{1,0:T(8,128)S(1)} fusion(f32[192,256]{1,0:T(8,128)S(1)} %get-tuple-element.461, s32[2048]{0:T(1024)S(1)} %bitcast.121, f32[2048,256]{1,0:T(8,128)S(1)} %convolution_multiply_fusion.5), kind=kCustom, calls=%fused_computation.4.clone.clone.1 | custom fusion | flops 524288 | bytes 6299648 | tf_op jit(solution)/shard_map/while/body/eval_jaxpr/scatter-add | solution.py:170
  83.1 1.9 collective-permute-start.3
  85.1 6.7 collective-permute-start.2
  91.8 17.2 %while.27 = (s32[]{:T(128)}, f32[2,64,256]{2,1,0:T(8,128)S(1)}, f32[2,2048]{1,0:T(2,128)S(1)}, f32[2,2048]{1,0:T(2,128)S(1)}, bf16[20,256]{1,0:T(8,128)(2,1)S(1)...) while((s32[]{:T(128)}, f32[2,64,256]{2,1,0:T(8,128)S(1)}, f32[2,2048]{1,0:T(2,128)S(1)}, ...), condition=%wide.region_2.3_spmd, body=%wide.region_0.0_spmd.sunk | while | flops 23312424 | bytes 3459337 | solution.py:125
  92.2 7.5 gather_fusion
  99.7 0.7 bitcast_reduce_fusion.2
  100.7 7.5 gather_fusion
  108.3 0.7 bitcast_reduce_fusion.2
  109.1 101.7 %psum.62 = f32[20,256]{1,0:T(8,128)} all-reduce(f32[20,256]{1,0:T(8,128)S(1)} %get-tuple-element.215), channel_id=1, replica_groups=mesh['dp'=8,'space'=64] {'dp','space'}, use_global_device_ids=true, to_apply=%region_14.15 | all-reduce | flops 5120 | bytes 40960 | tf_op jit(solution)/shard_map/psum | solution.py:196
  210.8 1.0 scatter_custom_fusion.1
  211.7 1.0 scatter_custom_fusion.2
  213.0 0.9 convolution_bitcast_fusion.1
  213.9 90.9 %all-reduce.7.cloned.1.call-done = (f32[512,256]{1,0:T(8,128)}, f32[512,256]{1,0:T(8,128)}, f32[512,256]{1,0:T(8,128)}, f32[512,256]{1,0:T(8,128)}) async-done(((f32[512,256]{1,0:T(8,128)}, f32[512,256]{1,0:T(8,128)}, f32[512,256]{1,0:T(8,128)}, f32[512,256]{1,0:T(8,128)}), (f32[512,256]{1,0:T(8,128)}, f32[512,256]{1,0:T(8,128)}, f32[512,256]{1,0:T(8,128)}, ...) | async-done | bytes 2097168 | tf_op jit(solution)/shard_map/psum | solution.py:110
  304.9 2.3 fusion.38
  307.2 2.2 fusion.37
  309.5 0.4 fusion.32
  309.9 1.1 fusion.29
  311.0 29.8 %psum.63 = f32[20,256]{1,0:T(8,128)} all-reduce(f32[20,256]{1,0:T(8,128)S(1)} %fusion.32), channel_id=1, replica_groups=mesh['dp'=8,'space'=64] {'dp'}, use_global_device_ids=true, to_apply=%region_15.16 | all-reduce | flops 5120 | bytes 40960 | tf_op jit(solution)/shard_map/psum | solution.py:195
  340.9 0.9 convolution_bitcast_fusion
  341.8 0.9 fusion.27
  342.7 1.8 fusion.31
  344.5 451.4 %all-reduce.5.cloned.1.call-done = (f32[256,256]{0,1:T(8,128)}, f32[256,256]{0,1:T(8,128)}) async-done(((f32[256,256]{0,1:T(8,128)}, f32[256,256]{0,1:T(8,128)}), (f32[256,256]{0,1:T(8,128)}, f32[256,256]{0,1:T(8,128)})) %all-reduce.5.cloned.1.call-update) | async-done | bytes 524304 | tf_op jit(solution)/shard_map/psum | solution.py:196
  795.8 1.8 copy.25
  797.6 1.8 copy.26
  (126 shorter events, 3.8 us)
Async XLA Ops:
  7.2 1.4 copy-start
  7.2 27.3 %copy-start.8 = (bf16[1,128,256]{2,1,0:T(8,128)(2,1)S(1)}, bf16[1,128,256]{2,1,0:T(8,128)(2,1)}, u32[]{:S(2)}) copy-start(bf16[1,128,256]{2,1,0:T(8,128)(2,1)} %param.29) | copy-start | bytes 196612
  7.2 297.7 %all-reduce.7.cloned.1.call-start = ((), (), s32[]{:S(2)}) async-start(), calls=%async_computation.1 | async-start | bytes 4194304 | tf_op jit(solution)/shard_map/psum | solution.py:110
  8.0 0.6 copy-start.29
  8.0 20.6 %copy-start.28 = (s32[32]{0:T(128)}, s32[32]{0:T(128)S(1)}, u32[]{:S(2)}) copy-start(s32[32]{0:T(128)S(1)} %get-tuple-element.312) | copy-start | bytes 388
  10.2 31.1 %collective-permute-start = (bf16[32,256]{1,0:T(8,128)(2,1)S(1)}, bf16[32,256]{1,0:T(8,128)(2,1)S(1)}, u32[]{:S(2)}, u32[]{:S(2)}) collective-permute-start(bf16[32,256]{1,0:T(8,128)(2,1)S(1)} %gather_fusion.2), channel_id=1, source_target_pairs={{0,1},{1,2},{2,3},{3,4},{4,5},{5,6},{6,7},{7,8},{8,9},{9,10},{10,1... | collective-permute-start | bytes 49160 | tf_op jit(solution)/shard_map/ppermute | solution.py:17
  14.9 26.4 %collective-permute-start.1 = (bf16[32,256]{1,0:T(8,128)(2,1)S(1)}, bf16[32,256]{1,0:T(8,128)(2,1)S(1)}, u32[]{:S(2)}, u32[]{:S(2)}) collective-permute-start(bf16[32,256]{1,0:T(8,128)(2,1)S(1)} %gather_fusion.3), channel_id=1, source_target_pairs={{0,63},{1,0},{2,1},{3,2},{4,3},{5,4},{6,5},{7,6},{8,7},{9,8},{10,9... | collective-permute-start | bytes 49160 | tf_op jit(solution)/shard_map/ppermute | solution.py:17
  27.9 10.7 %copy-start.26 = (f32[128]{0:T(128)}, f32[128]{0:T(128)S(1)}, u32[]{:S(2)}) copy-start(f32[128]{0:T(128)S(1)} %compare_convert_fusion.1) | copy-start | bytes 1540
  28.6 10.0 %copy-start.19 = (f32[128]{0:T(128)}, f32[128]{0:T(128)S(1)}, u32[]{:S(2)}) copy-start(f32[128]{0:T(128)S(1)} %get-tuple-element.308) | copy-start | bytes 1540
  28.6 10.0 %copy-start.21 = (f32[128]{0:T(128)}, f32[128]{0:T(128)S(1)}, u32[]{:S(2)}) copy-start(f32[128]{0:T(128)S(1)} %get-tuple-element.309) | copy-start | bytes 1540
  28.6 10.0 %copy-start.23 = (f32[128]{0:T(128)}, f32[128]{0:T(128)S(1)}, u32[]{:S(2)}) copy-start(f32[128]{0:T(128)S(1)} %get-tuple-element.310) | copy-start | bytes 1540
  29.3 9.2 %copy-start.9 = (f32[1,512]{1,0:T(1,128)}, f32[1,512]{1,0:T(1,128)S(1)}, u32[]{:S(2)}) copy-start(f32[1,512]{1,0:T(1,128)S(1)} %get-tuple-element.304) | copy-start | bytes 6148
  29.4 9.2 %copy-start.11 = (f32[1,512]{1,0:T(1,128)}, f32[1,512]{1,0:T(1,128)S(1)}, u32[]{:S(2)}) copy-start(f32[1,512]{1,0:T(1,128)S(1)} %get-tuple-element.306) | copy-start | bytes 6148
  29.4 9.2 %copy-start.13 = (f32[1,512]{1,0:T(1,128)}, f32[1,512]{1,0:T(1,128)S(1)}, u32[]{:S(2)}) copy-start(f32[1,512]{1,0:T(1,128)S(1)} %get-tuple-element.307) | copy-start | bytes 6148
  29.4 11.1 %copy-start.15 = (f32[1,512]{1,0:T(1,128)}, f32[1,512]{1,0:T(1,128)S(1)}, u32[]{:S(2)}) copy-start(f32[1,512]{1,0:T(1,128)S(1)} %get-tuple-element.305) | copy-start | bytes 6148
  32.5 6.7 copy-start.32
  34.5 5.9 copy-start.25
  36.5 4.4 copy-start.17
  36.5 4.6 copy-start.18
  38.5 2.9 copy-start.7
  38.6 757.2 %all-reduce.5.cloned.1.call-start = ((), (), s32[]{:S(2)}) async-start(), calls=%async_computation | async-start | bytes 1048576 | tf_op jit(solution)/shard_map/psum | solution.py:196
  38.7 2.4 copy-start.30
  83.1 128.6 %collective-permute-start.3 = (bf16[32,256]{1,0:T(8,128)(2,1)S(1)}, bf16[32,256]{1,0:T(8,128)(2,1)S(1)}, u32[]{:S(2)}, u32[]{:S(2)}) collective-permute-start(bf16[32,256]{1,0:T(8,128)(2,1)S(1)} %get-tuple-element.302), channel_id=1, source_target_pairs={{0,1},{1,2},{2,3},{3,4},{4,5},{5,6},{6,7},{7,8},{8,9},{9,10},{10,1... | collective-permute-start | bytes 49160 | tf_op jit(solution)/shard_map/ppermute | solution.py:17
  85.1 125.7 %collective-permute-start.2 = (bf16[32,256]{1,0:T(8,128)(2,1)S(1)}, bf16[32,256]{1,0:T(8,128)(2,1)S(1)}, u32[]{:S(2)}, u32[]{:S(2)}) collective-permute-start(bf16[32,256]{1,0:T(8,128)(2,1)S(1)} %get-tuple-element.303), channel_id=1, source_target_pairs={{0,63},{1,0},{2,1},{3,2},{4,3},{5,4},{6,5},{7,6},{8,7},{9,8},{10,9... | collective-permute-start | bytes 49160 | tf_op jit(solution)/shard_map/ppermute | solution.py:17
  91.8 121.2 %copy-start.5 = (bf16[1,128,256]{2,1,0:T(8,128)(2,1)S(1)}, bf16[1,128,256]{2,1,0:T(8,128)(2,1)}, u32[]{:S(2)}) copy-start(bf16[1,128,256]{2,1,0:T(8,128)(2,1)} %param.17) | copy-start | bytes 196612
  91.8 213.1 %copy-start.10 = (f32[1,512]{1,0:T(1,128)S(1)}, f32[1,512]{1,0:T(1,128)}, u32[]{:S(2)}) copy-start(f32[1,512]{1,0:T(1,128)} %copy-done.9) | copy-start | bytes 6148
  91.8 213.1 %copy-start.12 = (f32[1,512]{1,0:T(1,128)S(1)}, f32[1,512]{1,0:T(1,128)}, u32[]{:S(2)}) copy-start(f32[1,512]{1,0:T(1,128)} %copy-done.11) | copy-start | bytes 6148
  91.8 213.1 %copy-start.14 = (f32[1,512]{1,0:T(1,128)S(1)}, f32[1,512]{1,0:T(1,128)}, u32[]{:S(2)}) copy-start(f32[1,512]{1,0:T(1,128)} %copy-done.13) | copy-start | bytes 6148
  91.8 213.1 %copy-start.20 = (f32[128]{0:T(128)S(1)}, f32[128]{0:T(128)}, u32[]{:S(2)}) copy-start(f32[128]{0:T(128)} %copy-done.19) | copy-start | bytes 1540
  91.8 213.1 %copy-start.22 = (f32[128]{0:T(128)S(1)}, f32[128]{0:T(128)}, u32[]{:S(2)}) copy-start(f32[128]{0:T(128)} %copy-done.21) | copy-start | bytes 1540
  91.8 213.1 %copy-start.24 = (f32[128]{0:T(128)S(1)}, f32[128]{0:T(128)}, u32[]{:S(2)}) copy-start(f32[128]{0:T(128)} %copy-done.23) | copy-start | bytes 1540
  109.0 200.4 %copy-start.16 = (f32[1,512]{1,0:T(1,128)S(1)}, f32[1,512]{1,0:T(1,128)}, u32[]{:S(2)}) copy-start(f32[1,512]{1,0:T(1,128)} %copy-done.15) | copy-start | bytes 6148
  109.0 200.4 %copy-start.31 = (f32[20]{0:T(128)S(1)}, f32[20]{0:T(128)}, u32[]{:S(2)}) copy-start(f32[20]{0:T(128)} %copy-done.30) | copy-start | bytes 244
  304.9 4.6 copy-start.1
  304.9 4.6 copy-start.2
  304.9 4.6 copy-start.3
  304.9 4.6 copy-start.4
  304.9 4.9 copy-start.27
  309.5 32.3 %copy-start.6 = (bf16[256,256]{1,0:T(8,128)(2,1)S(1)}, bf16[256,256]{1,0:T(8,128)(2,1)}, u32[]{:S(2)}) copy-start(bf16[256,256]{1,0:T(8,128)(2,1)} %param.27) | copy-start | bytes 393220
Sparse Core Ops, SparseCore 0:
  38.7 266.1 all-reduce.6
  341.9 453.8 all-reduce.4
where the time goes:
time: 807 us; the launch traced here: 806 us
  waiting for transfers between devices  542 us (67%)
  blocking collectives  132 us (16%)
  local copies, waits for them, and re-layouts  37.7 us (5%)
  other arithmetic  29.4 us (4%)
  starting transfers between devices  25 us (3%)
  matrix products  24.5 us (3%)
  between operations  15.4 us (2%)
    psum x1, waiting for transfers between devices, body(): lax.psum((message_term, charge_term, filter_term), ('dp', 'space'))  451 us
    psum x1, blocking collectives, body(): lax.psum((message_term, charge_term, filter_term), ('dp', 'space'))  102 us
    psum x1, waiting for transfers between devices, body(): lax.psum((contract_rows(cosines, charge), contract_rows(sines, charge)),...  90.9 us
    psum x1, blocking collectives, body(): grad_kspace = lax.psum(kspace_term, 'dp')  29.8 us
    ppermute x4, starting transfers between devices, passed_along(): return lax.ppermute(value, axis, pairs)  24.9 us
    scatter-add x2, other arithmetic, backward_block(): ext_grad = ext_grad.at[index_piece].add(weighted * edge_weights)  23.3 us
  transfers between devices with their start and end apart: 6, of which 2 were waited for; matrix products, arithmetic and copies ran while one was open for 10% of the time, Pallas kernels for 0%

commit v1 on v0

v1 whole, which is shorter than its diff:
```python
import math

import jax
import jax.numpy as jnp
import numpy as np
from jax import lax
from jax.experimental import pallas as pl
from jax.experimental.pallas import tpu as pltpu
from jax.sharding import Mesh, PartitionSpec as P

cutoff_radius = 5.0
kspace_limit = 8.0 * math.pi * math.sqrt(3.0)
ewald_scale_factor = 4.0
two_pi = 2.0 * math.pi

bf16 = jnp.bfloat16
f32 = jnp.float32

SLOTS_OWN = 6
ROWS_OWN = 4 * SLOTS_OWN
PACK_ROWS = 16
PACK_COLS = 384
GRAD_CHUNKS = 32

NN = (((1,), (0,)), ((), ()))
NT = (((1,), (1,)), ((), ()))
TN = (((0,), (0,)), ((), ()))


def dot(left, right, dims=NN, precision=None):
    return lax.dot_general(left, right, dims, precision=precision, preferred_element_type=f32)


def cosine_coefficients():
    nodes = np.cos((np.arange(64) + 0.5) * np.pi / 64)
    u = 0.125 + 0.125 * nodes
    fit = np.polynomial.chebyshev.Chebyshev.fit(u, np.cos(two_pi * np.sqrt(u)), 7, domain=[0.0, 0.25])
    return [float(c) for c in fit.convert(kind=np.polynomial.Polynomial).coef]


COSINE = cosine_coefficients()


def cosine_of_turns(turns):
    r = turns - jnp.floor(turns + 0.5)
    u = r * r
    out = jnp.full_like(u, COSINE[-1])
    for c in COSINE[-2::-1]:
        out = out * u + c
    return out


def wave_rows(owners):
    rows = np.zeros((owners * ROWS_OWN, 8), np.float32)
    for owner in range(owners):
        for place in range(ROWS_OWN):
            v = owner * SLOTS_OWN + place % SLOTS_OWN + 1
            nz = (v + 4) % 9 - 4
            m = (v - nz) // 9
            ny = (m + 4) % 9 - 4
            nx = (m - ny) // 9
            quarter = -0.25 if (place // SLOTS_OWN) % 2 else 0.0
            rows[owner * ROWS_OWN + place, :4] = (nx, ny, nz, quarter)
    return rows


def packed(rows24):
    tail = rows24[..., 16:24, :]
    side = jnp.concatenate([tail[..., :128], tail[..., 128:]], axis=-2)
    return jnp.concatenate([rows24[..., :16, :], side], axis=-1)


def unpacked(rows16):
    tail = jnp.concatenate([rows16[..., 0:8, 256:], rows16[..., 8:16, 256:]], axis=-1)
    return jnp.concatenate([rows16[..., :256], tail], axis=-2)


def column_iota(shape, axis):
    return lax.broadcasted_iota(jnp.int32, shape, axis)


def send_kernel(feat_ref, wm_ref, list_ref, hidden_ref, act_ref, down_ref, up_ref):
    hidden = dot(feat_ref[...], wm_ref[...])
    hidden_ref[...] = hidden
    act = (hidden * jax.nn.sigmoid(hidden)).astype(bf16)
    act_ref[...] = act
    atoms = act.shape[0]
    ghosts = list_ref.shape[1]
    lists = list_ref[...]
    for which, ref in ((0, down_ref), (1, up_ref)):
        pick = column_iota((atoms, ghosts), 0) == lists[which : which + 1, :]
        ref[...] = dot(pick.astype(f32).astype(bf16), act, TN).astype(bf16)


def wave_kernel(count_ref, feat_ref, cot_ref, frac_ref, rows_ref, table_ref, sums_ref):
    atoms, channels = feat_ref.shape
    live = column_iota((atoms, channels), 0) < count_ref[0, 0]
    zero = jnp.zeros((atoms, channels), f32)
    feat = jnp.where(live, feat_ref[...].astype(f32), zero).astype(bf16)
    cot = jnp.where(live, cot_ref[...].astype(f32), zero).astype(bf16)
    frac = frac_ref[...]
    which = column_iota((8, atoms), 0)
    coords = jnp.where(which == 0, frac[0:1, :], 0.0)
    coords = jnp.where(which == 1, frac[1:2, :], coords)
    coords = jnp.where(which == 2, frac[2:3, :], coords)
    coords = jnp.where(which == 3, 1.0, coords)
    high = coords.astype(bf16)
    rest = coords - high.astype(f32)
    middle = rest.astype(bf16)
    low = (rest - middle.astype(f32)).astype(bf16)
    rows = rows_ref[...]
    turns = dot(rows, high) + (dot(rows, middle) + dot(rows, low))
    table = cosine_of_turns(turns)
    total = table.shape[0]
    owners = total // ROWS_OWN
    table = table.reshape(owners, ROWS_OWN, atoms)
    first = column_iota((owners, ROWS_OWN, atoms), 1) < ROWS_OWN // 2
    nothing = jnp.zeros_like(table)
    both = jnp.concatenate(
        [jnp.where(first, table, nothing), jnp.where(first, nothing, table)], axis=-1
    )
    both = both.reshape(total, 2 * atoms).astype(bf16)
    table_ref[...] = both
    sums = dot(both, jnp.concatenate([feat, cot], axis=0))
    sums_ref[...] = packed(sums.reshape(owners, ROWS_OWN, channels)).astype(bf16)


def edge_kernel(
    count_ref,
    act_ref,
    lower_ref,
    upper_ref,
    index_ref,
    used_ref,
    length_ref,
    wf_ref,
    cot_ref,
    messages_ref,
    own_ref,
    to_lower_ref,
    to_upper_ref,
    filter_ref,
    pick_s,
    basis_s,
    grad_s,
    push_s,
):
    atoms, channels = act_ref.shape
    slots = index_ref.shape[1]
    bins = wf_ref.shape[0]
    ghosts = lower_ref.shape[0]
    table = atoms + 2 * ghosts
    padded = basis_s.shape[0]
    ext = jnp.concatenate(
        [act_ref[...].astype(f32), lower_ref[...].astype(f32), upper_ref[...].astype(f32)], axis=0
    )
    ext_t = ext.T.astype(bf16)
    index_t = index_ref[...].T
    length_t = length_ref[...].T
    live = column_iota((1, atoms), 1) < count_ref[0, 0]
    cot_t = jnp.where(live, cot_ref[...].astype(f32).T, 0.0)
    cot_pair = jnp.concatenate([cot_t, cot_t], axis=1)
    used = jnp.where(live, used_ref[...], 0)
    valid = column_iota((slots, atoms), 0) < used
    envelope = 0.5 * (jnp.cos(math.pi * length_t / cutoff_radius) + 1.0)
    envelope = jnp.where(valid, envelope, 0.0)
    bin_at = column_iota((padded, 2 * atoms), 0).astype(f32)
    spacing = cutoff_radius / (bins - 1)
    row_at = column_iota((table, 2 * atoms), 0)
    wf = wf_ref[...]
    total = jnp.zeros((channels, 2 * atoms), f32)
    for step in range(slots // 2):
        j = 2 * step

        def paired(rows):
            return jnp.concatenate([rows[j : j + 1, :], rows[j + 1 : j + 2, :]], axis=1)

        here = pl.ds(step * 2 * atoms, 2 * atoms)
        scaled = (paired(length_t) - cutoff_radius * bin_at / (bins - 1)) / spacing
        basis = jnp.exp(-0.5 * scaled * scaled) * paired(envelope)
        basis = jnp.where(bin_at < bins, basis, 0.0).astype(bf16)
        basis_s[:, here] = basis
        weights = dot(wf, basis[:bins], TN)
        pick = jnp.where(row_at == paired(index_t), 1.0, 0.0).astype(bf16)
        pick_s[:, here] = pick
        gathered = dot(ext_t, pick)
        total = total + weights * gathered
        grad_s[:, here] = (cot_pair * gathered).astype(bf16)
        push_s[:, here] = (cot_pair * weights).astype(bf16)
    messages_ref[...] = (total[:, :atoms] + total[:, atoms:]).T
    filter_ref[...] = dot(basis_s[...], grad_s[...], NT)
    ext_grad = dot(push_s[...], pick_s[...], NT).T
    own_ref[...] = ext_grad[:atoms]
    to_lower_ref[...] = ext_grad[atoms : atoms + ghosts].astype(bf16)
    to_upper_ref[...] = ext_grad[atoms + ghosts :].astype(bf16)


def wave_vector_length(slot):
    v = slot + 1.0
    m = jnp.floor((v + 4.5) / 9.0)
    nz = v - 9.0 * m
    nx = jnp.floor((m + 4.5) / 9.0)
    ny = m - 9.0 * nx
    return two_pi * jnp.sqrt(nx * nx + ny * ny + nz * nz)


def wave_basis(slot, bin_at, bins):
    spacing = kspace_limit / (bins - 1)
    scaled = (wave_vector_length(slot) - kspace_limit * bin_at / (bins - 1)) / spacing
    return jnp.where(bin_at < bins, jnp.exp(-0.5 * scaled * scaled), 0.0)


def swapped_halves(rows):
    half = rows.shape[0] // 2
    return jnp.concatenate([rows[half:], rows[:half]], axis=0)


def split_two(value):
    high = value.astype(bf16)
    return high, (value - high.astype(f32)).astype(bf16)


def middle_kernel(
    scale,
    owner_ref,
    sums_ref,
    index_ref,
    wc_ref,
    wk_ref,
    own_ref,
    back_upper_ref,
    back_lower_ref,
    list_ref,
    hidden_ref,
    feat_ref,
    filter_ref,
    pre_ref,
    grads_ref,
    weights_ref,
):
    bins, channels = wk_ref.shape
    sums = unpacked(sums_ref[...])
    first_slot = (owner_ref[0] * SLOTS_OWN).astype(f32)

    def slot_of(shape, axis):
        place = column_iota(shape, axis).astype(f32)
        return first_slot + place - SLOTS_OWN * jnp.floor((place + 0.5) / SLOTS_OWN)

    waves = index_ref.shape[1]
    index = index_ref[...].astype(f32)
    codes = jnp.abs(81.0 * index[0:1] + 9.0 * index[1:2] + index[2:3])
    same = jnp.where(slot_of((ROWS_OWN, waves), 0) + 1.0 == codes, 1.0, 0.0)
    times = jnp.sum(same, axis=1, keepdims=True)
    across = (ROWS_OWN, bins)
    basis = wave_basis(slot_of(across, 0), column_iota(across, 1).astype(f32), bins).astype(bf16)
    wave_filter = dot(basis, wk_ref[...])
    high, low = split_two(sums)
    factor = dot(high, wc_ref[...]) + dot(low, wc_ref[...])
    first = column_iota((ROWS_OWN, channels), 0) < ROWS_OWN // 2
    weights = (times * scale) * wave_filter * jnp.where(first, factor, sums)
    weights = weights.astype(bf16)
    weights_ref[...] = packed(weights.astype(f32)).astype(bf16)
    filter_grad = jnp.where(first, (times * scale) * factor * swapped_halves(sums), 0.0)
    down = (ROWS_OWN, ROWS_OWN)
    basis_down = wave_basis(slot_of(down, 1), column_iota(down, 0).astype(f32), bins)
    basis_down = basis_down.astype(bf16).astype(f32)
    kspace = dot(basis_down, filter_grad, precision=lax.Precision.HIGHEST)
    pushed = swapped_halves(weights.astype(f32)).astype(bf16)
    none = jnp.zeros_like(sums)
    high, low = split_two(jnp.where(first, sums, none))
    charge = dot(high, pushed, TN) + dot(low, pushed, TN)

    atoms = own_ref.shape[0]
    ghosts = list_ref.shape[1]
    lists = list_ref[...]
    act_grad = own_ref[...]
    for which, ref in ((1, back_upper_ref), (0, back_lower_ref)):
        place = column_iota((atoms, ghosts), 0) == lists[which : which + 1, :]
        act_grad = act_grad + dot(place.astype(f32).astype(bf16), ref[...])
    hidden = hidden_ref[...]
    sigma = jax.nn.sigmoid(hidden)
    pre = (act_grad * (sigma * (1.0 + hidden * (1.0 - sigma)))).astype(bf16)
    pre_ref[...] = pre
    message = dot(feat_ref[...], pre, TN)
    share = channels // GRAD_CHUNKS
    both = jnp.concatenate(
        [message.reshape(GRAD_CHUNKS, share, channels), charge.reshape(GRAD_CHUNKS, share, channels)],
        axis=1,
    )
    grads_ref[:, :, :channels] = both.astype(bf16)
    small = jnp.concatenate([filter_ref[...], kspace], axis=0)
    groups = small.shape[0] // 8
    for chunk in range(GRAD_CHUNKS):
        if chunk < groups:
            rows = small[8 * chunk : 8 * chunk + 8]
            side = jnp.concatenate([rows[:, :128], rows[:, 128:]], axis=0).astype(bf16)
        else:
            side = jnp.zeros((PACK_ROWS, 128), bf16)
        grads_ref[chunk, :, channels:] = side


def final_kernel(
    count_ref,
    table_ref,
    weights_ref,
    feat_ref,
    messages_ref,
    cot_ref,
    pre_ref,
    wm_ref,
    wc_ref,
    updated_ref,
    grad_ref,
):
    atoms, channels = feat_ref.shape
    total = table_ref.shape[0]
    rows = unpacked(weights_ref[...].astype(f32)).reshape(total, channels).astype(bf16)
    both = dot(table_ref[...], rows, TN)
    live = column_iota((atoms, channels), 0) < count_ref[0, 0]
    added = jnp.where(live, messages_ref[...] + both[:atoms], 0.0)
    updated_ref[...] = (feat_ref[...].astype(f32) + added).astype(bf16)
    charge_grad = jnp.where(live, both[atoms:], 0.0).astype(bf16)
    grad_ref[...] = (
        cot_ref[...].astype(f32)
        + dot(pre_ref[...], wm_ref[...], NT)
        + dot(charge_grad, wc_ref[...], NT)
    )


def on_core(kernel, out_shape, in_smem, n_in, scratch=()):
    smem = pl.BlockSpec(memory_space=pltpu.SMEM)
    vmem = pl.BlockSpec(memory_space=pltpu.VMEM)
    return pl.pallas_call(
        kernel,
        out_shape=out_shape,
        in_specs=[smem] * in_smem + [vmem] * (n_in - in_smem),
        out_specs=[vmem] * len(out_shape),
        scratch_shapes=list(scratch),
        compiler_params=pltpu.CompilerParams(vmem_limit_bytes=48 * 1024 * 1024),
    )


def shape(dims, kind):
    return jax.ShapeDtypeStruct(dims, kind)


def exchanged(value, axis):
    return lax.all_to_all(value, axis, 0, 0, tiled=True)


def summed(parts):
    return jnp.sum(parts.astype(f32), axis=0)


def body(
    features,
    fractional,
    counts,
    neighbor_index,
    neighbor_count,
    send_list,
    distances,
    wave_index,
    w_message,
    w_filter,
    w_charge,
    w_kspace,
    cotangent,
):
    feat, cot, lists = features[0], cotangent[0], send_list[0, 0]
    atoms, channels = feat.shape
    slots = neighbor_index.shape[2]
    ghosts = lists.shape[1]
    bins = w_filter.shape[0]
    waves = wave_index.shape[1]
    size_z, size_y = lax.axis_size("z"), lax.axis_size("y")
    domains = size_z * size_y
    space = ("z", "y")
    scale = ewald_scale_factor / math.sqrt(atoms * domains * waves)

    def passed_along(value, steps):
        return lax.ppermute(value, space, [(s, (s + steps) % domains) for s in range(domains)])

    hidden, act, down, up = on_core(
        send_kernel,
        [
            shape((atoms, channels), f32),
            shape((atoms, channels), bf16),
            shape((ghosts, channels), bf16),
            shape((ghosts, channels), bf16),
        ],
        0,
        3,
    )(feat, w_message, lists)
    from_lower = passed_along(up, 1)
    from_upper = passed_along(down, -1)

    total = domains * ROWS_OWN
    table, sums = on_core(
        wave_kernel,
        [shape((total, 2 * atoms), bf16), shape((domains, PACK_ROWS, PACK_COLS), bf16)],
        1,
        5,
    )(counts, feat, cot, fractional[0], jnp.asarray(wave_rows(domains), bf16))
    sums = exchanged(sums.reshape(size_y, size_z * PACK_ROWS, PACK_COLS), "y")
    sums = summed(sums).astype(bf16)

    messages, own, to_lower, to_upper, filter_term = on_core(
        edge_kernel,
        [
            shape((atoms, channels), f32),
            shape((atoms, channels), f32),
            shape((ghosts, channels), bf16),
            shape((ghosts, channels), bf16),
            shape((ROWS_OWN, channels), f32),
        ],
        1,
        9,
        [
            pltpu.VMEM((atoms + 2 * ghosts, slots * atoms), bf16),
            pltpu.VMEM((ROWS_OWN, slots * atoms), bf16),
            pltpu.VMEM((channels, slots * atoms), bf16),
            pltpu.VMEM((channels, slots * atoms), bf16),
        ],
    )(
        counts,
        act,
        from_lower,
        from_upper,
        neighbor_index[0],
        neighbor_count,
        distances[0],
        w_filter,
        cot,
    )
    back_upper = passed_along(to_lower, -1)
    back_lower = passed_along(to_upper, 1)

    sums = exchanged(sums.reshape(size_z, PACK_ROWS, PACK_COLS), "z")
    sums = summed(sums)
    owner = lax.axis_index("y") * size_z + lax.axis_index("z")
    pre, grads, weights = on_core(
        lambda *refs: middle_kernel(scale, *refs),
        [
            shape((atoms, channels), bf16),
            shape((GRAD_CHUNKS, PACK_ROWS, PACK_COLS), bf16),
            shape((PACK_ROWS, PACK_COLS), bf16),
        ],
        1,
        12,
    )(
        owner.reshape(1).astype(jnp.int32),
        sums,
        wave_index,
        w_charge,
        w_kspace,
        own,
        back_upper,
        back_lower,
        lists,
        hidden,
        feat,
        filter_term,
    )
    grads = exchanged(grads, ("x", "core", "y"))
    grads = summed(grads).astype(bf16)
    both = jnp.concatenate([weights, grads], axis=0)
    both = exchanged(jnp.broadcast_to(both[None], (size_z,) + both.shape), "z")
    weights = both[:, :PACK_ROWS].reshape(size_z * PACK_ROWS, PACK_COLS)
    grads = summed(both[:, PACK_ROWS:]).astype(bf16)
    both = jnp.concatenate([weights, grads], axis=0)
    both = exchanged(jnp.broadcast_to(both[None], (size_y,) + both.shape), "y")
    weights = both[:, : size_z * PACK_ROWS].reshape(domains, PACK_ROWS, PACK_COLS)
    grads = both[:, size_z * PACK_ROWS :]
    slabs = lax.axis_size("x") * lax.axis_size("core")
    grads = exchanged(jnp.broadcast_to(grads[None], (slabs,) + grads.shape), ("x", "core"))
    grads = grads.reshape(GRAD_CHUNKS, PACK_ROWS, PACK_COLS)

    updated, grad_features = on_core(
        final_kernel,
        [shape((atoms, channels), bf16), shape((atoms, channels), f32)],
        1,
        9,
    )(counts, table, weights, feat, messages, cot, pre, w_message, w_charge)

    grads = grads.astype(f32)
    grad_message = grads[:, 0:8, :channels].reshape(channels, channels)
    grad_charge = grads[:, 8:16, :channels].reshape(channels, channels)
    small = jnp.concatenate([grads[:6, 0:8, channels:], grads[:6, 8:16, channels:]], axis=2)
    small = small.reshape(2, ROWS_OWN, channels)
    return (
        updated[None],
        grad_features[None],
        grad_message,
        grad_charge,
        small[0, :bins],
        small[1, :bins],
    )


def solution(mesh):
    fine = Mesh(mesh.devices.reshape(4, 2, 16, 4), ("x", "core", "z", "y"))
    dp, space = ("x", "core"), ("z", "y")
    placed = (
        P(dp, space, None),
        P(dp, None, space),
        P(dp, space),
        P(dp, space, None),
        P(dp, space),
        P(dp, space, None, None),
        P(dp, space, None),
        P(),
        P(),
        P(),
        P(),
        P(),
        P(dp, space, None),
    )
    return jax.shard_map(
        body,
        mesh=fine,
        in_specs=placed,
        out_specs=(P(dp, space, None), P(dp, space, None), P(), P(), P(), P()),
        check_vma=False,
    )
```

time: 807 us -> 150 us (0.19)
  waiting for transfers between devices: 542 us -> 13.4 us
  blocking collectives: 132 us -> 74.1 us
  local copies, waits for them, and re-layouts: 37.7 us -> 7.26 us
  other arithmetic: 29.4 us -> 1.09 us
  matrix products: 24.5 us -> 0 us
  starting transfers between devices: 25 us -> 45.1 us
  between operations: 15.4 us -> 1.54 us
    psum x2 -> x0, waiting for transfers between devices: 542 us -> none  [the longest x1 451 us: body(): lax.psum((message_term, charge_term, filter_term), ('dp', 'space'))]
    psum x2 -> x0, blocking collectives: 132 us -> none  [the longest x1 102 us: body(): lax.psum((message_term, charge_term, filter_term), ('dp', 'space'))]
    all_to_all x0 -> x4, blocking collectives: none -> 74.1 us  [exchanged(): return lax.all_to_all(value, axis, 0, 0, tiled=True)]
    gather x6 -> x0, local copies, waits for them, and re-layouts: 31.3 us -> none  [the longest x2 15 us: backward_block(): gathered = extended[index_piece].astype(jnp.float32)]
    all_to_all x0 -> x2, starting transfers between devices: none -> 27.9 us  [exchanged(): return lax.all_to_all(value, axis, 0, 0, tiled=True)]
    scatter-add x4 -> x0, other arithmetic: 25.3 us -> none  [the longest x2 23.3 us: backward_block(): ext_grad = ext_grad.at[index_piece].add(weighted * edge_weights)]
    dot_general x22 -> x0, matrix products: 24.5 us -> none  [the longest x11 12.8 us: contract_rows(): lax.dot_general(left, right, (((0,), (0,)), ((), ())), preferred_element_...]
  transfers between devices with their start and end apart: 6 -> 6, of which waited for: 2 -> 3; matrix products, arithmetic and copies ran while one was open for 10% -> 0% of each run, Pallas kernels for 0% -> 3%
where the time goes in v1:
time: 150 us; the launch traced here: 149 us
  blocking collectives  74.1 us (49%)
  starting transfers between devices  45.1 us (30%)
  waiting for transfers between devices  13.4 us (9%)
  local copies, waits for them, and re-layouts  7.26 us (5%)
  Pallas kernels  6.35 us (4%)
  between operations  1.54 us (1%)
    all_to_all x4, blocking collectives, exchanged(): return lax.all_to_all(value, axis, 0, 0, tiled=True)  74.1 us
    all_to_all x2, starting transfers between devices, exchanged(): return lax.all_to_all(value, axis, 0, 0, tiled=True)  27.9 us
    ppermute x4, starting transfers between devices, passed_along(): lax.ppermute(value, space, [(s, (s + steps) % domains) for s in range(dom...  17.1 us
    all_to_all x2, waiting for transfers between devices, exchanged(): return lax.all_to_all(value, axis, 0, 0, tiled=True)  6.79 us
    ppermute x4, waiting for transfers between devices, passed_along(): lax.ppermute(value, space, [(s, (s + steps) % domains) for s in range(dom...  6.58 us
    unnamed x33, local copies, waits for them, and re-layouts  4.83 us
  transfers between devices with their start and end apart: 6, of which 3 were waited for; matrix products, arithmetic and copies ran while one was open for 0% of the time, Pallas kernels for 3%

profile of v1, /device:TPU:1, one launch (start us, length us, event | category | flops | bytes accessed | tf_op | source)
XLA Modules:
  0.0 148.8 jit_solution(9068295032130246383)
XLA Ops:
  0.6 0.0 copy-start.14
  1.3 0.0 copy-done.14
  1.3 0.0 copy-start
  1.3 0.8 copy-done
  2.2 0.8 copy-done.2
  3.0 1.0 copy-done.6
  4.0 1.2 shard_map.181
  5.2 13.2 %all_to_all.30 = bf16[4,256,384]{2,1,0:T(8,128)(2,1)S(1)} all-to-all(bf16[4,256,384]{2,1,0:T(8,128)(2,1)S(1)} %bitcast.32), channel_id=1, replica_groups=mesh['x'=4,'core'=2,'z'=16,'y'=4] {'y'}, dimensions={0} | all-to-all | bytes 1572864 | tf_op jit(solution)/shard_map/all_to_all | solution.py:348
  18.3 0.8 reduce_sum.45
  19.2 18.1 %all-to-all-start.1 = ((bf16[16,16,384]{2,1,0:T(8,128)(2,1)}), bf16[16,16,384]{2,1,0:T(8,128)(2,1)S(1)}, u32[]{:S(2)}, u32[]{:S(2)}) async-start(bf16[16,16,384]{2,1,0:T(8,128)(2,1)} %bitcast.4), calls=%async_computation.1 | async-start | bytes 393216 | tf_op jit(solution)/shard_map/all_to_all | solution.py:348
  37.2 0.0 copy-start.10
  37.3 0.0 copy-done.1
  37.3 0.0 copy-done.5
  37.3 0.7 copy-done.10
  37.9 0.3 shard_map.182
  38.3 2.2 %collective-permute-start = (bf16[32,256]{1,0:T(8,128)(2,1)S(1)}, bf16[32,256]{1,0:T(8,128)(2,1)S(1)}, u32[]{:S(2)}, u32[]{:S(2)}) collective-permute-start(bf16[32,256]{1,0:T(8,128)(2,1)S(1)} %get-tuple-element.25), channel_id=1, source_target_pairs={{0,1},{1,2},{2,3},{3,4},{4,5},{5,6},{6,7},{7,8},{8,9},{9,10},{10,1... | collective-permute-start | bytes 49160 | tf_op jit(solution)/shard_map/ppermute | solution.py:382
  40.5 6.4 %collective-permute-start.1 = (bf16[32,256]{1,0:T(8,128)(2,1)S(1)}, bf16[32,256]{1,0:T(8,128)(2,1)S(1)}, u32[]{:S(2)}, u32[]{:S(2)}) collective-permute-start(bf16[32,256]{1,0:T(8,128)(2,1)S(1)} %get-tuple-element.26), channel_id=1, source_target_pairs={{0,63},{1,0},{2,1},{3,2},{4,3},{5,4},{6,5},{7,6},{8,7},{9,8},{10,9... | collective-permute-start | bytes 49160 | tf_op jit(solution)/shard_map/ppermute | solution.py:382
  46.9 0.0 copy-start.13
  46.9 0.1 copy.22
  47.0 0.6 copy-done.13
  47.6 0.1 copy.23
  47.7 0.8 collective-permute-done.lower_ref
  48.5 0.0 collective-permute-done.1.upper_ref
  48.5 0.0 copy-done.7
  48.5 0.6 copy-done.11
  49.2 2.9 %shard_map.183 = (f32[128,256]{1,0:T(8,128)S(1)}, f32[128,256]{1,0:T(8,128)S(1)}, bf16[32,256]{1,0:T(8,128)(2,1)S(1)}, bf16[32,256]{1,0:T(8,128)(2,1)S(1)}, f32[24,256]{1,0:T(8,128)S(1)}) custom-call(s32[1,1]{1,0:T(1,128)S(6)} %copy.27.count_ref, bf16[128,256]{1,0:T(8,128)(2,1)S(1)} %get-tuple-element.24.act_ref, ...), custom_call_target="tpu_custom_call" | custom-call | tf_op jit(solution)/shard_map/pallas_call | solution.py:408
  52.1 0.0 copy-start.4
  52.1 6.6 %collective-permute-start.2 = (bf16[32,256]{1,0:T(8,128)(2,1)S(1)}, bf16[32,256]{1,0:T(8,128)(2,1)S(1)}, u32[]{:S(2)}, u32[]{:S(2)}) collective-permute-start(bf16[32,256]{1,0:T(8,128)(2,1)S(1)} %get-tuple-element.28), channel_id=1, source_target_pairs={{0,63},{1,0},{2,1},{3,2},{4,3},{5,4},{6,5},{7,6},{8,7},{9,8},{10,9... | collective-permute-start | bytes 49160 | tf_op jit(solution)/shard_map/ppermute | solution.py:382
  58.7 1.9 %collective-permute-start.3 = (bf16[32,256]{1,0:T(8,128)(2,1)S(1)}, bf16[32,256]{1,0:T(8,128)(2,1)S(1)}, u32[]{:S(2)}, u32[]{:S(2)}) collective-permute-start(bf16[32,256]{1,0:T(8,128)(2,1)S(1)} %get-tuple-element.29), channel_id=1, source_target_pairs={{0,1},{1,2},{2,3},{3,4},{4,5},{5,6},{6,7},{7,8},{8,9},{9,10},{10,1... | collective-permute-start | bytes 49160 | tf_op jit(solution)/shard_map/ppermute | solution.py:382
  60.6 0.0 all-to-all-done.1
  60.6 0.0 copy-start.8
  60.6 0.0 copy-start.9
  60.7 0.0 collective-permute-done.2.refs_6_
  60.7 5.8 %collective-permute-done.3.refs_7_ = bf16[32,256]{1,0:T(8,128)(2,1)S(1)} collective-permute-done((bf16[32,256]{1,0:T(8,128)(2,1)S(1)}, bf16[32,256]{1,0:T(8,128)(2,1)S(1)}, u32[]{:S(2)}, u32[]{:S(2)}) %collective-permute-start.3) | collective-permute-done | bytes 16416 | tf_op jit(solution)/shard_map/ppermute | solution.py:382
  66.5 0.7 shard_map.184
  67.2 19.0 %all_to_all.31 = bf16[32,16,384]{2,1,0:T(8,128)(2,1)S(1)} all-to-all(bf16[32,16,384]{2,1,0:T(8,128)(2,1)S(1)} %get-tuple-element.33), channel_id=1, replica_groups=mesh['x'=4,'core'=2,'z'=16,'y'=4] {'x','core','y'}, dimensions={0} | all-to-all | bytes 786432 | tf_op jit(solution)/shard_map/all_to_all | solution.py:348
  86.2 0.1 reduce_sum.47
  86.4 29.6 %all_to_all.32 = bf16[16,32,384]{2,1,0:T(8,128)(2,1)S(1)} all-to-all(bf16[16,32,384]{2,1,0:T(8,128)(2,1)S(1)} %broadcast_in_dim.10), channel_id=1, replica_groups=mesh['x'=4,'core'=2,'z'=16,'y'=4] {'z'}, dimensions={0} | all-to-all | bytes 786432 | tf_op jit(solution)/shard_map/all_to_all | solution.py:348
  116.0 0.1 broadcast_in_dim.11
  116.1 12.4 %all_to_all.33 = bf16[4,272,384]{2,1,0:T(8,128)(2,1)S(1)} all-to-all(bf16[4,272,384]{2,1,0:T(8,128)(2,1)S(1)} %broadcast_in_dim.11), channel_id=1, replica_groups=mesh['x'=4,'core'=2,'z'=16,'y'=4] {'y'}, dimensions={0} | all-to-all | bytes 1671168 | tf_op jit(solution)/shard_map/all_to_all | solution.py:348
  128.5 0.8 broadcast_in_dim.28
  129.3 9.9 %all-to-all-start.5 = ((bf16[8,4,16,384]{3,2,1,0:T(8,128)(2,1)}), bf16[8,4,16,384]{3,2,1,0:T(8,128)(2,1)S(1)}, u32[]{:S(2)}, u32[]{:S(2)}) async-start(bf16[8,4,16,384]{3,2,1,0:T(8,128)(2,1)} %broadcast_in_dim.28), calls=%async_computation.5 | async-start | bytes 786432 | tf_op jit(solution)/shard_map/all_to_all | solution.py:348
  139.1 0.1 slice.42
  139.2 1.2 shard_map.185
  140.4 6.8 %all-to-all-done.5 = bf16[8,4,16,384]{3,2,1,0:T(8,128)(2,1)S(1)} async-done(((bf16[8,4,16,384]{3,2,1,0:T(8,128)(2,1)}), bf16[8,4,16,384]{3,2,1,0:T(8,128)(2,1)S(1)}, u32[]{:S(2)}, u32[]{:S(2)}) %all-to-all-start.5) | async-done | bytes 393248 | tf_op jit(solution)/shard_map/all_to_all | solution.py:348
  147.2 0.1 bitcast_convert_fusion
  147.3 0.8 slice_bitcast_fusion
  148.2 0.6 slice_bitcast_fusion.2
  (22 shorter events, 0.2 us)
Async XLA Ops:
  0.6 0.7 copy-start.14
  1.3 0.8 copy-start
  2.2 0.8 copy-start.2
  3.0 1.0 copy-start.6
  19.2 18.1 %copy-start.1 = (bf16[1,128,256]{2,1,0:T(8,128)(2,1)S(1)}, bf16[1,128,256]{2,1,0:T(8,128)(2,1)}, u32[]{:S(2)}) copy-start(bf16[1,128,256]{2,1,0:T(8,128)(2,1)} %param.14) | copy-start | bytes 196612
  19.2 18.1 %copy-start.5 = (bf16[256,256]{1,0:T(8,128)(2,1)S(1)}, bf16[256,256]{1,0:T(8,128)(2,1)}, u32[]{:S(2)}) copy-start(bf16[256,256]{1,0:T(8,128)(2,1)} %wm_ref.3) | copy-start | bytes 393220
  19.2 41.5 %all-to-all-start.1 = ((bf16[16,16,384]{2,1,0:T(8,128)(2,1)}), bf16[16,16,384]{2,1,0:T(8,128)(2,1)S(1)}, u32[]{:S(2)}, u32[]{:S(2)}) async-start(bf16[16,16,384]{2,1,0:T(8,128)(2,1)} %bitcast.4), calls=%async_computation.1 | async-start | bytes 393216 | tf_op jit(solution)/shard_map/all_to_all | solution.py:348
  37.2 0.7 copy-start.10
  37.9 8.9 %copy-start.12 = (s32[1,128,32]{1,2,0:T(8,128)S(1)}, s32[1,128,32]{1,2,0:T(8,128)}, u32[]{:S(2)}) copy-start(s32[1,128,32]{1,2,0:T(8,128)} %param.17) | copy-start | bytes 49156
  38.3 10.2 %collective-permute-start = (bf16[32,256]{1,0:T(8,128)(2,1)S(1)}, bf16[32,256]{1,0:T(8,128)(2,1)S(1)}, u32[]{:S(2)}, u32[]{:S(2)}) collective-permute-start(bf16[32,256]{1,0:T(8,128)(2,1)S(1)} %get-tuple-element.25), channel_id=1, source_target_pairs={{0,1},{1,2},{2,3},{3,4},{4,5},{5,6},{6,7},{7,8},{8,9},{9,10},{10,1... | collective-permute-start | bytes 49160 | tf_op jit(solution)/shard_map/ppermute | solution.py:382
  40.5 8.1 %collective-permute-start.1 = (bf16[32,256]{1,0:T(8,128)(2,1)S(1)}, bf16[32,256]{1,0:T(8,128)(2,1)S(1)}, u32[]{:S(2)}, u32[]{:S(2)}) collective-permute-start(bf16[32,256]{1,0:T(8,128)(2,1)S(1)} %get-tuple-element.26), channel_id=1, source_target_pairs={{0,63},{1,0},{2,1},{3,2},{4,3},{5,4},{6,5},{7,6},{8,7},{9,8},{10,9... | collective-permute-start | bytes 49160 | tf_op jit(solution)/shard_map/ppermute | solution.py:382
  46.9 0.7 copy-start.13
  47.6 0.9 copy-start.3
  47.6 0.9 copy-start.7
  48.5 0.7 copy-start.11
  52.1 14.4 %copy-start.4 = (bf16[256,256]{1,0:T(8,128)(2,1)S(1)}, bf16[256,256]{1,0:T(8,128)(2,1)}, u32[]{:S(2)}) copy-start(bf16[256,256]{1,0:T(8,128)(2,1)} %wc_ref.1) | copy-start | bytes 393220
  52.1 8.6 %collective-permute-start.2 = (bf16[32,256]{1,0:T(8,128)(2,1)S(1)}, bf16[32,256]{1,0:T(8,128)(2,1)S(1)}, u32[]{:S(2)}, u32[]{:S(2)}) collective-permute-start(bf16[32,256]{1,0:T(8,128)(2,1)S(1)} %get-tuple-element.28), channel_id=1, source_target_pairs={{0,63},{1,0},{2,1},{3,2},{4,3},{5,4},{6,5},{7,6},{8,7},{9,8},{10,9... | collective-permute-start | bytes 49160 | tf_op jit(solution)/shard_map/ppermute | solution.py:382
  58.7 7.8 %collective-permute-start.3 = (bf16[32,256]{1,0:T(8,128)(2,1)S(1)}, bf16[32,256]{1,0:T(8,128)(2,1)S(1)}, u32[]{:S(2)}, u32[]{:S(2)}) collective-permute-start(bf16[32,256]{1,0:T(8,128)(2,1)S(1)} %get-tuple-element.29), channel_id=1, source_target_pairs={{0,1},{1,2},{2,3},{3,4},{4,5},{5,6},{6,7},{7,8},{8,9},{9,10},{10,1... | collective-permute-start | bytes 49160 | tf_op jit(solution)/shard_map/ppermute | solution.py:382
  60.6 5.9 %copy-start.8 = (bf16[20,256]{1,0:T(8,128)(2,1)S(1)}, bf16[20,256]{1,0:T(8,128)(2,1)}, u32[]{:S(2)}) copy-start(bf16[20,256]{1,0:T(8,128)(2,1)} %refs_4_.1) | copy-start | bytes 30724
  60.6 5.9 %copy-start.9 = (s32[3,512]{1,0:T(4,128)S(1)}, s32[3,512]{1,0:T(4,128)}, u32[]{:S(2)}) copy-start(s32[3,512]{1,0:T(4,128)} %refs_2_.1) | copy-start | bytes 18436
  129.3 18.0 %all-to-all-start.5 = ((bf16[8,4,16,384]{3,2,1,0:T(8,128)(2,1)}), bf16[8,4,16,384]{3,2,1,0:T(8,128)(2,1)S(1)}, u32[]{:S(2)}, u32[]{:S(2)}) async-start(bf16[8,4,16,384]{3,2,1,0:T(8,128)(2,1)} %broadcast_in_dim.28), calls=%async_computation.5 | async-start | bytes 786432 | tf_op jit(solution)/shard_map/all_to_all | solution.py:348

commit v2 on v1

--- a/solution.py
+++ b/solution.py
@@ -21,6 +21,7 @@
 PACK_ROWS = 16
 PACK_COLS = 384
 GRAD_CHUNKS = 32
+TAIL_ROWS = 32
 
 NN = (((1,), (0,)), ((), ()))
 NT = (((1,), (1,)), ((), ()))
@@ -92,7 +93,8 @@
         ref[...] = dot(pick.astype(f32).astype(bf16), act, TN).astype(bf16)
 
 
-def wave_kernel(count_ref, feat_ref, cot_ref, frac_ref, rows_ref, table_ref, sums_ref):
+def share_kernel(count_ref, feat_ref, cot_ref, frac_ref, out_ref):
+    copies = out_ref.shape[0]
     atoms, channels = feat_ref.shape
     live = column_iota((atoms, channels), 0) < count_ref[0, 0]
     zero = jnp.zeros((atoms, channels), f32)
@@ -104,24 +106,41 @@
     coords = jnp.where(which == 1, frac[1:2, :], coords)
     coords = jnp.where(which == 2, frac[2:3, :], coords)
     coords = jnp.where(which == 3, 1.0, coords)
-    high = coords.astype(bf16)
-    rest = coords - high.astype(f32)
-    middle = rest.astype(bf16)
-    low = (rest - middle.astype(f32)).astype(bf16)
-    rows = rows_ref[...]
-    turns = dot(rows, high) + (dot(rows, middle) + dot(rows, low))
-    table = cosine_of_turns(turns)
-    total = table.shape[0]
+    high = coords.astype(bf16).astype(f32)
+    middle = (coords - high).astype(bf16).astype(f32)
+    low = (coords - high) - middle
+    left = jnp.concatenate([high, low], axis=0)
+    right = jnp.concatenate([middle, jnp.zeros_like(low)], axis=0)
+    coords = jnp.concatenate([left, right], axis=1).astype(bf16)
+    for copy in range(copies):
+        out_ref[copy, 0:atoms, :] = feat
+        out_ref[copy, atoms : 2 * atoms, :] = cot
+        out_ref[copy, 2 * atoms : 2 * atoms + 16, :] = coords
+
+
+def wave_kernel(place_ref, atoms_ref, rows_ref, table_ref, sums_ref):
+    peers = atoms_ref.shape[0]
+    channels = atoms_ref.shape[2]
+    atoms = channels // 2
+    total = table_ref.shape[0]
     owners = total // ROWS_OWN
-    table = table.reshape(owners, ROWS_OWN, atoms)
+    rows = rows_ref[pl.ds(pl.multiple_of(place_ref[0] * total, 16), total), :]
+    sums = jnp.zeros((total, channels), f32)
     first = column_iota((owners, ROWS_OWN, atoms), 1) < ROWS_OWN // 2
-    nothing = jnp.zeros_like(table)
-    both = jnp.concatenate(
-        [jnp.where(first, table, nothing), jnp.where(first, nothing, table)], axis=-1
-    )
-    both = both.reshape(total, 2 * atoms).astype(bf16)
-    table_ref[...] = both
-    sums = dot(both, jnp.concatenate([feat, cot], axis=0))
+    for peer in range(peers):
+        coords = atoms_ref[peer, 2 * atoms :, :].astype(f32)
+        high = coords[0:8, :atoms].astype(bf16)
+        middle = coords[0:8, atoms:].astype(bf16)
+        low = coords[8:16, :atoms].astype(bf16)
+        turns = dot(rows, high) + (dot(rows, middle) + dot(rows, low))
+        table = cosine_of_turns(turns).reshape(owners, ROWS_OWN, atoms)
+        nothing = jnp.zeros_like(table)
+        both = jnp.concatenate(
+            [jnp.where(first, table, nothing), jnp.where(first, nothing, table)], axis=-1
+        )
+        both = both.reshape(total, 2 * atoms).astype(bf16)
+        table_ref[:, 2 * atoms * peer : 2 * atoms * (peer + 1)] = both
+        sums = sums + dot(both, atoms_ref[peer, : 2 * atoms, :])
     sums_ref[...] = packed(sums.reshape(owners, ROWS_OWN, channels)).astype(bf16)
 
 
@@ -146,7 +165,7 @@
     push_s,
 ):
     atoms, channels = act_ref.shape
-    slots = index_ref.shape[1]
+    slots = index_ref.shape[0]
     bins = wf_ref.shape[0]
     ghosts = lower_ref.shape[0]
     table = atoms + 2 * ghosts
@@ -155,8 +174,8 @@
         [act_ref[...].astype(f32), lower_ref[...].astype(f32), upper_ref[...].astype(f32)], axis=0
     )
     ext_t = ext.T.astype(bf16)
-    index_t = index_ref[...].T
-    length_t = length_ref[...].T
+    index_t = index_ref[...]
+    length_t = length_ref[...]
     live = column_iota((1, atoms), 1) < count_ref[0, 0]
     cot_t = jnp.where(live, cot_ref[...].astype(f32).T, 0.0)
     cot_pair = jnp.concatenate([cot_t, cot_t], axis=1)
@@ -193,6 +212,42 @@
     own_ref[...] = ext_grad[:atoms]
     to_lower_ref[...] = ext_grad[atoms : atoms + ghosts].astype(bf16)
     to_upper_ref[...] = ext_grad[atoms + ghosts :].astype(bf16)
+
+
+def total_of(parts_ref, rows=slice(None)):
+    total = parts_ref[0, rows].astype(f32)
+    for part in range(1, parts_ref.shape[0]):
+        total = total + parts_ref[part, rows].astype(f32)
+    return total
+
+
+def join_kernel(parts_ref, weights_ref, out_ref):
+    total = total_of(parts_ref).astype(bf16)
+    both = jnp.concatenate([weights_ref[...], total], axis=0)
+    out_ref[...] = jnp.broadcast_to(both[None], out_ref.shape)
+
+
+def apply_kernel(parts_ref, table_ref, out_ref):
+    peers, rows, channels = out_ref.shape
+    owners = parts_ref.shape[0]
+    total = table_ref.shape[0]
+    weights = unpacked(parts_ref[:, :PACK_ROWS, :].astype(f32))
+    weights = weights.reshape(total, channels).astype(bf16)
+    grads = unpacked(total_of(parts_ref, slice(PACK_ROWS, 2 * PACK_ROWS)))
+    grads = jnp.concatenate([grads, jnp.zeros((TAIL_ROWS - ROWS_OWN, channels), f32)], axis=0)
+    grads = grads.astype(bf16)
+    body_rows = rows - TAIL_ROWS
+    for peer in range(peers):
+        piece = table_ref[:, body_rows * peer : body_rows * (peer + 1)]
+        out_ref[peer, :body_rows, :] = dot(piece, weights, TN).astype(bf16)
+        out_ref[peer, body_rows:, :] = grads
+
+
+def hand_on_kernel(parts_ref, out_ref):
+    copies, peers, rows, channels = out_ref.shape
+    first = parts_ref.shape[1] - rows
+    tails = parts_ref[:, first:, :]
+    out_ref[...] = jnp.broadcast_to(tails[None], out_ref.shape)
 
 
 def wave_vector_length(slot):
@@ -239,7 +294,7 @@
     weights_ref,
 ):
     bins, channels = wk_ref.shape
-    sums = unpacked(sums_ref[...])
+    sums = unpacked(total_of(sums_ref))
     first_slot = (owner_ref[0] * SLOTS_OWN).astype(f32)
 
     def slot_of(shape, axis):
@@ -300,22 +355,10 @@
 
 
 def final_kernel(
-    count_ref,
-    table_ref,
-    weights_ref,
-    feat_ref,
-    messages_ref,
-    cot_ref,
-    pre_ref,
-    wm_ref,
-    wc_ref,
-    updated_ref,
-    grad_ref,
+    count_ref, parts_ref, feat_ref, messages_ref, cot_ref, pre_ref, wm_ref, wc_ref, updated_ref, grad_ref
 ):
     atoms, channels = feat_ref.shape
-    total = table_ref.shape[0]
-    rows = unpacked(weights_ref[...].astype(f32)).reshape(total, channels).astype(bf16)
-    both = dot(table_ref[...], rows, TN)
+    both = total_of(parts_ref, slice(0, 2 * atoms))
     live = column_iota((atoms, channels), 0) < count_ref[0, 0]
     added = jnp.where(live, messages_ref[...] + both[:atoms], 0.0)
     updated_ref[...] = (feat_ref[...].astype(f32) + added).astype(bf16)
@@ -325,6 +368,17 @@
         + dot(pre_ref[...], wm_ref[...], NT)
         + dot(charge_grad, wc_ref[...], NT)
     )
+
+
+def unpack_kernel(grads_ref, message_ref, charge_ref, filter_ref, kspace_ref):
+    channels = message_ref.shape[1]
+    grads = grads_ref[...].astype(f32)
+    message_ref[...] = grads[:, 0:8, :].reshape(channels, channels)
+    charge_ref[...] = grads[:, 8:16, :].reshape(channels, channels)
+    small = grads[:6, 16:24, :]
+    bins = filter_ref.shape[0]
+    filter_ref[...] = small[:3].reshape(ROWS_OWN, channels)[:bins]
+    kspace_ref[...] = small[3:].reshape(ROWS_OWN, channels)[:bins]
 
 
 def on_core(kernel, out_shape, in_smem, n_in, scratch=()):
@@ -346,10 +400,6 @@
 
 def exchanged(value, axis):
     return lax.all_to_all(value, axis, 0, 0, tiled=True)
-
-
-def summed(parts):
-    return jnp.sum(parts.astype(f32), axis=0)
 
 
 def body(
@@ -392,18 +442,14 @@
         0,
         3,
     )(feat, w_message, lists)
+    block = 2 * atoms + 16
+    shared = on_core(share_kernel, [shape((size_y, block, channels), bf16)], 1, 4)(
+        counts, feat, cot, fractional[0]
+    )[0]
+    shared, up, down = lax.optimization_barrier((shared, up, down))
+    shared = exchanged(shared, "y")
     from_lower = passed_along(up, 1)
     from_upper = passed_along(down, -1)
-
-    total = domains * ROWS_OWN
-    table, sums = on_core(
-        wave_kernel,
-        [shape((total, 2 * atoms), bf16), shape((domains, PACK_ROWS, PACK_COLS), bf16)],
-        1,
-        5,
-    )(counts, feat, cot, fractional[0], jnp.asarray(wave_rows(domains), bf16))
-    sums = exchanged(sums.reshape(size_y, size_z * PACK_ROWS, PACK_COLS), "y")
-    sums = summed(sums).astype(bf16)
 
     messages, own, to_lower, to_upper, filter_term = on_core(
         edge_kernel,
@@ -427,18 +473,28 @@
         act,
         from_lower,
         from_upper,
-        neighbor_index[0],
+        neighbor_index[0].T,
         neighbor_count,
-        distances[0],
+        distances[0].T,
         w_filter,
         cot,
     )
+    place_y, place_z = lax.axis_index("y"), lax.axis_index("z")
+    total = size_z * ROWS_OWN
+    table, sums = on_core(
+        wave_kernel,
+        [
+            shape((total, size_y * 2 * atoms), bf16),
+            shape((size_z, PACK_ROWS, PACK_COLS), bf16),
+        ],
+        1,
+        3,
+    )(place_y.reshape(1).astype(jnp.int32), shared, jnp.asarray(wave_rows(domains), bf16))
+    sums, to_lower, to_upper = lax.optimization_barrier((sums, to_lower, to_upper))
     back_upper = passed_along(to_lower, -1)
     back_lower = passed_along(to_upper, 1)
-
-    sums = exchanged(sums.reshape(size_z, PACK_ROWS, PACK_COLS), "z")
-    sums = summed(sums)
-    owner = lax.axis_index("y") * size_z + lax.axis_index("z")
+    sums = exchanged(sums, "z")
+    owner = place_y * size_z + place_z
     pre, grads, weights = on_core(
         lambda *refs: middle_kernel(scale, *refs),
         [
@@ -462,40 +518,38 @@
         feat,
         filter_term,
     )
-    grads = exchanged(grads, ("x", "core", "y"))
-    grads = summed(grads).astype(bf16)
-    both = jnp.concatenate([weights, grads], axis=0)
-    both = exchanged(jnp.broadcast_to(both[None], (size_z,) + both.shape), "z")
-    weights = both[:, :PACK_ROWS].reshape(size_z * PACK_ROWS, PACK_COLS)
-    grads = summed(both[:, PACK_ROWS:]).astype(bf16)
-    both = jnp.concatenate([weights, grads], axis=0)
-    both = exchanged(jnp.broadcast_to(both[None], (size_y,) + both.shape), "y")
-    weights = both[:, : size_z * PACK_ROWS].reshape(domains, PACK_ROWS, PACK_COLS)
-    grads = both[:, size_z * PACK_ROWS :]
+    parts = exchanged(grads, ("x", "core", "y"))
+    parts = on_core(join_kernel, [shape((size_z, 2 * PACK_ROWS, PACK_COLS), bf16)], 0, 2)(
+        parts, weights
+    )[0]
+    parts = exchanged(parts, "z")
+    rows = 2 * atoms + TAIL_ROWS
+    parts = on_core(apply_kernel, [shape((size_y, rows, channels), bf16)], 0, 2)(parts, table)[0]
+    parts = exchanged(parts, "y")
     slabs = lax.axis_size("x") * lax.axis_size("core")
-    grads = exchanged(jnp.broadcast_to(grads[None], (slabs,) + grads.shape), ("x", "core"))
-    grads = grads.reshape(GRAD_CHUNKS, PACK_ROWS, PACK_COLS)
+    grads = on_core(hand_on_kernel, [shape((slabs, size_y, TAIL_ROWS, channels), bf16)], 0, 1)(
+        parts
+    )[0]
+    grads = exchanged(grads, ("x", "core")).reshape(GRAD_CHUNKS, TAIL_ROWS, channels)
 
     updated, grad_features = on_core(
         final_kernel,
         [shape((atoms, channels), bf16), shape((atoms, channels), f32)],
         1,
-        9,
-    )(counts, table, weights, feat, messages, cot, pre, w_message, w_charge)
-
-    grads = grads.astype(f32)
-    grad_message = grads[:, 0:8, :channels].reshape(channels, channels)
-    grad_charge = grads[:, 8:16, :channels].reshape(channels, channels)
-    small = jnp.concatenate([grads[:6, 0:8, channels:], grads[:6, 8:16, channels:]], axis=2)
-    small = small.reshape(2, ROWS_OWN, channels)
-    return (
-        updated[None],
-        grad_features[None],
-        grad_message,
-        grad_charge,
-        small[0, :bins],
-        small[1, :bins],
-    )
+        8,
+    )(counts, parts, feat, messages, cot, pre, w_message, w_charge)
+    grad_message, grad_charge, grad_filter, grad_kspace = on_core(
+        unpack_kernel,
+        [
+            shape((channels, channels), f32),
+            shape((channels, channels), f32),
+            shape((bins, channels), f32),
+            shape((bins, channels), f32),
+        ],
+        0,
+        1,
+    )(grads)
+    return (updated[None], grad_features[None], grad_message, grad_charge, grad_filter, grad_kspace)
 
 
 def solution(mesh):

time: 150 us -> 135 us (0.900)
  blocking collectives: 74.1 us -> 56.3 us
  local copies, waits for them, and re-layouts: 7.26 us -> 3.63 us
  Pallas kernels: 6.35 us -> 9.31 us
  starting transfers between devices: 45.1 us -> 47.9 us
  waiting for transfers between devices: 13.4 us -> 15.8 us
    all_to_all x4 -> x3, blocking collectives: 74.1 us -> 56.3 us  [exchanged(): return lax.all_to_all(value, axis, 0, 0, tiled=True)]
    ppermute x4, starting transfers between devices: 17.1 us -> 24.5 us  [passed_along(): lax.ppermute(value, space, [(s, (s + steps) % domains) for s in range(dom...]
    all_to_all x2 -> x3, starting transfers between devices: 27.9 us -> 23.4 us  [exchanged(): return lax.all_to_all(value, axis, 0, 0, tiled=True)]
    pallas_call x1 -> x6, Pallas kernels: 1.17 us -> 4.65 us  [the longest x1 1.55 us: body(): on_core(wave_kernel, [shape((total, size_y * 2 * atoms), bf16), shape((si...]
    all_to_all x2 -> x3, waiting for transfers between devices: 6.79 us -> 8.6 us  [exchanged(): return lax.all_to_all(value, axis, 0, 0, tiled=True)]
    unnamed x33 -> x31, local copies, waits for them, and re-layouts: 4.83 us -> 3.63 us
  transfers between devices with their start and end apart: 6 -> 7, of which waited for: 3 -> 3; matrix products, arithmetic and copies ran while one was open for 0% -> 0% of each run, Pallas kernels for 3% -> 3%
where the time goes in v2:
time: 135 us; the launch traced here: 134 us
  blocking collectives  56.3 us (42%)
  starting transfers between devices  47.9 us (35%)
  waiting for transfers between devices  15.8 us (12%)
  Pallas kernels  9.31 us (7%)
  local copies, waits for them, and re-layouts  3.63 us (3%)
  between operations  1.47 us (1%)
    all_to_all x3, blocking collectives, exchanged(): return lax.all_to_all(value, axis, 0, 0, tiled=True)  56.3 us
    ppermute x4, starting transfers between devices, passed_along(): lax.ppermute(value, space, [(s, (s + steps) % domains) for s in range(dom...  24.5 us
    all_to_all x3, starting transfers between devices, exchanged(): return lax.all_to_all(value, axis, 0, 0, tiled=True)  23.4 us
    all_to_all x3, waiting for transfers between devices, exchanged(): return lax.all_to_all(value, axis, 0, 0, tiled=True)  8.6 us
    ppermute x4, waiting for transfers between devices, passed_along(): lax.ppermute(value, space, [(s, (s + steps) % domains) for s in range(dom...  7.16 us
    unnamed x31, local copies, waits for them, and re-layouts  3.63 us
    pallas_call x1, Pallas kernels, body(): on_core(edge_kernel, [shape((atoms, channels), f32), shape((atoms, channe...  2.74 us
  transfers between devices with their start and end apart: 7, of which 3 were waited for; matrix products, arithmetic and copies ran while one was open for 0% of the time, Pallas kernels for 3%

profile of v2, /device:TPU:1, one launch (start us, length us, event | category | flops | bytes accessed | tf_op | source)
XLA Modules:
  0.0 134.3 jit_solution(6893131480205779508)
XLA Ops:
  0.6 0.0 copy-start.14
  1.3 0.0 copy-done.14
  1.3 0.0 copy-start.12
  1.3 0.7 copy-done.12
  2.0 0.0 copy-start
  2.0 0.8 copy-done
  2.8 0.0 copy-start.4
  2.8 0.9 copy-done.4
  3.7 0.0 copy-start.2
  3.8 0.3 shard_map.182
  4.1 0.5 copy-done.2
  4.6 0.9 shard_map.181
  5.5 5.2 %all-to-all-start = ((bf16[4,272,256]{2,1,0:T(8,128)(2,1)}), bf16[4,272,256]{2,1,0:T(8,128)(2,1)S(1)}, u32[]{:S(2)}, u32[]{:S(2)}) async-start(bf16[4,272,256]{2,1,0:T(8,128)(2,1)} %shard_map.181), calls=%async_computation | async-start | bytes 1114112 | tf_op jit(solution)/shard_map/all_to_all | solution.py:402
  10.6 3.4 %collective-permute-start = (bf16[32,256]{1,0:T(8,128)(2,1)S(1)}, bf16[32,256]{1,0:T(8,128)(2,1)S(1)}, u32[]{:S(2)}, u32[]{:S(2)}) collective-permute-start(bf16[32,256]{1,0:T(8,128)(2,1)S(1)} %get-tuple-element.37), channel_id=1, source_target_pairs={{0,1},{1,2},{2,3},{3,4},{4,5},{5,6},{6,7},{7,8},{8,9},{9,10},{10,1... | collective-permute-start | bytes 49160 | tf_op jit(solution)/shard_map/ppermute | solution.py:432
  14.0 12.1 %collective-permute-start.1 = (bf16[32,256]{1,0:T(8,128)(2,1)S(1)}, bf16[32,256]{1,0:T(8,128)(2,1)S(1)}, u32[]{:S(2)}, u32[]{:S(2)}) collective-permute-start(bf16[32,256]{1,0:T(8,128)(2,1)S(1)} %get-tuple-element.38), channel_id=1, source_target_pairs={{0,63},{1,0},{2,1},{3,2},{4,3},{5,4},{6,5},{7,6},{8,7},{9,8},{10,9... | collective-permute-start | bytes 49160 | tf_op jit(solution)/shard_map/ppermute | solution.py:432
  26.1 0.0 collective-permute-done.lower_ref
  26.1 0.8 collective-permute-done.1.upper_ref
  26.9 0.0 copy-done.7
  26.9 0.0 copy-done.8
  26.9 0.0 copy-done.9
  26.9 0.6 copy-done.13
  27.6 2.7 %shard_map.184 = (f32[128,256]{1,0:T(8,128)S(1)}, f32[128,256]{1,0:T(8,128)S(1)}, bf16[32,256]{1,0:T(8,128)(2,1)S(1)}, bf16[32,256]{1,0:T(8,128)(2,1)S(1)}, f32[24,256]{1,0:T(8,128)S(1)}) custom-call(s32[1,1]{1,0:T(1,128)S(6)} %copy.23.count_ref, bf16[128,256]{1,0:T(8,128)(2,1)S(1)} %get-tuple-element.36.act_ref, ...), custom_call_target="tpu_custom_call" | custom-call | tf_op jit(solution)/shard_map/pallas_call | solution.py:454
  30.3 0.0 all-to-all-done.atoms_ref
  30.3 0.0 copy-done.6
  30.3 1.5 %shard_map.183 = (bf16[384,1024]{1,0:T(8,128)(2,1)S(1)}, bf16[16,16,384]{2,1,0:T(8,128)(2,1)}) custom-call(s32[1]{0:T(128)} %bitcast.1.place_ref, bf16[4,272,256]{2,1,0:T(8,128)(2,1)S(1)} %all-to-all-done.atoms_ref, bf16[1536,8]{1,0:T(8,128)(2,1)S(1)} %copy-done.6), custom_call_target="tpu_custom_call" | custom-call | tf_op jit(solution)/shard_map/pallas_call | solution.py:484
  31.9 8.2 %all-to-all-start.1 = ((bf16[16,16,384]{2,1,0:T(8,128)(2,1)}), bf16[16,16,384]{2,1,0:T(8,128)(2,1)S(1)}, u32[]{:S(2)}, u32[]{:S(2)}) async-start(bf16[16,16,384]{2,1,0:T(8,128)(2,1)} %get-tuple-element.41), calls=%async_computation.1 | async-start | bytes 393216 | tf_op jit(solution)/shard_map/all_to_all | solution.py:402
  40.1 0.0 copy-start.10
  40.1 7.1 %collective-permute-start.2 = (bf16[32,256]{1,0:T(8,128)(2,1)S(1)}, bf16[32,256]{1,0:T(8,128)(2,1)S(1)}, u32[]{:S(2)}, u32[]{:S(2)}) collective-permute-start(bf16[32,256]{1,0:T(8,128)(2,1)S(1)} %get-tuple-element.43), channel_id=1, source_target_pairs={{0,63},{1,0},{2,1},{3,2},{4,3},{5,4},{6,5},{7,6},{8,7},{9,8},{10,9... | collective-permute-start | bytes 49160 | tf_op jit(solution)/shard_map/ppermute | solution.py:432
  47.3 1.9 %collective-permute-start.3 = (bf16[32,256]{1,0:T(8,128)(2,1)S(1)}, bf16[32,256]{1,0:T(8,128)(2,1)S(1)}, u32[]{:S(2)}, u32[]{:S(2)}) collective-permute-start(bf16[32,256]{1,0:T(8,128)(2,1)S(1)} %get-tuple-element.44), channel_id=1, source_target_pairs={{0,1},{1,2},{2,3},{3,4},{4,5},{5,6},{6,7},{7,8},{8,9},{9,10},{10,1... | collective-permute-start | bytes 49160 | tf_op jit(solution)/shard_map/ppermute | solution.py:432
  49.2 0.0 collective-permute-done.2.refs_6_
  49.2 6.3 %collective-permute-done.3.refs_7_ = bf16[32,256]{1,0:T(8,128)(2,1)S(1)} collective-permute-done((bf16[32,256]{1,0:T(8,128)(2,1)S(1)}, bf16[32,256]{1,0:T(8,128)(2,1)S(1)}, u32[]{:S(2)}, u32[]{:S(2)}) %collective-permute-start.3) | collective-permute-done | bytes 16416 | tf_op jit(solution)/shard_map/ppermute | solution.py:432
  55.5 0.0 all-to-all-done.1.refs_1_
  55.5 0.0 copy-done.1
  55.5 0.0 copy-done.3
  55.5 0.0 copy-done.11
  55.5 0.0 copy-done.10
  55.6 0.7 shard_map.185
  56.3 19.5 %all_to_all.30.parts_ref = bf16[32,16,384]{2,1,0:T(8,128)(2,1)S(1)} all-to-all(bf16[32,16,384]{2,1,0:T(8,128)(2,1)S(1)} %get-tuple-element.47), channel_id=1, replica_groups=mesh['x'=4,'core'=2,'z'=16,'y'=4] {'x','core','y'}, dimensions={0} | all-to-all | bytes 786432 | tf_op jit(solution)/shard_map/all_to_all | solution.py:402
  75.8 0.1 shard_map.186
  75.8 25.7 %all_to_all.31.parts_ref = bf16[16,32,384]{2,1,0:T(8,128)(2,1)S(1)} all-to-all(bf16[16,32,384]{2,1,0:T(8,128)(2,1)S(1)} %shard_map.186), channel_id=1, replica_groups=mesh['x'=4,'core'=2,'z'=16,'y'=4] {'z'}, dimensions={0} | all-to-all | bytes 786432 | tf_op jit(solution)/shard_map/all_to_all | solution.py:402
  101.5 0.5 shard_map.187
  102.0 11.1 %all_to_all.32.parts_ref = bf16[4,288,256]{2,1,0:T(8,128)(2,1)S(1)} all-to-all(bf16[4,288,256]{2,1,0:T(8,128)(2,1)S(1)} %shard_map.187), channel_id=1, replica_groups=mesh['x'=4,'core'=2,'z'=16,'y'=4] {'y'}, dimensions={0} | all-to-all | bytes 1179648 | tf_op jit(solution)/shard_map/all_to_all | solution.py:402
  113.1 0.9 shard_map.189
  114.0 10.0 %all-to-all-start.5 = ((bf16[8,4,32,256]{3,2,1,0:T(8,128)(2,1)}), bf16[8,4,32,256]{3,2,1,0:T(8,128)(2,1)S(1)}, u32[]{:S(2)}, u32[]{:S(2)}) async-start(bf16[8,4,32,256]{3,2,1,0:T(8,128)(2,1)} %shard_map.189), calls=%async_computation.5 | async-start | bytes 1048576 | tf_op jit(solution)/shard_map/all_to_all | solution.py:402
  124.0 0.0 copy-done.5
  124.0 0.9 shard_map.188
  124.9 8.6 %all-to-all-done.5 = bf16[8,4,32,256]{3,2,1,0:T(8,128)(2,1)S(1)} async-done(((bf16[8,4,32,256]{3,2,1,0:T(8,128)(2,1)}), bf16[8,4,32,256]{3,2,1,0:T(8,128)(2,1)S(1)}, u32[]{:S(2)}, u32[]{:S(2)}) %all-to-all-start.5) | async-done | bytes 524320 | tf_op jit(solution)/shard_map/all_to_all | solution.py:402
  133.5 0.8 shard_map.190
  (10 shorter events, 0.0 us)
Async XLA Ops:
  0.6 0.7 copy-start.14
  1.3 0.7 copy-start.12
  2.0 0.8 copy-start
  2.8 0.9 copy-start.4
  3.7 0.8 copy-start.2
  5.5 21.5 %copy-start.7 = (s32[1,128,32]{1,2,0:T(8,128)S(1)}, s32[1,128,32]{1,2,0:T(8,128)}, u32[]{:S(2)}) copy-start(s32[1,128,32]{1,2,0:T(8,128)} %param.17) | copy-start | bytes 49156
  5.5 21.5 %copy-start.8 = (f32[1,128,32]{1,2,0:T(8,128)S(1)}, f32[1,128,32]{1,2,0:T(8,128)}, u32[]{:S(2)}) copy-start(f32[1,128,32]{1,2,0:T(8,128)} %param.20) | copy-start | bytes 49156
  5.5 21.5 %copy-start.9 = (bf16[20,256]{1,0:T(8,128)(2,1)S(1)}, bf16[20,256]{1,0:T(8,128)(2,1)}, u32[]{:S(2)}) copy-start(bf16[20,256]{1,0:T(8,128)(2,1)} %wf_ref.1) | copy-start | bytes 30724
  5.5 24.9 %copy-start.6 = (bf16[1536,8]{1,0:T(8,128)(2,1)S(1)}, bf16[1536,8]{1,0:T(8,128)(2,1)}, u32[]{:S(2)}) copy-start(bf16[1536,8]{1,0:T(8,128)(2,1)} %constant.13.clone.rows_ref) | copy-start | bytes 73732
  5.5 24.8 %all-to-all-start = ((bf16[4,272,256]{2,1,0:T(8,128)(2,1)}), bf16[4,272,256]{2,1,0:T(8,128)(2,1)S(1)}, u32[]{:S(2)}, u32[]{:S(2)}) async-start(bf16[4,272,256]{2,1,0:T(8,128)(2,1)} %shard_map.181), calls=%async_computation | async-start | bytes 1114112 | tf_op jit(solution)/shard_map/all_to_all | solution.py:402
  10.6 15.4 %collective-permute-start = (bf16[32,256]{1,0:T(8,128)(2,1)S(1)}, bf16[32,256]{1,0:T(8,128)(2,1)S(1)}, u32[]{:S(2)}, u32[]{:S(2)}) collective-permute-start(bf16[32,256]{1,0:T(8,128)(2,1)S(1)} %get-tuple-element.37), channel_id=1, source_target_pairs={{0,1},{1,2},{2,3},{3,4},{4,5},{5,6},{6,7},{7,8},{8,9},{9,10},{10,1... | collective-permute-start | bytes 49160 | tf_op jit(solution)/shard_map/ppermute | solution.py:432
  14.0 12.9 %collective-permute-start.1 = (bf16[32,256]{1,0:T(8,128)(2,1)S(1)}, bf16[32,256]{1,0:T(8,128)(2,1)S(1)}, u32[]{:S(2)}, u32[]{:S(2)}) collective-permute-start(bf16[32,256]{1,0:T(8,128)(2,1)S(1)} %get-tuple-element.38), channel_id=1, source_target_pairs={{0,63},{1,0},{2,1},{3,2},{4,3},{5,4},{6,5},{7,6},{8,7},{9,8},{10,9... | collective-permute-start | bytes 49160 | tf_op jit(solution)/shard_map/ppermute | solution.py:432
  26.9 0.7 copy-start.13
  31.9 23.7 %copy-start.1 = (bf16[1,128,256]{2,1,0:T(8,128)(2,1)S(1)}, bf16[1,128,256]{2,1,0:T(8,128)(2,1)}, u32[]{:S(2)}) copy-start(bf16[1,128,256]{2,1,0:T(8,128)(2,1)} %param.14) | copy-start | bytes 196612
  31.9 23.7 %copy-start.3 = (bf16[256,256]{1,0:T(8,128)(2,1)S(1)}, bf16[256,256]{1,0:T(8,128)(2,1)}, u32[]{:S(2)}) copy-start(bf16[256,256]{1,0:T(8,128)(2,1)} %wc_ref.1) | copy-start | bytes 393220
  31.9 23.7 %copy-start.11 = (s32[3,512]{1,0:T(4,128)S(1)}, s32[3,512]{1,0:T(4,128)}, u32[]{:S(2)}) copy-start(s32[3,512]{1,0:T(4,128)} %refs_2_.1) | copy-start | bytes 18436
  31.9 23.6 %all-to-all-start.1 = ((bf16[16,16,384]{2,1,0:T(8,128)(2,1)}), bf16[16,16,384]{2,1,0:T(8,128)(2,1)S(1)}, u32[]{:S(2)}, u32[]{:S(2)}) async-start(bf16[16,16,384]{2,1,0:T(8,128)(2,1)} %get-tuple-element.41), calls=%async_computation.1 | async-start | bytes 393216 | tf_op jit(solution)/shard_map/all_to_all | solution.py:402
  40.1 15.4 %copy-start.10 = (bf16[20,256]{1,0:T(8,128)(2,1)S(1)}, bf16[20,256]{1,0:T(8,128)(2,1)}, u32[]{:S(2)}) copy-start(bf16[20,256]{1,0:T(8,128)(2,1)} %refs_4_.1) | copy-start | bytes 30724
  40.1 9.1 %collective-permute-start.2 = (bf16[32,256]{1,0:T(8,128)(2,1)S(1)}, bf16[32,256]{1,0:T(8,128)(2,1)S(1)}, u32[]{:S(2)}, u32[]{:S(2)}) collective-permute-start(bf16[32,256]{1,0:T(8,128)(2,1)S(1)} %get-tuple-element.43), channel_id=1, source_target_pairs={{0,63},{1,0},{2,1},{3,2},{4,3},{5,4},{6,5},{7,6},{8,7},{9,8},{10,9... | collective-permute-start | bytes 49160 | tf_op jit(solution)/shard_map/ppermute | solution.py:432
  47.3 8.3 %collective-permute-start.3 = (bf16[32,256]{1,0:T(8,128)(2,1)S(1)}, bf16[32,256]{1,0:T(8,128)(2,1)S(1)}, u32[]{:S(2)}, u32[]{:S(2)}) collective-permute-start(bf16[32,256]{1,0:T(8,128)(2,1)S(1)} %get-tuple-element.44), channel_id=1, source_target_pairs={{0,1},{1,2},{2,3},{3,4},{4,5},{5,6},{6,7},{7,8},{8,9},{9,10},{10,1... | collective-permute-start | bytes 49160 | tf_op jit(solution)/shard_map/ppermute | solution.py:432
  114.0 10.0 %copy-start.5 = (bf16[256,256]{1,0:T(8,128)(2,1)S(1)}, bf16[256,256]{1,0:T(8,128)(2,1)}, u32[]{:S(2)}) copy-start(bf16[256,256]{1,0:T(8,128)(2,1)} %wm_ref.3) | copy-start | bytes 393220
  114.0 19.5 %all-to-all-start.5 = ((bf16[8,4,32,256]{3,2,1,0:T(8,128)(2,1)}), bf16[8,4,32,256]{3,2,1,0:T(8,128)(2,1)S(1)}, u32[]{:S(2)}, u32[]{:S(2)}) async-start(bf16[8,4,32,256]{3,2,1,0:T(8,128)(2,1)} %shard_map.189), calls=%async_computation.5 | async-start | bytes 1048576 | tf_op jit(solution)/shard_map/all_to_all | solution.py:402

commit v3 on v2

v3 whole, which is shorter than its diff:
```python
import math

import jax
import jax.numpy as jnp
import numpy as np
from jax import lax
from jax.experimental import pallas as pl
from jax.experimental.pallas import tpu as pltpu
from jax.sharding import Mesh, PartitionSpec as P

cutoff_radius = 5.0
kspace_limit = 8.0 * math.pi * math.sqrt(3.0)
ewald_scale_factor = 4.0
two_pi = 2.0 * math.pi

bf16 = jnp.bfloat16
f32 = jnp.float32

SLOTS_OWN = 6
ROWS_OWN = 4 * SLOTS_OWN
LANES = 128
PACK_ROWS = 2 * ROWS_OWN
GRAD_CHUNKS = 32
CHUNK_ROWS = 40

NN = (((1,), (0,)), ((), ()))
NT = (((1,), (1,)), ((), ()))
TN = (((0,), (0,)), ((), ()))


def dot(left, right, dims=NN, precision=None):
    return lax.dot_general(left, right, dims, precision=precision, preferred_element_type=f32)


def cosine_coefficients():
    nodes = np.cos((np.arange(64) + 0.5) * np.pi / 64)
    u = 0.125 + 0.125 * nodes
    fit = np.polynomial.chebyshev.Chebyshev.fit(u, np.cos(two_pi * np.sqrt(u)), 7, domain=[0.0, 0.25])
    return [float(c) for c in fit.convert(kind=np.polynomial.Polynomial).coef]


COSINE = cosine_coefficients()


def cosine_of_turns(turns):
    r = turns - jnp.floor(turns + 0.5)
    u = r * r
    out = jnp.full_like(u, COSINE[-1])
    for c in COSINE[-2::-1]:
        out = out * u + c
    return out


def wave_rows(owners):
    rows = np.zeros((owners * ROWS_OWN, 8), np.float32)
    for owner in range(owners):
        for place in range(ROWS_OWN):
            v = owner * SLOTS_OWN + place % SLOTS_OWN + 1
            nz = (v + 4) % 9 - 4
            m = (v - nz) // 9
            ny = (m + 4) % 9 - 4
            nx = (m - ny) // 9
            quarter = -0.25 if (place // SLOTS_OWN) % 2 else 0.0
            rows[owner * ROWS_OWN + place, :4] = (nx, ny, nz, quarter)
    return rows


def packed(rows):
    return jnp.concatenate([rows[..., :LANES], rows[..., LANES:]], axis=-2)


def unpacked(rows):
    half = rows.shape[-2] // 2
    return jnp.concatenate([rows[..., :half, :], rows[..., half:, :]], axis=-1)


def column_iota(shape, axis):
    return lax.broadcasted_iota(jnp.int32, shape, axis)


def silu(value):
    return value * jax.nn.sigmoid(value)


NO_ROW = 255


def first_kernel(
    count_ref,
    feat_ref,
    cot_ref,
    frac_ref,
    list_ref,
    index_ref,
    used_ref,
    length_ref,
    shared_ref,
    block_ref,
    list_s,
):
    copies = shared_ref.shape[0]
    atoms, channels = feat_ref.shape
    ghosts = list_ref.shape[1]
    slots = index_ref.shape[0]
    live = column_iota((atoms, channels), 0) < count_ref[0, 0]
    zero = jnp.zeros((atoms, channels), f32)
    feat = jnp.where(live, feat_ref[...].astype(f32), zero).astype(bf16)
    cot = jnp.where(live, cot_ref[...].astype(f32), zero).astype(bf16)
    frac = frac_ref[...]
    which = column_iota((8, atoms), 0)
    coords = jnp.where(which == 0, frac[0:1, :], 0.0)
    coords = jnp.where(which == 1, frac[1:2, :], coords)
    coords = jnp.where(which == 2, frac[2:3, :], coords)
    coords = jnp.where(which == 3, 1.0, coords)
    high, middle, low = split_three(coords)
    list_s[...] = jnp.zeros_like(list_s)
    list_s[0:2, 0:ghosts] = list_ref[...].astype(f32)
    left = jnp.concatenate([high, low], axis=0)
    right = jnp.concatenate([middle, list_s[...]], axis=0)
    coords = jnp.concatenate([left, right], axis=1).astype(bf16)
    valid = column_iota((slots, atoms), 0) < used_ref[...]
    index = jnp.where(valid, index_ref[...], NO_ROW).astype(f32)
    high, middle, low = split_three(length_ref[...])
    edges = jnp.concatenate(
        [jnp.concatenate([index, high], axis=1), jnp.concatenate([middle, low], axis=1)], axis=0
    ).astype(bf16)

    def fill(ref):
        ref[0:atoms, :] = feat
        ref[atoms : 2 * atoms, :] = cot
        ref[2 * atoms : 2 * atoms + 16, :] = coords
        ref[2 * atoms + 16 :, :] = edges

    for copy in range(copies):
        fill(shared_ref.at[copy])
    fill(block_ref)


def split_three(value):
    high = value.astype(bf16).astype(f32)
    middle = (value - high).astype(bf16).astype(f32)
    return high, middle, (value - high) - middle


def wave_kernel(place_ref, atoms_ref, rows_ref, table_ref, sums_ref):
    peers = atoms_ref.shape[0]
    channels = atoms_ref.shape[2]
    atoms = channels // 2
    total = table_ref.shape[0]
    owners = total // ROWS_OWN
    rows = rows_ref[pl.ds(pl.multiple_of(place_ref[0] * total, 16), total), :]
    sums = jnp.zeros((total, channels), f32)
    first = column_iota((owners, ROWS_OWN, atoms), 1) < ROWS_OWN // 2
    for peer in range(peers):
        coords = atoms_ref[peer, 2 * atoms : 2 * atoms + 16, :].astype(f32)
        high = coords[0:8, :atoms].astype(bf16)
        middle = coords[0:8, atoms:].astype(bf16)
        low = coords[8:16, :atoms].astype(bf16)
        turns = dot(rows, high) + (dot(rows, middle) + dot(rows, low))
        table = cosine_of_turns(turns).reshape(owners, ROWS_OWN, atoms)
        nothing = jnp.zeros_like(table)
        both = jnp.concatenate(
            [jnp.where(first, table, nothing), jnp.where(first, nothing, table)], axis=-1
        )
        both = both.reshape(total, 2 * atoms).astype(bf16)
        table_ref[:, 2 * atoms * peer : 2 * atoms * (peer + 1)] = both
        sums = sums + dot(both, atoms_ref[peer, : 2 * atoms, :])
    sums_ref[...] = packed(sums.reshape(owners, ROWS_OWN, channels)).astype(bf16)


def edge_kernel(
    count_ref,
    place_ref,
    feat_ref,
    wrap_ref,
    shared_ref,
    wm_ref,
    index_ref,
    used_ref,
    length_ref,
    wf_ref,
    cot_ref,
    list_ref,
    messages_ref,
    pre_ref,
    message_ref,
    filter_ref,
    pick_s,
    basis_s,
    grad_s,
    push_s,
    near_pick_s,
    near_push_s,
    near_s,
):
    atoms, channels = feat_ref.shape
    slots = index_ref.shape[0]
    ghosts = list_ref.shape[1]
    bins = wf_ref.shape[0]
    table = atoms + 2 * ghosts
    padded = basis_s.shape[0]
    peers = shared_ref.shape[0]
    place = place_ref[0]
    at_end = [place == 0, place == peers - 1]
    beside = [lax.rem(place + peers - 1, peers), lax.rem(place + 1, peers)]

    def take_block(side):
        @pl.when(at_end[side])
        def _():
            near_s[side] = wrap_ref[...]

        @pl.when(jnp.logical_not(at_end[side]))
        def _():
            near_s[side] = shared_ref[beside[side]]

    take_block(0)
    take_block(1)

    def ghost_rows(side):
        lists = near_s[side, 2 * atoms : 2 * atoms + 16, :].astype(f32)[8:16, atoms:]
        picked = lists[1 - side : 2 - side, :ghosts]
        rows = column_iota((atoms, ghosts), 0).astype(f32) == picked
        rows = dot(rows.astype(f32).astype(bf16), near_s[side, :atoms, :], TN).astype(bf16)
        return silu(dot(rows, wm_ref[...])).astype(bf16).astype(f32)

    hidden = dot(feat_ref[...], wm_ref[...])
    act = silu(hidden).astype(bf16).astype(f32)
    ext_t = jnp.concatenate([act, ghost_rows(0), ghost_rows(1)], axis=0).T.astype(bf16)
    bin_at = column_iota((padded, 2 * atoms), 0).astype(f32)
    spacing = cutoff_radius / (bins - 1)
    wf = wf_ref[...]

    def envelope_of(length, valid):
        envelope = 0.5 * (jnp.cos(math.pi * length / cutoff_radius) + 1.0)
        return jnp.where(valid, envelope, 0.0)

    def paired(rows, j):
        return jnp.concatenate([rows[j : j + 1, :], rows[j + 1 : j + 2, :]], axis=1)

    def basis_of(length, envelope, j):
        scaled = (paired(length, j) - cutoff_radius * bin_at / (bins - 1)) / spacing
        basis = jnp.exp(-0.5 * scaled * scaled) * paired(envelope, j)
        return jnp.where(bin_at < bins, basis, 0.0).astype(bf16)

    def doubled(value):
        return jnp.concatenate([value, value], axis=1)

    index = index_ref[...]
    length = length_ref[...]
    live = column_iota((1, atoms), 1) < count_ref[0, 0]
    cot_pair = doubled(jnp.where(live, cot_ref[...].astype(f32).T, 0.0))
    used = jnp.where(live, used_ref[...], 0)
    envelope = envelope_of(length, column_iota((slots, atoms), 0) < used)
    row_at = column_iota((table, 2 * atoms), 0)
    total = jnp.zeros((channels, 2 * atoms), f32)
    for step in range(slots // 2):
        j = 2 * step
        here = pl.ds(step * 2 * atoms, 2 * atoms)
        basis = basis_of(length, envelope, j)
        basis_s[:, here] = basis
        weights = dot(wf, basis[:bins], TN)
        pick = jnp.where(row_at == paired(index, j), 1.0, 0.0).astype(bf16)
        pick_s[:, here] = pick[:atoms]
        gathered = dot(ext_t, pick)
        total = total + weights * gathered
        grad_s[:, here] = (cot_pair * gathered).astype(bf16)
        push_s[:, here] = (cot_pair * weights).astype(bf16)
    messages_ref[...] = (total[:, :atoms] + total[:, atoms:]).T
    filter_ref[...] = dot(basis_s[...], grad_s[...], NT)
    act_grad = dot(push_s[...], pick_s[...], NT)

    ghost_at = column_iota((ghosts, 2 * atoms), 0).astype(f32)
    lists = list_ref[...]
    for side in range(2):
        edges = near_s[side, 2 * atoms + 16 :, :].astype(f32)
        near_index = edges[:slots, :atoms]
        near_length = edges[:slots, atoms:] + (edges[slots:, :atoms] + edges[slots:, atoms:])
        first = atoms + ghosts * (1 - side)
        near_index = near_index - first
        inside = jnp.logical_and(near_index >= 0.0, near_index < ghosts)
        near_envelope = envelope_of(near_length, inside)
        near_cot = doubled(near_s[side, atoms : 2 * atoms, :].astype(f32).T)
        for step in range(slots // 2):
            j = 2 * step
            here = pl.ds(step * 2 * atoms, 2 * atoms)
            weights = dot(wf, basis_of(near_length, near_envelope, j)[:bins], TN)
            pick = jnp.where(ghost_at == paired(near_index, j), 1.0, 0.0).astype(bf16)
            near_pick_s[side, :, here] = pick
            near_push_s[side, :, here] = (near_cot * weights).astype(bf16)
        near_grad = dot(near_push_s[side], near_pick_s[side], NT)
        at = column_iota((atoms, ghosts), 0) == lists[side : side + 1, :]
        at = at.astype(f32).astype(bf16)
        high, low = split_two(near_grad)
        act_grad = act_grad + (dot(high, at, NT) + dot(low, at, NT))
    sigma = jax.nn.sigmoid(hidden)
    pre = (act_grad.T * (sigma * (1.0 + hidden * (1.0 - sigma)))).astype(bf16)
    pre_ref[...] = pre
    message_ref[...] = dot(feat_ref[...], pre, TN)


def total_of(parts_ref, rows=slice(None)):
    total = parts_ref[0, rows].astype(f32)
    for part in range(1, parts_ref.shape[0]):
        total = total + parts_ref[part, rows].astype(f32)
    return total


def join_kernel(parts_ref, weights_ref, out_ref):
    total = jnp.sum(parts_ref[...].astype(f32), axis=0)
    both = jnp.concatenate([weights_ref[...].astype(f32), total], axis=0).astype(bf16)
    out_ref[...] = jnp.broadcast_to(both[None], out_ref.shape)


def apply_kernel(parts_ref, table_ref, out_ref):
    peers, rows, lanes = out_ref.shape
    total = table_ref.shape[0]
    parts = parts_ref[...].astype(f32)
    weights = unpacked(parts[:, :PACK_ROWS]).reshape(total, 2 * lanes).astype(bf16)
    grads = jnp.sum(parts[:, PACK_ROWS:], axis=0).astype(bf16)
    half = (rows - CHUNK_ROWS) // 2
    for peer in range(peers):
        piece = table_ref[:, half * peer : half * (peer + 1)]
        out_ref[peer, : 2 * half, :] = packed(dot(piece, weights, TN)).astype(bf16)
        out_ref[peer, 2 * half :, :] = grads


def hand_on_kernel(parts_ref, out_ref):
    rows = out_ref.shape[2]
    first = parts_ref.shape[1] - rows
    out_ref[...] = jnp.broadcast_to(parts_ref[:, first:, :][None], out_ref.shape)


def wave_vector_length(slot):
    v = slot + 1.0
    m = jnp.floor((v + 4.5) / 9.0)
    nz = v - 9.0 * m
    nx = jnp.floor((m + 4.5) / 9.0)
    ny = m - 9.0 * nx
    return two_pi * jnp.sqrt(nx * nx + ny * ny + nz * nz)


def wave_basis(slot, bin_at, bins):
    spacing = kspace_limit / (bins - 1)
    scaled = (wave_vector_length(slot) - kspace_limit * bin_at / (bins - 1)) / spacing
    return jnp.where(bin_at < bins, jnp.exp(-0.5 * scaled * scaled), 0.0)


def swapped_halves(rows):
    half = rows.shape[0] // 2
    return jnp.concatenate([rows[half:], rows[:half]], axis=0)


def split_two(value):
    high = value.astype(bf16)
    return high, (value - high.astype(f32)).astype(bf16)


def middle_kernel(
    scale,
    owner_ref,
    sums_ref,
    index_ref,
    wc_ref,
    wk_ref,
    message_ref,
    filter_ref,
    grads_ref,
    weights_ref,
):
    bins, channels = wk_ref.shape
    sums = unpacked(total_of(sums_ref))
    first_slot = (owner_ref[0] * SLOTS_OWN).astype(f32)

    def slot_of(shape, axis):
        place = column_iota(shape, axis).astype(f32)
        return first_slot + place - SLOTS_OWN * jnp.floor((place + 0.5) / SLOTS_OWN)

    waves = index_ref.shape[1]
    index = index_ref[...].astype(f32)
    codes = jnp.abs(81.0 * index[0:1] + 9.0 * index[1:2] + index[2:3])
    same = jnp.where(slot_of((ROWS_OWN, waves), 0) + 1.0 == codes, 1.0, 0.0)
    times = jnp.sum(same, axis=1, keepdims=True)
    across = (ROWS_OWN, bins)
    basis = wave_basis(slot_of(across, 0), column_iota(across, 1).astype(f32), bins).astype(bf16)
    wave_filter = dot(basis, wk_ref[...])
    high, low = split_two(sums)
    factor = dot(high, wc_ref[...]) + dot(low, wc_ref[...])
    first = column_iota((ROWS_OWN, channels), 0) < ROWS_OWN // 2
    weights = (times * scale) * wave_filter * jnp.where(first, factor, sums)
    weights = weights.astype(bf16)
    weights_ref[...] = packed(weights.astype(f32)).astype(bf16)
    filter_grad = jnp.where(first, (times * scale) * factor * swapped_halves(sums), 0.0)
    down = (ROWS_OWN, ROWS_OWN)
    basis_down = wave_basis(slot_of(down, 1), column_iota(down, 0).astype(f32), bins)
    basis_down = basis_down.astype(bf16).astype(f32)
    kspace = dot(basis_down, filter_grad, precision=lax.Precision.HIGHEST)
    pushed = swapped_halves(weights.astype(f32)).astype(bf16)
    none = jnp.zeros_like(sums)
    high, low = split_two(jnp.where(first, sums, none))
    charge = dot(high, pushed, TN) + dot(low, pushed, TN)

    share = channels // GRAD_CHUNKS
    small = packed(jnp.concatenate([filter_ref[...], kspace], axis=0))
    spare = GRAD_CHUNKS * share - small.shape[0]
    small = jnp.concatenate([small, jnp.zeros((spare, LANES), f32)], axis=0)
    grads = [
        packed(message_ref[...].reshape(GRAD_CHUNKS, share, channels)),
        packed(charge.reshape(GRAD_CHUNKS, share, channels)),
        small.reshape(GRAD_CHUNKS, share, LANES),
    ]
    grads_ref[...] = jnp.concatenate(grads, axis=1).astype(bf16)


def final_kernel(
    count_ref, parts_ref, feat_ref, messages_ref, cot_ref, pre_ref, wm_ref, wc_ref, updated_ref, grad_ref
):
    atoms, channels = feat_ref.shape
    both = unpacked(total_of(parts_ref, slice(0, 4 * atoms)))
    live = column_iota((atoms, channels), 0) < count_ref[0, 0]
    added = jnp.where(live, messages_ref[...] + both[:atoms], 0.0)
    updated_ref[...] = (feat_ref[...].astype(f32) + added).astype(bf16)
    charge_grad = jnp.where(live, both[atoms:], 0.0).astype(bf16)
    grad_ref[...] = (
        cot_ref[...].astype(f32)
        + dot(pre_ref[...], wm_ref[...], NT)
        + dot(charge_grad, wc_ref[...], NT)
    )


def unpack_kernel(grads_ref, message_ref, charge_ref, filter_ref, kspace_ref):
    channels = message_ref.shape[1]
    grads = grads_ref[...].astype(f32)
    message_ref[...] = unpacked(grads[:, 0:16]).reshape(channels, channels)
    charge_ref[...] = unpacked(grads[:, 16:32]).reshape(channels, channels)
    small = unpacked(grads[: 4 * ROWS_OWN // 8, 32:40].reshape(4 * ROWS_OWN, LANES))
    bins = filter_ref.shape[0]
    filter_ref[...] = small[:bins]
    kspace_ref[...] = small[ROWS_OWN : ROWS_OWN + bins]


def on_core(kernel, out_shape, in_smem, n_in, scratch=()):
    smem = pl.BlockSpec(memory_space=pltpu.SMEM)
    vmem = pl.BlockSpec(memory_space=pltpu.VMEM)
    return pl.pallas_call(
        kernel,
        out_shape=out_shape,
        in_specs=[smem] * in_smem + [vmem] * (n_in - in_smem),
        out_specs=[vmem] * len(out_shape),
        scratch_shapes=list(scratch),
        compiler_params=pltpu.CompilerParams(vmem_limit_bytes=48 * 1024 * 1024),
    )


def shape(dims, kind):
    return jax.ShapeDtypeStruct(dims, kind)


def exchanged(value, axis):
    return lax.all_to_all(value, axis, 0, 0, tiled=True)


def body(
    features,
    fractional,
    counts,
    neighbor_index,
    neighbor_count,
    send_list,
    distances,
    wave_index,
    w_message,
    w_filter,
    w_charge,
    w_kspace,
    cotangent,
):
    feat, cot, lists = features[0], cotangent[0], send_list[0, 0]
    atoms, channels = feat.shape
    slots = neighbor_index.shape[2]
    ghosts = lists.shape[1]
    bins = w_filter.shape[0]
    waves = wave_index.shape[1]
    size_z, size_y = lax.axis_size("z"), lax.axis_size("y")
    domains = size_z * size_y
    space = ("z", "y")
    scale = ewald_scale_factor / math.sqrt(atoms * domains * waves)

    place_y, place_z = lax.axis_index("y"), lax.axis_index("z")
    here = place_y.reshape(1).astype(jnp.int32)
    index, length = neighbor_index[0].T, distances[0].T
    rows = 2 * atoms + 16 + 2 * slots
    shared, block = on_core(
        first_kernel,
        [shape((size_y, rows, channels), bf16), shape((rows, channels), bf16)],
        1,
        8,
        [pltpu.VMEM((8, LANES), f32)],
    )(counts, feat, cot, fractional[0], lists, index, neighbor_count, length)
    ends = [(z * size_y + size_y - 1, (z + 1) % size_z * size_y) for z in range(size_z)]
    wrap = lax.ppermute(block, space, ends + [(t, s) for s, t in ends])
    shared = exchanged(shared, "y")
    shared, wrap = lax.optimization_barrier((shared, wrap))

    total = size_z * ROWS_OWN
    table, sums = on_core(
        wave_kernel,
        [shape((total, size_y * 2 * atoms), bf16), shape((size_z, PACK_ROWS, LANES), bf16)],
        1,
        3,
    )(here, shared, jnp.asarray(wave_rows(domains), bf16))
    sums = exchanged(sums, "z")

    edges = slots * atoms
    messages, pre, message_term, filter_term = on_core(
        edge_kernel,
        [
            shape((atoms, channels), f32),
            shape((atoms, channels), bf16),
            shape((channels, channels), f32),
            shape((ROWS_OWN, channels), f32),
        ],
        2,
        12,
        [
            pltpu.VMEM((atoms, edges), bf16),
            pltpu.VMEM((ROWS_OWN, edges), bf16),
            pltpu.VMEM((channels, edges), bf16),
            pltpu.VMEM((channels, edges), bf16),
            pltpu.VMEM((2, ghosts, edges), bf16),
            pltpu.VMEM((2, channels, edges), bf16),
            pltpu.VMEM((2, rows, channels), bf16),
        ],
    )(
        counts,
        here,
        feat,
        wrap,
        shared,
        w_message,
        index,
        neighbor_count,
        length,
        w_filter,
        cot,
        lists,
    )
    owner = place_y * size_z + place_z
    grads, weights = on_core(
        lambda *refs: middle_kernel(scale, *refs),
        [
            shape((GRAD_CHUNKS, CHUNK_ROWS, LANES), bf16),
            shape((PACK_ROWS, LANES), bf16),
        ],
        1,
        7,
    )(
        owner.reshape(1).astype(jnp.int32),
        sums,
        wave_index,
        w_charge,
        w_kspace,
        message_term,
        filter_term,
    )
    parts = exchanged(grads, ("x", "core", "y"))
    rows = PACK_ROWS + CHUNK_ROWS
    parts = on_core(join_kernel, [shape((size_z, rows, LANES), bf16)], 0, 2)(parts, weights)[0]
    parts = exchanged(parts, "z")
    rows = 4 * atoms + CHUNK_ROWS
    parts = on_core(apply_kernel, [shape((size_y, rows, LANES), bf16)], 0, 2)(parts, table)[0]
    parts = exchanged(parts, "y")
    slabs = lax.axis_size("x") * lax.axis_size("core")
    grads = on_core(hand_on_kernel, [shape((slabs, size_y, CHUNK_ROWS, LANES), bf16)], 0, 1)(
        parts
    )[0]
    grads = exchanged(grads, ("x", "core")).reshape(GRAD_CHUNKS, CHUNK_ROWS, LANES)

    updated, grad_features = on_core(
        final_kernel,
        [shape((atoms, channels), bf16), shape((atoms, channels), f32)],
        1,
        8,
    )(counts, parts, feat, messages, cot, pre, w_message, w_charge)
    grad_message, grad_charge, grad_filter, grad_kspace = on_core(
        unpack_kernel,
        [
            shape((channels, channels), f32),
            shape((channels, channels), f32),
            shape((bins, channels), f32),
            shape((bins, channels), f32),
        ],
        0,
        1,
    )(grads)
    return (updated[None], grad_features[None], grad_message, grad_charge, grad_filter, grad_kspace)


def solution(mesh):
    fine = Mesh(mesh.devices.reshape(4, 2, 16, 4), ("x", "core", "z", "y"))
    dp, space = ("x", "core"), ("z", "y")
    placed = (
        P(dp, space, None),
        P(dp, None, space),
        P(dp, space),
        P(dp, space, None),
        P(dp, space),
        P(dp, space, None, None),
        P(dp, space, None),
        P(),
        P(),
        P(),
        P(),
        P(),
        P(dp, space, None),
    )
    return jax.shard_map(
        body,
        mesh=fine,
        in_specs=placed,
        out_specs=(P(dp, space, None), P(dp, space, None), P(), P(), P(), P()),
        check_vma=False,
    )
```

time: 135 us -> 126 us (0.933)
  starting transfers between devices: 47.9 us -> 37.8 us
  Pallas kernels: 9.31 us -> 13.5 us
  blocking collectives: 56.3 us -> 53.6 us
  waiting for transfers between devices: 15.8 us -> 13.8 us
  local copies, waits for them, and re-layouts: 3.63 us -> 5.07 us
    ppermute x4 -> x1, starting transfers between devices: 24.5 us -> 13.5 us  [body(): wrap = lax.ppermute(block, space, ends + [(t, s) for s, t in ends])]
    pallas_call x1, Pallas kernels: 2.74 us -> 7.51 us  [body(): on_core(edge_kernel, [shape((atoms, channels), f32), shape((atoms, channe...]
    ppermute x4 -> x1, waiting for transfers between devices: 7.16 us -> 3.44 us  [body(): wrap = lax.ppermute(block, space, ends + [(t, s) for s, t in ends])]
    all_to_all x3, blocking collectives: 56.3 us -> 53.6 us  [exchanged(): return lax.all_to_all(value, axis, 0, 0, tiled=True)]
    all_to_all x3, waiting for transfers between devices: 8.6 us -> 10.4 us  [exchanged(): return lax.all_to_all(value, axis, 0, 0, tiled=True)]
    unnamed x31 -> x33, local copies, waits for them, and re-layouts: 3.63 us -> 5.07 us
    pallas_call x6 -> x5, Pallas kernels: 3.31 us -> 2.71 us  [the longest x1 0.95 us: body(): on_core(first_kernel, [shape((size_y, rows, channels), bf16), shape((rows...]
  transfers between devices with their start and end apart: 7 -> 4, of which waited for: 3 -> 3; matrix products, arithmetic and copies ran while one was open for 0% -> 0% of each run, Pallas kernels for 3% -> 7%
where the time goes in v3:
time: 126 us; the launch traced here: 125 us
  blocking collectives  53.6 us (43%)
  starting transfers between devices  37.8 us (30%)
  waiting for transfers between devices  13.8 us (11%)
  Pallas kernels  13.5 us (11%)
  local copies, waits for them, and re-layouts  5.07 us (4%)
  between operations  1.43 us (1%)
    all_to_all x3, blocking collectives, exchanged(): return lax.all_to_all(value, axis, 0, 0, tiled=True)  53.6 us
    all_to_all x3, starting transfers between devices, exchanged(): return lax.all_to_all(value, axis, 0, 0, tiled=True)  24.3 us
    ppermute x1, starting transfers between devices, body(): wrap = lax.ppermute(block, space, ends + [(t, s) for s, t in ends])  13.5 us
    all_to_all x3, waiting for transfers between devices, exchanged(): return lax.all_to_all(value, axis, 0, 0, tiled=True)  10.4 us
    pallas_call x1, Pallas kernels, body(): on_core(edge_kernel, [shape((atoms, channels), f32), shape((atoms, channe...  7.51 us
    unnamed x33, local copies, waits for them, and re-layouts  5.07 us
    ppermute x1, waiting for transfers between devices, body(): wrap = lax.ppermute(block, space, ends + [(t, s) for s, t in ends])  3.44 us
  transfers between devices with their start and end apart: 4, of which 3 were waited for; matrix products, arithmetic and copies ran while one was open for 0% of the time, Pallas kernels for 7%

profile of v3, /device:TPU:1, one launch (start us, length us, event | category | flops | bytes accessed | tf_op | source)
XLA Modules:
  0.0 125.1 jit_solution(5988208145840023162)
XLA Ops:
  0.6 0.0 copy-start.7
  1.3 0.7 copy.22
  2.0 0.0 copy-start.15
  2.0 0.0 copy-done.7
  2.0 0.7 copy-done.15
  2.6 0.0 copy-start
  2.6 0.8 copy-done
  3.5 0.0 copy-start.2
  3.5 0.8 copy-done.2
  4.3 0.0 copy-start.8
  4.3 0.7 copy-done.8
  5.0 0.0 copy-start.13
  5.0 0.7 copy-done.13
  5.7 0.9 shard_map.181
  6.7 5.1 %all-to-all-start = ((bf16[4,336,256]{2,1,0:T(8,128)(2,1)}), bf16[4,336,256]{2,1,0:T(8,128)(2,1)S(1)}, u32[]{:S(2)}, u32[]{:S(2)}) async-start(bf16[4,336,256]{2,1,0:T(8,128)(2,1)} %get-tuple-element.24), calls=%async_computation | async-start | bytes 1376256 | tf_op jit(solution)/shard_map/all_to_all | solution.py:459
  11.8 13.5 %collective-permute-start = (bf16[336,256]{1,0:T(8,128)(2,1)S(1)}, bf16[336,256]{1,0:T(8,128)(2,1)S(1)}, u32[]{:S(2)}, u32[]{:S(2)}) collective-permute-start(bf16[336,256]{1,0:T(8,128)(2,1)S(1)} %get-tuple-element.25), channel_id=1, source_target_pairs={{3,4},{7,8},{11,12},{15,16},{19,20},{23,24},{27,28},{31,32},{35,36... | collective-permute-start | bytes 516104 | tf_op jit(solution)/shard_map/ppermute | solution.py:500
  25.3 3.4 %collective-permute-done.wrap_ref = bf16[336,256]{1,0:T(8,128)(2,1)S(1)} collective-permute-done((bf16[336,256]{1,0:T(8,128)(2,1)S(1)}, bf16[336,256]{1,0:T(8,128)(2,1)S(1)}, u32[]{:S(2)}, u32[]{:S(2)}) %collective-permute-start) | collective-permute-done | bytes 172064 | tf_op jit(solution)/shard_map/ppermute | solution.py:500
  28.8 0.0 all-to-all-done.atoms_ref.shared_ref
  28.8 0.0 copy-done.6
  28.8 1.5 %shard_map.182 = (bf16[384,1024]{1,0:T(8,128)(2,1)S(1)}, bf16[16,48,128]{2,1,0:T(8,128)(2,1)}) custom-call(s32[1]{0:T(128)} %bitcast.1.place_ref, bf16[4,336,256]{2,1,0:T(8,128)(2,1)S(1)} %all-to-all-done.atoms_ref.shared_ref, bf16[1536,8]{1,0:T(8,128)(2,1)S(1)} %copy-done.6), custom_call_target="tpu_custom_call" | custom-call | tf_op jit(solution)/shard_map/pallas_call | solution.py:505
  30.3 0.0 copy-start.1
  30.3 0.0 copy-start.3
  30.3 0.0 copy-start.5
  30.3 0.0 copy-start.10
  30.3 10.0 %all-to-all-start.1 = ((bf16[16,48,128]{2,1,0:T(8,128)(2,1)}), bf16[16,48,128]{2,1,0:T(8,128)(2,1)S(1)}, u32[]{:S(2)}, u32[]{:S(2)}) async-start(bf16[16,48,128]{2,1,0:T(8,128)(2,1)} %get-tuple-element.27), calls=%async_computation.1 | async-start | bytes 393216 | tf_op jit(solution)/shard_map/all_to_all | solution.py:459
  40.4 0.0 copy-start.14
  40.4 0.0 copy-done.1
  40.4 0.0 copy-done.3
  40.4 0.0 copy-done.5
  40.4 0.0 copy-done.9
  40.4 0.0 copy-done.10
  40.4 0.6 copy-done.14
  41.0 7.5 %shard_map.183 = (f32[128,256]{1,0:T(8,128)S(1)}, bf16[128,256]{1,0:T(8,128)(2,1)S(1)}, f32[256,256]{1,0:T(8,128)S(1)}, f32[24,256]{1,0:T(8,128)S(1)}) custom-call(s32[1,1]{1,0:T(1,128)S(6)} %copy.23.count_ref, s32[1]{0:T(128)} %bitcast.1.place_ref, bf16[128,256]{1,0:T(8,128)(2,1)S(1)} %bitcast.19, bf16[336,256]{1,0:T(8,128)(2,1)S(1)} %collective-permute-done.wrap_ref, ...), custom_call_target="tpu_custom_call" | custom-call | tf_op jit(solution)/shard_map/pallas_call | solution.py:514
  48.6 4.1 %all-to-all-done.1.refs_1_ = bf16[16,48,128]{2,1,0:T(8,128)(2,1)S(1)} async-done(((bf16[16,48,128]{2,1,0:T(8,128)(2,1)}), bf16[16,48,128]{2,1,0:T(8,128)(2,1)S(1)}, u32[]{:S(2)}, u32[]{:S(2)}) %all-to-all-start.1) | async-done | bytes 196640 | tf_op jit(solution)/shard_map/all_to_all | solution.py:459
  52.7 0.0 copy-done.4
  52.7 0.0 copy-done.11
  52.7 0.0 copy-done.12
  52.7 0.4 shard_map.184
  53.2 21.0 %all_to_all.30.parts_ref = bf16[32,40,128]{2,1,0:T(8,128)(2,1)S(1)} all-to-all(bf16[32,40,128]{2,1,0:T(8,128)(2,1)S(1)} %get-tuple-element.31), channel_id=1, replica_groups=mesh['x'=4,'core'=2,'z'=16,'y'=4] {'x','core','y'}, dimensions={0} | all-to-all | bytes 655360 | tf_op jit(solution)/shard_map/all_to_all | solution.py:459
  74.1 0.1 shard_map.185
  74.2 20.4 %all_to_all.31.parts_ref = bf16[16,88,128]{2,1,0:T(8,128)(2,1)S(1)} all-to-all(bf16[16,88,128]{2,1,0:T(8,128)(2,1)S(1)} %shard_map.185), channel_id=1, replica_groups=mesh['x'=4,'core'=2,'z'=16,'y'=4] {'z'}, dimensions={0} | all-to-all | bytes 720896 | tf_op jit(solution)/shard_map/all_to_all | solution.py:459
  94.6 0.5 shard_map.186
  95.0 12.2 %all_to_all.32.parts_ref = bf16[4,552,128]{2,1,0:T(8,128)(2,1)S(1)} all-to-all(bf16[4,552,128]{2,1,0:T(8,128)(2,1)S(1)} %shard_map.186), channel_id=1, replica_groups=mesh['x'=4,'core'=2,'z'=16,'y'=4] {'y'}, dimensions={0} | all-to-all | bytes 1130496 | tf_op jit(solution)/shard_map/all_to_all | solution.py:459
  107.3 0.8 shard_map.188
  108.0 9.1 %all-to-all-start.5 = ((bf16[8,4,40,128]{3,2,1,0:T(8,128)(2,1)}), bf16[8,4,40,128]{3,2,1,0:T(8,128)(2,1)S(1)}, u32[]{:S(2)}, u32[]{:S(2)}) async-start(bf16[8,4,40,128]{3,2,1,0:T(8,128)(2,1)} %shard_map.188), calls=%async_computation.5 | async-start | bytes 655360 | tf_op jit(solution)/shard_map/all_to_all | solution.py:459
  117.2 0.9 shard_map.187
  118.1 6.2 %all-to-all-done.5 = bf16[8,4,40,128]{3,2,1,0:T(8,128)(2,1)S(1)} async-done(((bf16[8,4,40,128]{3,2,1,0:T(8,128)(2,1)}), bf16[8,4,40,128]{3,2,1,0:T(8,128)(2,1)S(1)}, u32[]{:S(2)}, u32[]{:S(2)}) %all-to-all-start.5) | async-done | bytes 327712 | tf_op jit(solution)/shard_map/all_to_all | solution.py:459
  124.3 0.8 shard_map.189
  (5 shorter events, 0.0 us)
Async XLA Ops:
  0.6 1.4 %copy-start.7 = (s32[1,128,32]{1,2,0:T(8,128)S(1)}, s32[1,128,32]{1,2,0:T(8,128)}, u32[]{:S(2)}) copy-start(s32[1,128,32]{1,2,0:T(8,128)} %param.17) | copy-start | bytes 49156
  2.0 0.7 copy-start.15
  2.6 0.8 copy-start
  3.5 0.8 copy-start.2
  4.3 0.7 copy-start.8
  5.0 0.7 copy-start.13
  6.7 22.1 %copy-start.6 = (bf16[1536,8]{1,0:T(8,128)(2,1)S(1)}, bf16[1536,8]{1,0:T(8,128)(2,1)}, u32[]{:S(2)}) copy-start(bf16[1536,8]{1,0:T(8,128)(2,1)} %constant.13.clone.rows_ref) | copy-start | bytes 73732
  6.7 22.1 %all-to-all-start = ((bf16[4,336,256]{2,1,0:T(8,128)(2,1)}), bf16[4,336,256]{2,1,0:T(8,128)(2,1)S(1)}, u32[]{:S(2)}, u32[]{:S(2)}) async-start(bf16[4,336,256]{2,1,0:T(8,128)(2,1)} %get-tuple-element.24), calls=%async_computation | async-start | bytes 1376256 | tf_op jit(solution)/shard_map/all_to_all | solution.py:459
  11.8 17.0 %collective-permute-start = (bf16[336,256]{1,0:T(8,128)(2,1)S(1)}, bf16[336,256]{1,0:T(8,128)(2,1)S(1)}, u32[]{:S(2)}, u32[]{:S(2)}) collective-permute-start(bf16[336,256]{1,0:T(8,128)(2,1)S(1)} %get-tuple-element.25), channel_id=1, source_target_pairs={{3,4},{7,8},{11,12},{15,16},{19,20},{23,24},{27,28},{31,32},{35,36... | collective-permute-start | bytes 516104 | tf_op jit(solution)/shard_map/ppermute | solution.py:500
  30.3 10.1 %copy-start.1 = (bf16[1,128,256]{2,1,0:T(8,128)(2,1)S(1)}, bf16[1,128,256]{2,1,0:T(8,128)(2,1)}, u32[]{:S(2)}) copy-start(bf16[1,128,256]{2,1,0:T(8,128)(2,1)} %param.14) | copy-start | bytes 196612
  30.3 10.1 %copy-start.3 = (bf16[1,128,256]{2,1,0:T(8,128)(2,1)S(1)}, bf16[1,128,256]{2,1,0:T(8,128)(2,1)}, u32[]{:S(2)}) copy-start(bf16[1,128,256]{2,1,0:T(8,128)(2,1)} %param.26) | copy-start | bytes 196612
  30.3 10.1 %copy-start.5 = (bf16[256,256]{1,0:T(8,128)(2,1)S(1)}, bf16[256,256]{1,0:T(8,128)(2,1)}, u32[]{:S(2)}) copy-start(bf16[256,256]{1,0:T(8,128)(2,1)} %wm_ref.3) | copy-start | bytes 393220
  30.3 10.1 %copy-start.9 = (f32[1,128,32]{1,2,0:T(8,128)S(1)}, f32[1,128,32]{1,2,0:T(8,128)}, u32[]{:S(2)}) copy-start(f32[1,128,32]{1,2,0:T(8,128)} %param.20) | copy-start | bytes 49156
  30.3 10.1 %copy-start.10 = (bf16[20,256]{1,0:T(8,128)(2,1)S(1)}, bf16[20,256]{1,0:T(8,128)(2,1)}, u32[]{:S(2)}) copy-start(bf16[20,256]{1,0:T(8,128)(2,1)} %wf_ref.1) | copy-start | bytes 30724
  30.3 22.3 %all-to-all-start.1 = ((bf16[16,48,128]{2,1,0:T(8,128)(2,1)}), bf16[16,48,128]{2,1,0:T(8,128)(2,1)S(1)}, u32[]{:S(2)}, u32[]{:S(2)}) async-start(bf16[16,48,128]{2,1,0:T(8,128)(2,1)} %get-tuple-element.27), calls=%async_computation.1 | async-start | bytes 393216 | tf_op jit(solution)/shard_map/all_to_all | solution.py:459
  40.4 0.7 copy-start.14
  41.0 11.7 %copy-start.4 = (bf16[256,256]{1,0:T(8,128)(2,1)S(1)}, bf16[256,256]{1,0:T(8,128)(2,1)}, u32[]{:S(2)}) copy-start(bf16[256,256]{1,0:T(8,128)(2,1)} %wc_ref.1) | copy-start | bytes 393220
  41.0 11.7 %copy-start.11 = (bf16[20,256]{1,0:T(8,128)(2,1)S(1)}, bf16[20,256]{1,0:T(8,128)(2,1)}, u32[]{:S(2)}) copy-start(bf16[20,256]{1,0:T(8,128)(2,1)} %refs_4_.1) | copy-start | bytes 30724
  41.0 11.7 %copy-start.12 = (s32[3,512]{1,0:T(4,128)S(1)}, s32[3,512]{1,0:T(4,128)}, u32[]{:S(2)}) copy-start(s32[3,512]{1,0:T(4,128)} %refs_2_.1) | copy-start | bytes 18436
  108.0 16.3 %all-to-all-start.5 = ((bf16[8,4,40,128]{3,2,1,0:T(8,128)(2,1)}), bf16[8,4,40,128]{3,2,1,0:T(8,128)(2,1)S(1)}, u32[]{:S(2)}, u32[]{:S(2)}) async-start(bf16[8,4,40,128]{3,2,1,0:T(8,128)(2,1)} %shard_map.188), calls=%async_computation.5 | async-start | bytes 655360 | tf_op jit(solution)/shard_map/all_to_all | solution.py:459

commit v4 on v3

--- a/solution.py
+++ b/solution.py
@@ -87,6 +87,7 @@
 
 def first_kernel(
     count_ref,
+    place_ref,
     feat_ref,
     cot_ref,
     frac_ref,
@@ -95,10 +96,9 @@
     used_ref,
     length_ref,
     shared_ref,
-    block_ref,
+    wrap_ref,
     list_s,
 ):
-    copies = shared_ref.shape[0]
     atoms, channels = feat_ref.shape
     ghosts = list_ref.shape[1]
     slots = index_ref.shape[0]
@@ -106,11 +106,10 @@
     zero = jnp.zeros((atoms, channels), f32)
     feat = jnp.where(live, feat_ref[...].astype(f32), zero).astype(bf16)
     cot = jnp.where(live, cot_ref[...].astype(f32), zero).astype(bf16)
-    frac = frac_ref[...]
     which = column_iota((8, atoms), 0)
-    coords = jnp.where(which == 0, frac[0:1, :], 0.0)
-    coords = jnp.where(which == 1, frac[1:2, :], coords)
-    coords = jnp.where(which == 2, frac[2:3, :], coords)
+    coords = jnp.where(which == 0, frac_ref[0], 0.0)
+    coords = jnp.where(which == 1, frac_ref[1], coords)
+    coords = jnp.where(which == 2, frac_ref[2], coords)
     coords = jnp.where(which == 3, 1.0, coords)
     high, middle, low = split_three(coords)
     list_s[...] = jnp.zeros_like(list_s)
@@ -125,15 +124,16 @@
         [jnp.concatenate([index, high], axis=1), jnp.concatenate([middle, low], axis=1)], axis=0
     ).astype(bf16)
 
-    def fill(ref):
-        ref[0:atoms, :] = feat
-        ref[atoms : 2 * atoms, :] = cot
-        ref[2 * atoms : 2 * atoms + 16, :] = coords
-        ref[2 * atoms + 16 :, :] = edges
-
-    for copy in range(copies):
-        fill(shared_ref.at[copy])
-    fill(block_ref)
+    for copy in range(shared_ref.shape[0]):
+        shared_ref[copy, 0:atoms, :] = feat
+        shared_ref[copy, atoms : 2 * atoms, :] = cot
+        shared_ref[copy, 2 * atoms : 2 * atoms + 16, :] = coords
+        shared_ref[copy, 2 * atoms + 16 :, :] = edges
+    chosen = jnp.where(place_ref[0] == 0, list_ref[0:1, :], list_ref[1:2, :])
+    pick = (column_iota((atoms, ghosts), 0) == chosen).astype(f32).astype(bf16)
+    wrap_ref[0:ghosts, :] = dot(pick, feat, TN).astype(bf16)
+    wrap_ref[ghosts : ghosts + atoms, :] = cot
+    wrap_ref[ghosts + atoms :, :] = edges
 
 
 def split_three(value):
@@ -192,6 +192,7 @@
     near_pick_s,
     near_push_s,
     near_s,
+    near_rows_s,
 ):
     atoms, channels = feat_ref.shape
     slots = index_ref.shape[0]
@@ -207,21 +208,24 @@
     def take_block(side):
         @pl.when(at_end[side])
         def _():
-            near_s[side] = wrap_ref[...]
+            near_rows_s[side] = wrap_ref[:ghosts]
+            near_s[side, atoms : 2 * atoms] = wrap_ref[ghosts : ghosts + atoms]
+            near_s[side, 2 * atoms + 16 :] = wrap_ref[ghosts + atoms :]
 
         @pl.when(jnp.logical_not(at_end[side]))
         def _():
             near_s[side] = shared_ref[beside[side]]
+            lists = near_s[side, 2 * atoms : 2 * atoms + 16, :].astype(f32)[8:16, atoms:]
+            picked = lists[1 - side : 2 - side, :ghosts]
+            rows = column_iota((atoms, ghosts), 0).astype(f32) == picked
+            rows = dot(rows.astype(f32).astype(bf16), near_s[side, :atoms, :], TN)
+            near_rows_s[side] = rows.astype(bf16)
 
     take_block(0)
     take_block(1)
 
     def ghost_rows(side):
-        lists = near_s[side, 2 * atoms : 2 * atoms + 16, :].astype(f32)[8:16, atoms:]
-        picked = lists[1 - side : 2 - side, :ghosts]
-        rows = column_iota((atoms, ghosts), 0).astype(f32) == picked
-        rows = dot(rows.astype(f32).astype(bf16), near_s[side, :atoms, :], TN).astype(bf16)
-        return silu(dot(rows, wm_ref[...])).astype(bf16).astype(f32)
+        return silu(dot(near_rows_s[side], wm_ref[...])).astype(bf16).astype(f32)
 
     hidden = dot(feat_ref[...], wm_ref[...])
     act = silu(hidden).astype(bf16).astype(f32)
@@ -438,9 +442,20 @@
     kspace_ref[...] = small[ROWS_OWN : ROWS_OWN + bins]
 
 
-def on_core(kernel, out_shape, in_smem, n_in, scratch=()):
+def on_core(kernel, out_shape, in_smem, n_in, scratch=(), streamed=False):
     smem = pl.BlockSpec(memory_space=pltpu.SMEM)
     vmem = pl.BlockSpec(memory_space=pltpu.VMEM)
+    if streamed:
+        return lambda *args: pl.pallas_call(
+            kernel,
+            out_shape=out_shape,
+            grid=(1,),
+            in_specs=[smem] * in_smem
+            + [pl.BlockSpec(v.shape, lambda i, n=v.ndim: (0,) * n) for v in args[in_smem:]],
+            out_specs=[vmem] * len(out_shape),
+            scratch_shapes=list(scratch),
+            compiler_params=pltpu.CompilerParams(vmem_limit_bytes=60 * 1024 * 1024),
+        )(*args)
     return pl.pallas_call(
         kernel,
         out_shape=out_shape,
@@ -489,17 +504,20 @@
     here = place_y.reshape(1).astype(jnp.int32)
     index, length = neighbor_index[0].T, distances[0].T
     rows = 2 * atoms + 16 + 2 * slots
-    shared, block = on_core(
+    shared, wrap = on_core(
         first_kernel,
-        [shape((size_y, rows, channels), bf16), shape((rows, channels), bf16)],
-        1,
-        8,
+        [
+            shape((size_y, rows, channels), bf16),
+            shape((ghosts + atoms + 2 * slots, channels), bf16),
+        ],
+        2,
+        9,
         [pltpu.VMEM((8, LANES), f32)],
-    )(counts, feat, cot, fractional[0], lists, index, neighbor_count, length)
+        streamed=True,
+    )(counts, here, feat, cot, jnp.swapaxes(fractional, 0, 1), lists, index, neighbor_count, length)
     ends = [(z * size_y + size_y - 1, (z + 1) % size_z * size_y) for z in range(size_z)]
-    wrap = lax.ppermute(block, space, ends + [(t, s) for s, t in ends])
+    wrap = lax.ppermute(wrap, space, ends + [(t, s) for s, t in ends])
     shared = exchanged(shared, "y")
-    shared, wrap = lax.optimization_barrier((shared, wrap))
 
     total = size_z * ROWS_OWN
     table, sums = on_core(
@@ -508,6 +526,7 @@
         1,
         3,
     )(here, shared, jnp.asarray(wave_rows(domains), bf16))
+    sums, wrap = lax.optimization_barrier((sums, wrap))
     sums = exchanged(sums, "z")
 
     edges = slots * atoms
@@ -529,6 +548,7 @@
             pltpu.VMEM((2, ghosts, edges), bf16),
             pltpu.VMEM((2, channels, edges), bf16),
             pltpu.VMEM((2, rows, channels), bf16),
+            pltpu.VMEM((2, ghosts, channels), bf16),
         ],
     )(
         counts,

time: 126 us -> 121 us (0.960)
  local copies, waits for them, and re-layouts: 5.07 us -> 0.65 us
  waiting for transfers between devices: 13.8 us -> 10.9 us
  starting transfers between devices: 37.8 us -> 40.5 us
    unnamed x33 -> x26, local copies, waits for them, and re-layouts: 5.07 us -> 0.65 us
    ppermute x1, waiting for transfers between devices: 3.44 us -> 0.59 us  [body(): wrap = lax.ppermute(wrap, space, ends + [(t, s) for s, t in ends])]
    all_to_all x3, starting transfers between devices: 24.3 us -> 27 us  [exchanged(): return lax.all_to_all(value, axis, 0, 0, tiled=True)]
  transfers between devices with their start and end apart: 4 -> 4, of which waited for: 3 -> 3; matrix products, arithmetic and copies ran while one was open for 0% -> 0% of each run, Pallas kernels for 7% -> 8%
where the time goes in v4:
time: 121 us; the launch traced here: 120 us
  blocking collectives  52.5 us (43%)
  starting transfers between devices  40.5 us (33%)
  Pallas kernels  14.5 us (12%)
  waiting for transfers between devices  10.9 us (9%)
  between operations  1.45 us (1%)
    all_to_all x3, blocking collectives, exchanged(): return lax.all_to_all(value, axis, 0, 0, tiled=True)  52.5 us
    all_to_all x3, starting transfers between devices, exchanged(): return lax.all_to_all(value, axis, 0, 0, tiled=True)  27 us
    ppermute x1, starting transfers between devices, body(): wrap = lax.ppermute(wrap, space, ends + [(t, s) for s, t in ends])  13.5 us
    all_to_all x3, waiting for transfers between devices, exchanged(): return lax.all_to_all(value, axis, 0, 0, tiled=True)  10.3 us
    pallas_call x1, Pallas kernels, body(): on_core(edge_kernel, [shape((atoms, channels), f32), shape((atoms, channe...  7.59 us
  transfers between devices with their start and end apart: 4, of which 3 were waited for; matrix products, arithmetic and copies ran while one was open for 0% of the time, Pallas kernels for 8%

profile of v4, /device:TPU:1, one launch (start us, length us, event | category | flops | bytes accessed | tf_op | source)
XLA Modules:
  0.0 120.5 jit_solution(561942502843743799)
XLA Ops:
  1.3 1.8 %shard_map.181 = (bf16[4,336,256]{2,1,0:T(8,128)(2,1)}, bf16[224,256]{1,0:T(8,128)(2,1)}) custom-call(s32[1,1]{1,0:T(1,128)S(6)} %copy.20.count_ref, s32[1]{0:T(128)} %bitcast.1.place_ref, bf16[128,256]{1,0:T(8,128)(2,1)} %bitcast.16, bf16[128,256]{1,0:T(8,128)(2,1)} %bitcast.19, f32[3,1,128]{2,1,0:T(1,128)} %bitcast.28, s32[2,32]{1,0:T(2,128)} %bitcast.26, ...), custom_call_target="tpu_custom_call" | custom-call | tf_op jit(solution)/shard_map/pallas_call | solution.py:449
  3.1 0.0 copy-start.12
  3.1 0.0 copy-start.4
  3.1 5.1 %all-to-all-start = ((bf16[4,336,256]{2,1,0:T(8,128)(2,1)}), bf16[4,336,256]{2,1,0:T(8,128)(2,1)S(1)}, u32[]{:S(2)}, u32[]{:S(2)}) async-start(bf16[4,336,256]{2,1,0:T(8,128)(2,1)} %get-tuple-element.24), calls=%async_computation | async-start | bytes 1376256 | tf_op jit(solution)/shard_map/all_to_all | solution.py:474
  8.3 0.0 copy-done.12
  8.3 13.5 %collective-permute-start = (bf16[224,256]{1,0:T(8,128)(2,1)S(1)}, bf16[224,256]{1,0:T(8,128)(2,1)S(1)}, u32[]{:S(2)}, u32[]{:S(2)}) collective-permute-start(bf16[224,256]{1,0:T(8,128)(2,1)S(1)} %copy-done.12), channel_id=1, source_target_pairs={{3,4},{7,8},{11,12},{15,16},{19,20},{23,24},{27,28},{31,32},{35,36... | collective-permute-start | bytes 344072 | tf_op jit(solution)/shard_map/ppermute | solution.py:519
  21.8 0.0 all-to-all-done.atoms_ref.shared_ref
  21.8 0.0 copy-done.4
  21.8 1.6 %shard_map.182 = (bf16[384,1024]{1,0:T(8,128)(2,1)S(1)}, bf16[16,48,128]{2,1,0:T(8,128)(2,1)}) custom-call(s32[1]{0:T(128)} %bitcast.1.place_ref, bf16[4,336,256]{2,1,0:T(8,128)(2,1)S(1)} %all-to-all-done.atoms_ref.shared_ref, bf16[1536,8]{1,0:T(8,128)(2,1)S(1)} %copy-done.4), custom_call_target="tpu_custom_call" | custom-call | tf_op jit(solution)/shard_map/pallas_call | solution.py:523
  23.4 0.6 collective-permute-done.wrap_ref
  24.0 0.0 copy-start
  24.0 0.0 copy-start.1
  24.0 0.0 copy-start.3
  24.0 0.0 copy-start.5
  24.0 0.0 copy-start.6
  24.0 0.0 copy-start.7
  24.0 12.7 %all-to-all-start.1 = ((bf16[16,48,128]{2,1,0:T(8,128)(2,1)}), bf16[16,48,128]{2,1,0:T(8,128)(2,1)S(1)}, u32[]{:S(2)}, u32[]{:S(2)}) async-start(bf16[16,48,128]{2,1,0:T(8,128)(2,1)} %get-tuple-element.27), calls=%async_computation.1 | async-start | bytes 393216 | tf_op jit(solution)/shard_map/all_to_all | solution.py:474
  36.7 0.0 copy-start.10
  36.7 0.0 copy-start.11
  36.7 0.0 copy-done
  36.8 0.0 copy-done.1
  36.8 0.0 copy-done.3
  36.8 0.0 copy-done.5
  36.8 0.0 copy-done.6
  36.8 0.0 copy-done.7
  36.8 0.6 copy-done.10
  37.4 0.0 copy-done.11
  37.4 0.0 copy-start.2
  37.4 0.0 copy-start.8
  37.4 0.0 copy-start.9
  37.4 7.6 %shard_map.183 = (f32[128,256]{1,0:T(8,128)S(1)}, bf16[128,256]{1,0:T(8,128)(2,1)S(1)}, f32[256,256]{1,0:T(8,128)S(1)}, f32[24,256]{1,0:T(8,128)S(1)}) custom-call(s32[1,1]{1,0:T(1,128)S(6)} %copy.20.count_ref, s32[1]{0:T(128)} %bitcast.1.place_ref, bf16[128,256]{1,0:T(8,128)(2,1)S(1)} %bitcast.17, bf16[224,256]{1,0:T(8,128)(2,1)S(1)} %collective-permute-done.wrap_ref, ...), custom_call_target="tpu_custom_call" | custom-call | tf_op jit(solution)/shard_map/pallas_call | solution.py:533
  45.0 4.0 %all-to-all-done.1.refs_1_ = bf16[16,48,128]{2,1,0:T(8,128)(2,1)S(1)} async-done(((bf16[16,48,128]{2,1,0:T(8,128)(2,1)}), bf16[16,48,128]{2,1,0:T(8,128)(2,1)S(1)}, u32[]{:S(2)}, u32[]{:S(2)}) %all-to-all-start.1) | async-done | bytes 196640 | tf_op jit(solution)/shard_map/all_to_all | solution.py:474
  49.0 0.0 copy-done.2
  49.1 0.0 copy-done.8
  49.1 0.0 copy-done.9
  49.1 0.4 shard_map.184
  49.5 19.9 %all_to_all.30.parts_ref = bf16[32,40,128]{2,1,0:T(8,128)(2,1)S(1)} all-to-all(bf16[32,40,128]{2,1,0:T(8,128)(2,1)S(1)} %get-tuple-element.31), channel_id=1, replica_groups=mesh['x'=4,'core'=2,'z'=16,'y'=4] {'x','core','y'}, dimensions={0} | all-to-all | bytes 655360 | tf_op jit(solution)/shard_map/all_to_all | solution.py:474
  69.4 0.1 shard_map.185
  69.5 20.4 %all_to_all.31.parts_ref = bf16[16,88,128]{2,1,0:T(8,128)(2,1)S(1)} all-to-all(bf16[16,88,128]{2,1,0:T(8,128)(2,1)S(1)} %shard_map.185), channel_id=1, replica_groups=mesh['x'=4,'core'=2,'z'=16,'y'=4] {'z'}, dimensions={0} | all-to-all | bytes 720896 | tf_op jit(solution)/shard_map/all_to_all | solution.py:474
  89.9 0.5 shard_map.186
  90.4 12.2 %all_to_all.32.parts_ref = bf16[4,552,128]{2,1,0:T(8,128)(2,1)S(1)} all-to-all(bf16[4,552,128]{2,1,0:T(8,128)(2,1)S(1)} %shard_map.186), channel_id=1, replica_groups=mesh['x'=4,'core'=2,'z'=16,'y'=4] {'y'}, dimensions={0} | all-to-all | bytes 1130496 | tf_op jit(solution)/shard_map/all_to_all | solution.py:474
  102.6 0.8 shard_map.188
  103.4 9.1 %all-to-all-start.5 = ((bf16[8,4,40,128]{3,2,1,0:T(8,128)(2,1)}), bf16[8,4,40,128]{3,2,1,0:T(8,128)(2,1)S(1)}, u32[]{:S(2)}, u32[]{:S(2)}) async-start(bf16[8,4,40,128]{3,2,1,0:T(8,128)(2,1)} %shard_map.188), calls=%async_computation.5 | async-start | bytes 655360 | tf_op jit(solution)/shard_map/all_to_all | solution.py:474
  112.5 0.9 shard_map.187
  113.4 6.2 %all-to-all-done.5 = bf16[8,4,40,128]{3,2,1,0:T(8,128)(2,1)S(1)} async-done(((bf16[8,4,40,128]{3,2,1,0:T(8,128)(2,1)}), bf16[8,4,40,128]{3,2,1,0:T(8,128)(2,1)S(1)}, u32[]{:S(2)}, u32[]{:S(2)}) %all-to-all-start.5) | async-done | bytes 327712 | tf_op jit(solution)/shard_map/all_to_all | solution.py:474
  119.6 0.8 shard_map.189
Async XLA Ops:
  3.1 5.2 %copy-start.12 = (bf16[224,256]{1,0:T(8,128)(2,1)S(1)}, bf16[224,256]{1,0:T(8,128)(2,1)}, u32[]{:S(2)}) copy-start(bf16[224,256]{1,0:T(8,128)(2,1)} %get-tuple-element.26) | copy-start | bytes 344068
  3.1 18.7 %copy-start.4 = (bf16[1536,8]{1,0:T(8,128)(2,1)S(1)}, bf16[1536,8]{1,0:T(8,128)(2,1)}, u32[]{:S(2)}) copy-start(bf16[1536,8]{1,0:T(8,128)(2,1)} %constant.13.clone.rows_ref) | copy-start | bytes 73732
  3.1 18.7 %all-to-all-start = ((bf16[4,336,256]{2,1,0:T(8,128)(2,1)}), bf16[4,336,256]{2,1,0:T(8,128)(2,1)S(1)}, u32[]{:S(2)}, u32[]{:S(2)}) async-start(bf16[4,336,256]{2,1,0:T(8,128)(2,1)} %get-tuple-element.24), calls=%async_computation | async-start | bytes 1376256 | tf_op jit(solution)/shard_map/all_to_all | solution.py:474
  8.3 15.7 %collective-permute-start = (bf16[224,256]{1,0:T(8,128)(2,1)S(1)}, bf16[224,256]{1,0:T(8,128)(2,1)S(1)}, u32[]{:S(2)}, u32[]{:S(2)}) collective-permute-start(bf16[224,256]{1,0:T(8,128)(2,1)S(1)} %copy-done.12), channel_id=1, source_target_pairs={{3,4},{7,8},{11,12},{15,16},{19,20},{23,24},{27,28},{31,32},{35,36... | collective-permute-start | bytes 344072 | tf_op jit(solution)/shard_map/ppermute | solution.py:519
  24.0 12.8 %copy-start = (bf16[1,128,256]{2,1,0:T(8,128)(2,1)S(1)}, bf16[1,128,256]{2,1,0:T(8,128)(2,1)}, u32[]{:S(2)}) copy-start(bf16[1,128,256]{2,1,0:T(8,128)(2,1)} %param.14) | copy-start | bytes 196612
  24.0 12.8 %copy-start.1 = (bf16[1,128,256]{2,1,0:T(8,128)(2,1)S(1)}, bf16[1,128,256]{2,1,0:T(8,128)(2,1)}, u32[]{:S(2)}) copy-start(bf16[1,128,256]{2,1,0:T(8,128)(2,1)} %param.26) | copy-start | bytes 196612
  24.0 12.8 %copy-start.3 = (bf16[256,256]{1,0:T(8,128)(2,1)S(1)}, bf16[256,256]{1,0:T(8,128)(2,1)}, u32[]{:S(2)}) copy-start(bf16[256,256]{1,0:T(8,128)(2,1)} %wm_ref.3) | copy-start | bytes 393220
  24.0 12.8 %copy-start.5 = (s32[1,128,32]{1,2,0:T(8,128)S(1)}, s32[1,128,32]{1,2,0:T(8,128)}, u32[]{:S(2)}) copy-start(s32[1,128,32]{1,2,0:T(8,128)} %param.17) | copy-start | bytes 49156
  24.0 12.8 %copy-start.6 = (f32[1,128,32]{1,2,0:T(8,128)S(1)}, f32[1,128,32]{1,2,0:T(8,128)}, u32[]{:S(2)}) copy-start(f32[1,128,32]{1,2,0:T(8,128)} %param.20) | copy-start | bytes 49156
  24.0 12.8 %copy-start.7 = (bf16[20,256]{1,0:T(8,128)(2,1)S(1)}, bf16[20,256]{1,0:T(8,128)(2,1)}, u32[]{:S(2)}) copy-start(bf16[20,256]{1,0:T(8,128)(2,1)} %wf_ref.1) | copy-start | bytes 30724
  24.0 25.1 %all-to-all-start.1 = ((bf16[16,48,128]{2,1,0:T(8,128)(2,1)}), bf16[16,48,128]{2,1,0:T(8,128)(2,1)S(1)}, u32[]{:S(2)}, u32[]{:S(2)}) async-start(bf16[16,48,128]{2,1,0:T(8,128)(2,1)} %get-tuple-element.27), calls=%async_computation.1 | async-start | bytes 393216 | tf_op jit(solution)/shard_map/all_to_all | solution.py:474
  36.7 0.7 copy-start.10
  36.7 0.7 copy-start.11
  37.4 11.6 %copy-start.2 = (bf16[256,256]{1,0:T(8,128)(2,1)S(1)}, bf16[256,256]{1,0:T(8,128)(2,1)}, u32[]{:S(2)}) copy-start(bf16[256,256]{1,0:T(8,128)(2,1)} %wc_ref.1) | copy-start | bytes 393220
  37.4 11.6 %copy-start.8 = (bf16[20,256]{1,0:T(8,128)(2,1)S(1)}, bf16[20,256]{1,0:T(8,128)(2,1)}, u32[]{:S(2)}) copy-start(bf16[20,256]{1,0:T(8,128)(2,1)} %refs_4_.1) | copy-start | bytes 30724
  37.4 11.6 %copy-start.9 = (s32[3,512]{1,0:T(4,128)S(1)}, s32[3,512]{1,0:T(4,128)}, u32[]{:S(2)}) copy-start(s32[3,512]{1,0:T(4,128)} %refs_2_.1) | copy-start | bytes 18436
  103.4 16.3 %all-to-all-start.5 = ((bf16[8,4,40,128]{3,2,1,0:T(8,128)(2,1)}), bf16[8,4,40,128]{3,2,1,0:T(8,128)(2,1)S(1)}, u32[]{:S(2)}, u32[]{:S(2)}) async-start(bf16[8,4,40,128]{3,2,1,0:T(8,128)(2,1)} %shard_map.188), calls=%async_computation.5 | async-start | bytes 655360 | tf_op jit(solution)/shard_map/all_to_all | solution.py:474

commit v5 on v4

--- a/solution.py
+++ b/solution.py
@@ -82,26 +82,17 @@
     return value * jax.nn.sigmoid(value)
 
 
-NO_ROW = 255
-
-
 def first_kernel(
     count_ref,
-    place_ref,
     feat_ref,
     cot_ref,
     frac_ref,
     list_ref,
-    index_ref,
-    used_ref,
-    length_ref,
     shared_ref,
-    wrap_ref,
     list_s,
 ):
     atoms, channels = feat_ref.shape
     ghosts = list_ref.shape[1]
-    slots = index_ref.shape[0]
     live = column_iota((atoms, channels), 0) < count_ref[0, 0]
     zero = jnp.zeros((atoms, channels), f32)
     feat = jnp.where(live, feat_ref[...].astype(f32), zero).astype(bf16)
@@ -117,23 +108,10 @@
     left = jnp.concatenate([high, low], axis=0)
     right = jnp.concatenate([middle, list_s[...]], axis=0)
     coords = jnp.concatenate([left, right], axis=1).astype(bf16)
-    valid = column_iota((slots, atoms), 0) < used_ref[...]
-    index = jnp.where(valid, index_ref[...], NO_ROW).astype(f32)
-    high, middle, low = split_three(length_ref[...])
-    edges = jnp.concatenate(
-        [jnp.concatenate([index, high], axis=1), jnp.concatenate([middle, low], axis=1)], axis=0
-    ).astype(bf16)
-
     for copy in range(shared_ref.shape[0]):
         shared_ref[copy, 0:atoms, :] = feat
         shared_ref[copy, atoms : 2 * atoms, :] = cot
-        shared_ref[copy, 2 * atoms : 2 * atoms + 16, :] = coords
-        shared_ref[copy, 2 * atoms + 16 :, :] = edges
-    chosen = jnp.where(place_ref[0] == 0, list_ref[0:1, :], list_ref[1:2, :])
-    pick = (column_iota((atoms, ghosts), 0) == chosen).astype(f32).astype(bf16)
-    wrap_ref[0:ghosts, :] = dot(pick, feat, TN).astype(bf16)
-    wrap_ref[ghosts : ghosts + atoms, :] = cot
-    wrap_ref[ghosts + atoms :, :] = edges
+        shared_ref[copy, 2 * atoms :, :] = coords
 
 
 def split_three(value):
@@ -168,138 +146,128 @@
     sums_ref[...] = packed(sums.reshape(owners, ROWS_OWN, channels)).astype(bf16)
 
 
+def paired(rows, j):
+    return jnp.concatenate([rows[j : j + 1, :], rows[j + 1 : j + 2, :]], axis=1)
+
+
+def push_kernel(
+    count_ref,
+    place_ref,
+    feat_ref,
+    list_ref,
+    index_ref,
+    used_ref,
+    length_ref,
+    wf_ref,
+    cot_ref,
+    ext_ref,
+    basis_ref,
+    wrap_ref,
+    pick_s,
+    push_s,
+):
+    atoms, channels = cot_ref.shape
+    slots = index_ref.shape[0]
+    ghosts = list_ref.shape[1]
+    bins = wf_ref.shape[0]
+    table = ext_ref.shape[0]
+    at_start = place_ref[0] == 0
+    bin_at = column_iota((ROWS_OWN, 2 * atoms), 0).astype(f32)
+    spacing = cutoff_radius / (bins - 1)
+    wf = wf_ref[...]
+    index = index_ref[...]
+    length = length_ref[...]
+    live = column_iota((1, atoms), 1) < count_ref[0, 0]
+    cot = jnp.where(live, cot_ref[...].astype(f32).T, 0.0)
+    cot_pair = jnp.concatenate([cot, cot], axis=1)
+    used = jnp.where(live, used_ref[...], 0)
+    envelope = 0.5 * (jnp.cos(math.pi * length / cutoff_radius) + 1.0)
+    envelope = jnp.where(column_iota((slots, atoms), 0) < used, envelope, 0.0)
+    row_at = column_iota((table, 2 * atoms), 0)
+    for step in range(slots // 2):
+        j = 2 * step
+        here = pl.ds(step * 2 * atoms, 2 * atoms)
+        scaled = (paired(length, j) - cutoff_radius * bin_at / (bins - 1)) / spacing
+        basis = jnp.exp(-0.5 * scaled * scaled) * paired(envelope, j)
+        basis = jnp.where(bin_at < bins, basis, 0.0).astype(bf16)
+        basis_ref[:, here] = basis
+        pick_s[:, here] = jnp.where(row_at == paired(index, j), 1.0, 0.0).astype(bf16)
+        push_s[:, here] = (cot_pair * dot(wf, basis[:bins], TN)).astype(bf16)
+    ext = dot(push_s[...], pick_s[...], NT).T
+    ext_ref[...] = ext
+    chosen = jnp.where(at_start, list_ref[0:1, :], list_ref[1:2, :])
+    pick = (column_iota((atoms, ghosts), 0) == chosen).astype(f32).astype(bf16)
+    wrap_ref[:ghosts] = dot(pick, feat_ref[...], TN).astype(bf16)
+    lower, upper = ext[atoms : atoms + ghosts], ext[atoms + ghosts :]
+    wrap_ref[ghosts:] = jnp.where(at_start, lower, upper).astype(bf16)
+
+
 def edge_kernel(
-    count_ref,
     place_ref,
     feat_ref,
     wrap_ref,
     shared_ref,
     wm_ref,
     index_ref,
-    used_ref,
-    length_ref,
+    basis_ref,
     wf_ref,
-    cot_ref,
-    list_ref,
+    ext_ref,
     messages_ref,
-    pre_ref,
+    slope_ref,
     message_ref,
     filter_ref,
-    pick_s,
-    basis_s,
     grad_s,
-    push_s,
-    near_pick_s,
-    near_push_s,
     near_s,
-    near_rows_s,
 ):
     atoms, channels = feat_ref.shape
     slots = index_ref.shape[0]
-    ghosts = list_ref.shape[1]
+    ghosts = wrap_ref.shape[0] // 2
     bins = wf_ref.shape[0]
-    table = atoms + 2 * ghosts
-    padded = basis_s.shape[0]
+    table = ext_ref.shape[0]
     peers = shared_ref.shape[0]
     place = place_ref[0]
     at_end = [place == 0, place == peers - 1]
     beside = [lax.rem(place + peers - 1, peers), lax.rem(place + 1, peers)]
 
-    def take_block(side):
+    def take_rows(side):
+        here = pl.ds(side * ghosts, ghosts)
+
         @pl.when(at_end[side])
         def _():
-            near_rows_s[side] = wrap_ref[:ghosts]
-            near_s[side, atoms : 2 * atoms] = wrap_ref[ghosts : ghosts + atoms]
-            near_s[side, 2 * atoms + 16 :] = wrap_ref[ghosts + atoms :]
+            near_s[here] = wrap_ref[:ghosts]
 
         @pl.when(jnp.logical_not(at_end[side]))
         def _():
-            near_s[side] = shared_ref[beside[side]]
-            lists = near_s[side, 2 * atoms : 2 * atoms + 16, :].astype(f32)[8:16, atoms:]
+            lists = shared_ref[beside[side], 2 * atoms :, :].astype(f32)[8:16, atoms:]
             picked = lists[1 - side : 2 - side, :ghosts]
             rows = column_iota((atoms, ghosts), 0).astype(f32) == picked
-            rows = dot(rows.astype(f32).astype(bf16), near_s[side, :atoms, :], TN)
-            near_rows_s[side] = rows.astype(bf16)
-
-    take_block(0)
-    take_block(1)
-
-    def ghost_rows(side):
-        return silu(dot(near_rows_s[side], wm_ref[...])).astype(bf16).astype(f32)
-
-    hidden = dot(feat_ref[...], wm_ref[...])
-    act = silu(hidden).astype(bf16).astype(f32)
-    ext_t = jnp.concatenate([act, ghost_rows(0), ghost_rows(1)], axis=0).T.astype(bf16)
-    bin_at = column_iota((padded, 2 * atoms), 0).astype(f32)
-    spacing = cutoff_radius / (bins - 1)
+            rows = dot(rows.astype(f32).astype(bf16), shared_ref[beside[side], :atoms, :], TN)
+            near_s[here] = rows.astype(bf16)
+
+    take_rows(0)
+    take_rows(1)
+    feat = jnp.concatenate([feat_ref[...], near_s[...]], axis=0)
+    hidden = dot(feat, wm_ref[...])
+    sigma = jax.nn.sigmoid(hidden)
+    ext_t = (hidden * sigma).T.astype(bf16)
+    slope = sigma * (1.0 + hidden * (1.0 - sigma))
+    slope_ref[...] = slope[:atoms]
+    message_ref[...] = dot(feat, (ext_ref[...] * slope).astype(bf16), TN)
     wf = wf_ref[...]
-
-    def envelope_of(length, valid):
-        envelope = 0.5 * (jnp.cos(math.pi * length / cutoff_radius) + 1.0)
-        return jnp.where(valid, envelope, 0.0)
-
-    def paired(rows, j):
-        return jnp.concatenate([rows[j : j + 1, :], rows[j + 1 : j + 2, :]], axis=1)
-
-    def basis_of(length, envelope, j):
-        scaled = (paired(length, j) - cutoff_radius * bin_at / (bins - 1)) / spacing
-        basis = jnp.exp(-0.5 * scaled * scaled) * paired(envelope, j)
-        return jnp.where(bin_at < bins, basis, 0.0).astype(bf16)
-
-    def doubled(value):
-        return jnp.concatenate([value, value], axis=1)
-
     index = index_ref[...]
-    length = length_ref[...]
-    live = column_iota((1, atoms), 1) < count_ref[0, 0]
-    cot_pair = doubled(jnp.where(live, cot_ref[...].astype(f32).T, 0.0))
-    used = jnp.where(live, used_ref[...], 0)
-    envelope = envelope_of(length, column_iota((slots, atoms), 0) < used)
+    cot = shared_ref[place, atoms : 2 * atoms, :].astype(f32).T
+    cot_pair = jnp.concatenate([cot, cot], axis=1)
     row_at = column_iota((table, 2 * atoms), 0)
     total = jnp.zeros((channels, 2 * atoms), f32)
     for step in range(slots // 2):
-        j = 2 * step
         here = pl.ds(step * 2 * atoms, 2 * atoms)
-        basis = basis_of(length, envelope, j)
-        basis_s[:, here] = basis
-        weights = dot(wf, basis[:bins], TN)
-        pick = jnp.where(row_at == paired(index, j), 1.0, 0.0).astype(bf16)
-        pick_s[:, here] = pick[:atoms]
+        weights = dot(wf, basis_ref[:bins, here], TN)
+        pick = jnp.where(row_at == paired(index, 2 * step), 1.0, 0.0).astype(bf16)
         gathered = dot(ext_t, pick)
         total = total + weights * gathered
         grad_s[:, here] = (cot_pair * gathered).astype(bf16)
-        push_s[:, here] = (cot_pair * weights).astype(bf16)
     messages_ref[...] = (total[:, :atoms] + total[:, atoms:]).T
-    filter_ref[...] = dot(basis_s[...], grad_s[...], NT)
-    act_grad = dot(push_s[...], pick_s[...], NT)
-
-    ghost_at = column_iota((ghosts, 2 * atoms), 0).astype(f32)
-    lists = list_ref[...]
-    for side in range(2):
-        edges = near_s[side, 2 * atoms + 16 :, :].astype(f32)
-        near_index = edges[:slots, :atoms]
-        near_length = edges[:slots, atoms:] + (edges[slots:, :atoms] + edges[slots:, atoms:])
-        first = atoms + ghosts * (1 - side)
-        near_index = near_index - first
-        inside = jnp.logical_and(near_index >= 0.0, near_index < ghosts)
-        near_envelope = envelope_of(near_length, inside)
-        near_cot = doubled(near_s[side, atoms : 2 * atoms, :].astype(f32).T)
-        for step in range(slots // 2):
-            j = 2 * step
-            here = pl.ds(step * 2 * atoms, 2 * atoms)
-            weights = dot(wf, basis_of(near_length, near_envelope, j)[:bins], TN)
-            pick = jnp.where(ghost_at == paired(near_index, j), 1.0, 0.0).astype(bf16)
-            near_pick_s[side, :, here] = pick
-            near_push_s[side, :, here] = (near_cot * weights).astype(bf16)
-        near_grad = dot(near_push_s[side], near_pick_s[side], NT)
-        at = column_iota((atoms, ghosts), 0) == lists[side : side + 1, :]
-        at = at.astype(f32).astype(bf16)
-        high, low = split_two(near_grad)
-        act_grad = act_grad + (dot(high, at, NT) + dot(low, at, NT))
-    sigma = jax.nn.sigmoid(hidden)
-    pre = (act_grad.T * (sigma * (1.0 + hidden * (1.0 - sigma)))).astype(bf16)
-    pre_ref[...] = pre
-    message_ref[...] = dot(feat_ref[...], pre, TN)
+    filter_ref[...] = dot(basis_ref[...], grad_s[...], NT)
 
 
 def total_of(parts_ref, rows=slice(None)):
@@ -315,17 +283,23 @@
     out_ref[...] = jnp.broadcast_to(both[None], out_ref.shape)
 
 
-def apply_kernel(parts_ref, table_ref, out_ref):
+def apply_kernel(place_ref, parts_ref, table_ref, back_ref, out_ref):
     peers, rows, lanes = out_ref.shape
     total = table_ref.shape[0]
     parts = parts_ref[...].astype(f32)
     weights = unpacked(parts[:, :PACK_ROWS]).reshape(total, 2 * lanes).astype(bf16)
     grads = jnp.sum(parts[:, PACK_ROWS:], axis=0).astype(bf16)
-    half = (rows - CHUNK_ROWS) // 2
+    both = table_ref.shape[1] // peers
+    back = back_ref[2 * (back_ref.shape[0] // 3) :]
+    ghosts = back.shape[0] // 2
+    lower, upper = packed(back[:ghosts]), packed(back[ghosts:])
+    below = lax.rem(place_ref[0] + peers - 1, peers)
     for peer in range(peers):
-        piece = table_ref[:, half * peer : half * (peer + 1)]
-        out_ref[peer, : 2 * half, :] = packed(dot(piece, weights, TN)).astype(bf16)
-        out_ref[peer, 2 * half :, :] = grads
+        piece = table_ref[:, both * peer : both * (peer + 1)]
+        out_ref[peer, : 2 * both, :] = packed(dot(piece, weights, TN)).astype(bf16)
+        chosen = jnp.where(below == peer, lower, upper).astype(bf16)
+        out_ref[peer, 2 * both : 2 * both + 2 * ghosts, :] = chosen
+        out_ref[peer, 2 * both + 2 * ghosts :, :] = grads
 
 
 def hand_on_kernel(parts_ref, out_ref):
@@ -416,17 +390,42 @@
 
 
 def final_kernel(
-    count_ref, parts_ref, feat_ref, messages_ref, cot_ref, pre_ref, wm_ref, wc_ref, updated_ref, grad_ref
+    count_ref,
+    place_ref,
+    parts_ref,
+    feat_ref,
+    messages_ref,
+    cot_ref,
+    ext_ref,
+    slope_ref,
+    wrap_ref,
+    list_ref,
+    wm_ref,
+    wc_ref,
+    updated_ref,
+    grad_ref,
 ):
     atoms, channels = feat_ref.shape
+    ghosts = list_ref.shape[1]
+    peers = parts_ref.shape[0]
+    place = place_ref[0]
     both = unpacked(total_of(parts_ref, slice(0, 4 * atoms)))
     live = column_iota((atoms, channels), 0) < count_ref[0, 0]
     added = jnp.where(live, messages_ref[...] + both[:atoms], 0.0)
     updated_ref[...] = (feat_ref[...].astype(f32) + added).astype(bf16)
     charge_grad = jnp.where(live, both[atoms:], 0.0).astype(bf16)
+    wrapped = wrap_ref[ghosts:].astype(f32)
+    lists = list_ref[...]
+    act_grad = ext_ref[:atoms]
+    for which, step, end in ((0, peers - 1, 0), (1, 1, peers - 1)):
+        rows = parts_ref[lax.rem(place + step, peers), 4 * atoms : 4 * atoms + 2 * ghosts, :]
+        rows = jnp.where(place == end, wrapped, unpacked(rows.astype(f32))).astype(bf16)
+        at = column_iota((atoms, ghosts), 0) == lists[which : which + 1, :]
+        act_grad = act_grad + dot(at.astype(f32).astype(bf16), rows)
+    pre = (act_grad * slope_ref[...]).astype(bf16)
     grad_ref[...] = (
         cot_ref[...].astype(f32)
-        + dot(pre_ref[...], wm_ref[...], NT)
+        + dot(pre, wm_ref[...], NT)
         + dot(charge_grad, wc_ref[...], NT)
     )
 
@@ -503,20 +502,31 @@
     place_y, place_z = lax.axis_index("y"), lax.axis_index("z")
     here = place_y.reshape(1).astype(jnp.int32)
     index, length = neighbor_index[0].T, distances[0].T
-    rows = 2 * atoms + 16 + 2 * slots
-    shared, wrap = on_core(
+    rows = 2 * atoms + 16
+    shared = on_core(
         first_kernel,
+        [shape((size_y, rows, channels), bf16)],
+        1,
+        5,
+        [pltpu.VMEM((8, LANES), f32)],
+        streamed=True,
+    )(counts, feat, cot, jnp.swapaxes(fractional, 0, 1), lists)[0]
+    edges = slots * atoms
+    table_rows = atoms + 2 * ghosts
+    ext_grad, basis, wrap = on_core(
+        push_kernel,
         [
-            shape((size_y, rows, channels), bf16),
-            shape((ghosts + atoms + 2 * slots, channels), bf16),
+            shape((table_rows, channels), f32),
+            shape((ROWS_OWN, edges), bf16),
+            shape((2 * ghosts, channels), bf16),
         ],
         2,
         9,
-        [pltpu.VMEM((8, LANES), f32)],
-        streamed=True,
-    )(counts, here, feat, cot, jnp.swapaxes(fractional, 0, 1), lists, index, neighbor_count, length)
+        [pltpu.VMEM((table_rows, edges), bf16), pltpu.VMEM((channels, edges), bf16)],
+    )(counts, here, feat, lists, index, neighbor_count, length, w_filter, cot)
     ends = [(z * size_y + size_y - 1, (z + 1) % size_z * size_y) for z in range(size_z)]
-    wrap = lax.ppermute(wrap, space, ends + [(t, s) for s, t in ends])
+    ends = ends + [(t, s) for s, t in ends]
+    wrap = lax.ppermute(wrap, space, ends)
     shared = exchanged(shared, "y")
 
     total = size_z * ROWS_OWN
@@ -529,41 +539,18 @@
     sums, wrap = lax.optimization_barrier((sums, wrap))
     sums = exchanged(sums, "z")
 
-    edges = slots * atoms
-    messages, pre, message_term, filter_term = on_core(
+    messages, slope, message_term, filter_term = on_core(
         edge_kernel,
         [
             shape((atoms, channels), f32),
-            shape((atoms, channels), bf16),
+            shape((atoms, channels), f32),
             shape((channels, channels), f32),
             shape((ROWS_OWN, channels), f32),
         ],
-        2,
-        12,
-        [
-            pltpu.VMEM((atoms, edges), bf16),
-            pltpu.VMEM((ROWS_OWN, edges), bf16),
-            pltpu.VMEM((channels, edges), bf16),
-            pltpu.VMEM((channels, edges), bf16),
-            pltpu.VMEM((2, ghosts, edges), bf16),
-            pltpu.VMEM((2, channels, edges), bf16),
-            pltpu.VMEM((2, rows, channels), bf16),
-            pltpu.VMEM((2, ghosts, channels), bf16),
-        ],
-    )(
-        counts,
-        here,
-        feat,
-        wrap,
-        shared,
-        w_message,
-        index,
-        neighbor_count,
-        length,
-        w_filter,
-        cot,
-        lists,
-    )
+        1,
+        9,
+        [pltpu.VMEM((channels, edges), bf16), pltpu.VMEM((2 * ghosts, channels), bf16)],
+    )(here, feat, wrap, shared, w_message, index, basis, w_filter, ext_grad)
     owner = place_y * size_z + place_z
     grads, weights = on_core(
         lambda *refs: middle_kernel(scale, *refs),
@@ -586,8 +573,10 @@
     rows = PACK_ROWS + CHUNK_ROWS
     parts = on_core(join_kernel, [shape((size_z, rows, LANES), bf16)], 0, 2)(parts, weights)[0]
     parts = exchanged(parts, "z")
-    rows = 4 * atoms + CHUNK_ROWS
-    parts = on_core(apply_kernel, [shape((size_y, rows, LANES), bf16)], 0, 2)(parts, table)[0]
+    rows = 4 * atoms + 2 * ghosts + CHUNK_ROWS
+    parts = on_core(apply_kernel, [shape((size_y, rows, LANES), bf16)], 1, 4)(
+        here, parts, table, ext_grad
+    )[0]
     parts = exchanged(parts, "y")
     slabs = lax.axis_size("x") * lax.axis_size("core")
     grads = on_core(hand_on_kernel, [shape((slabs, size_y, CHUNK_ROWS, LANES), bf16)], 0, 1)(
@@ -598,9 +587,22 @@
     updated, grad_features = on_core(
         final_kernel,
         [shape((atoms, channels), bf16), shape((atoms, channels), f32)],
-        1,
-        8,
-    )(counts, parts, feat, messages, cot, pre, w_message, w_charge)
+        2,
+        12,
+    )(
+        counts,
+        here,
+        parts,
+        feat,
+        messages,
+        cot,
+        ext_grad,
+        slope,
+        wrap,
+        lists,
+        w_message,
+        w_charge,
+    )
     grad_message, grad_charge, grad_filter, grad_kspace = on_core(
         unpack_kernel,
         [

time: 121 us -> 118 us (0.975)
  waiting for transfers between devices: 10.9 us -> 16.2 us
  starting transfers between devices: 40.5 us -> 36.1 us
  Pallas kernels: 14.5 us -> 10.6 us
    all_to_all x3, waiting for transfers between devices: 10.3 us -> 16.2 us  [exchanged(): return lax.all_to_all(value, axis, 0, 0, tiled=True)]
    pallas_call x1, Pallas kernels: 7.59 us -> 2.24 us  [body(): on_core(edge_kernel, [shape((atoms, channels), f32), shape((atoms, channe...]
    all_to_all x3, starting transfers between devices: 27 us -> 22.6 us  [exchanged(): return lax.all_to_all(value, axis, 0, 0, tiled=True)]
    pallas_call x1 -> x2, Pallas kernels: 0.48 us -> 1.95 us  [the longest x1 1.47 us: body(): on_core(push_kernel, [shape((table_rows, channels), f32), shape((ROWS_OWN...]
  transfers between devices with their start and end apart: 4 -> 4, of which waited for: 3 -> 2; matrix products, arithmetic and copies ran while one was open for 0% -> 0% of each run, Pallas kernels for 8% -> 5%
where the time goes in v5:
time: 118 us; the launch traced here: 117 us
  blocking collectives  52.5 us (44%)
  starting transfers between devices  36.1 us (31%)
  waiting for transfers between devices  16.2 us (14%)
  Pallas kernels  10.6 us (9%)
  between operations  1.44 us (1%)
    all_to_all x3, blocking collectives, exchanged(): return lax.all_to_all(value, axis, 0, 0, tiled=True)  52.5 us
    all_to_all x3, starting transfers between devices, exchanged(): return lax.all_to_all(value, axis, 0, 0, tiled=True)  22.6 us
    all_to_all x3, waiting for transfers between devices, exchanged(): return lax.all_to_all(value, axis, 0, 0, tiled=True)  16.2 us
    ppermute x1, starting transfers between devices, body(): wrap = lax.ppermute(wrap, space, ends)  13.5 us
  transfers between devices with their start and end apart: 4, of which 2 were waited for; matrix products, arithmetic and copies ran while one was open for 0% of the time, Pallas kernels for 5%

profile of v5, /device:TPU:1, one launch (start us, length us, event | category | flops | bytes accessed | tf_op | source)
XLA Modules:
  0.0 117.5 jit_solution(12768985334961782595)
XLA Ops:
  1.3 1.7 %shard_map.181 = bf16[4,272,256]{2,1,0:T(8,128)(2,1)} custom-call(s32[1,1]{1,0:T(1,128)S(6)} %copy.20.count_ref, bf16[128,256]{1,0:T(8,128)(2,1)} %bitcast.16, bf16[128,256]{1,0:T(8,128)(2,1)} %bitcast.20, f32[3,1,128]{2,1,0:T(1,128)} %bitcast.29, s32[2,32]{1,0:T(2,128)} %bitcast.26), custom_call_target="tpu_custom_call" | custom-call | tf_op jit(solution)/shard_map/pallas_call | solution.py:448
  3.0 0.0 copy-start
  3.0 0.0 copy-start.1
  3.0 0.0 copy-start.5
  3.0 0.0 copy-start.6
  3.0 0.0 copy-start.7
  3.1 0.0 copy-start.4
  3.1 5.2 %all-to-all-start = ((bf16[4,272,256]{2,1,0:T(8,128)(2,1)}), bf16[4,272,256]{2,1,0:T(8,128)(2,1)S(1)}, u32[]{:S(2)}, u32[]{:S(2)}) async-start(bf16[4,272,256]{2,1,0:T(8,128)(2,1)} %shard_map.181), calls=%async_computation | async-start | bytes 1114112 | tf_op jit(solution)/shard_map/all_to_all | solution.py:473
  8.2 0.0 copy-start.9
  8.2 0.0 copy-start.11
  8.2 0.0 copy-done
  8.2 0.0 copy-done.1
  8.2 0.0 copy-done.5
  8.3 0.0 copy-done.6
  8.3 0.0 copy-done.7
  8.3 0.6 copy-done.9
  8.9 0.0 copy-done.11
  8.9 1.5 %shard_map.183 = (f32[192,256]{1,0:T(8,128)S(1)}, bf16[24,4096]{1,0:T(8,128)(2,1)S(1)}, bf16[64,256]{1,0:T(8,128)(2,1)S(1)}) custom-call(s32[1,1]{1,0:T(1,128)S(6)} %copy.20.count_ref, s32[1]{0:T(128)} %bitcast.place_ref, bf16[128,256]{1,0:T(8,128)(2,1)S(1)} %bitcast.17, s32[2,32]{1,0:T(2,128)S(1)} %bitcast.27, s32[32,128]{1,0:T(8,128)S(1)} %bitcast.23, ...), custom_call_target="tpu_custom_call" | custom-call | tf_op jit(solution)/shard_map/pallas_call | solution.py:516
  10.4 13.5 %collective-permute-start = (bf16[64,256]{1,0:T(8,128)(2,1)S(1)}, bf16[64,256]{1,0:T(8,128)(2,1)S(1)}, u32[]{:S(2)}, u32[]{:S(2)}) collective-permute-start(bf16[64,256]{1,0:T(8,128)(2,1)S(1)} %get-tuple-element.26), channel_id=1, source_target_pairs={{3,4},{7,8},{11,12},{15,16},{19,20},{23,24},{27,28},{31,32},{35,36... | collective-permute-start | bytes 98312 | tf_op jit(solution)/shard_map/ppermute | solution.py:529
  23.9 0.0 all-to-all-done.atoms_ref.shared_ref
  23.9 0.0 copy-done.4
  23.9 1.6 %shard_map.182 = (bf16[384,1024]{1,0:T(8,128)(2,1)S(1)}, bf16[16,48,128]{2,1,0:T(8,128)(2,1)}) custom-call(s32[1]{0:T(128)} %bitcast.place_ref, bf16[4,272,256]{2,1,0:T(8,128)(2,1)S(1)} %all-to-all-done.atoms_ref.shared_ref, bf16[1536,8]{1,0:T(8,128)(2,1)S(1)} %copy-done.4), custom_call_target="tpu_custom_call" | custom-call | tf_op jit(solution)/shard_map/pallas_call | solution.py:533
  25.5 0.0 collective-permute-done.wrap_ref
  25.5 0.0 copy-start.2
  25.5 8.3 %all-to-all-start.1 = ((bf16[16,48,128]{2,1,0:T(8,128)(2,1)}), bf16[16,48,128]{2,1,0:T(8,128)(2,1)S(1)}, u32[]{:S(2)}, u32[]{:S(2)}) async-start(bf16[16,48,128]{2,1,0:T(8,128)(2,1)} %get-tuple-element.27), calls=%async_computation.1 | async-start | bytes 393216 | tf_op jit(solution)/shard_map/all_to_all | solution.py:473
  33.8 0.0 copy-done.2
  33.8 0.0 copy-start.3
  33.8 0.0 copy-start.8
  33.8 0.0 copy-start.10
  33.8 2.2 %shard_map.184 = (f32[128,256]{1,0:T(8,128)S(1)}, f32[128,256]{1,0:T(8,128)S(1)}, f32[256,256]{1,0:T(8,128)S(1)}, f32[24,256]{1,0:T(8,128)S(1)}) custom-call(s32[1]{0:T(128)} %bitcast.place_ref, bf16[128,256]{1,0:T(8,128)(2,1)S(1)} %bitcast.18, bf16[64,256]{1,0:T(8,128)(2,1)S(1)} %collective-permute-done.wrap_ref, ...), custom_call_target="tpu_custom_call" | custom-call | tf_op jit(solution)/shard_map/pallas_call | solution.py:542
  36.0 10.0 %all-to-all-done.1.refs_1_ = bf16[16,48,128]{2,1,0:T(8,128)(2,1)S(1)} async-done(((bf16[16,48,128]{2,1,0:T(8,128)(2,1)}), bf16[16,48,128]{2,1,0:T(8,128)(2,1)S(1)}, u32[]{:S(2)}, u32[]{:S(2)}) %all-to-all-start.1) | async-done | bytes 196640 | tf_op jit(solution)/shard_map/all_to_all | solution.py:473
  46.1 0.0 copy-done.3
  46.1 0.0 copy-done.8
  46.1 0.0 copy-done.10
  46.1 0.4 shard_map.185
  46.6 20.2 %all_to_all.30.parts_ref = bf16[32,40,128]{2,1,0:T(8,128)(2,1)S(1)} all-to-all(bf16[32,40,128]{2,1,0:T(8,128)(2,1)S(1)} %get-tuple-element.33), channel_id=1, replica_groups=mesh['x'=4,'core'=2,'z'=16,'y'=4] {'x','core','y'}, dimensions={0} | all-to-all | bytes 655360 | tf_op jit(solution)/shard_map/all_to_all | solution.py:473
  66.7 0.1 shard_map.186
  66.8 19.7 %all_to_all.31.parts_ref = bf16[16,88,128]{2,1,0:T(8,128)(2,1)S(1)} all-to-all(bf16[16,88,128]{2,1,0:T(8,128)(2,1)S(1)} %shard_map.186), channel_id=1, replica_groups=mesh['x'=4,'core'=2,'z'=16,'y'=4] {'z'}, dimensions={0} | all-to-all | bytes 720896 | tf_op jit(solution)/shard_map/all_to_all | solution.py:473
  86.5 0.5 shard_map.187
  87.0 12.6 %all_to_all.32.parts_ref = bf16[4,616,128]{2,1,0:T(8,128)(2,1)S(1)} all-to-all(bf16[4,616,128]{2,1,0:T(8,128)(2,1)S(1)} %shard_map.187), channel_id=1, replica_groups=mesh['x'=4,'core'=2,'z'=16,'y'=4] {'y'}, dimensions={0} | all-to-all | bytes 1261568 | tf_op jit(solution)/shard_map/all_to_all | solution.py:473
  99.6 0.8 shard_map.189
  100.4 9.1 %all-to-all-start.5 = ((bf16[8,4,40,128]{3,2,1,0:T(8,128)(2,1)}), bf16[8,4,40,128]{3,2,1,0:T(8,128)(2,1)S(1)}, u32[]{:S(2)}, u32[]{:S(2)}) async-start(bf16[8,4,40,128]{3,2,1,0:T(8,128)(2,1)} %shard_map.189), calls=%async_computation.5 | async-start | bytes 655360 | tf_op jit(solution)/shard_map/all_to_all | solution.py:473
  109.5 1.0 shard_map.188
  110.5 6.2 %all-to-all-done.5 = bf16[8,4,40,128]{3,2,1,0:T(8,128)(2,1)S(1)} async-done(((bf16[8,4,40,128]{3,2,1,0:T(8,128)(2,1)}), bf16[8,4,40,128]{3,2,1,0:T(8,128)(2,1)S(1)}, u32[]{:S(2)}, u32[]{:S(2)}) %all-to-all-start.5) | async-done | bytes 327712 | tf_op jit(solution)/shard_map/all_to_all | solution.py:473
  116.6 0.8 shard_map.190
Async XLA Ops:
  3.0 5.2 %copy-start = (bf16[1,128,256]{2,1,0:T(8,128)(2,1)S(1)}, bf16[1,128,256]{2,1,0:T(8,128)(2,1)}, u32[]{:S(2)}) copy-start(bf16[1,128,256]{2,1,0:T(8,128)(2,1)} %param.14) | copy-start | bytes 196612
  3.0 5.2 %copy-start.1 = (bf16[1,128,256]{2,1,0:T(8,128)(2,1)S(1)}, bf16[1,128,256]{2,1,0:T(8,128)(2,1)}, u32[]{:S(2)}) copy-start(bf16[1,128,256]{2,1,0:T(8,128)(2,1)} %param.26) | copy-start | bytes 196612
  3.0 5.2 %copy-start.5 = (s32[1,128,32]{1,2,0:T(8,128)S(1)}, s32[1,128,32]{1,2,0:T(8,128)}, u32[]{:S(2)}) copy-start(s32[1,128,32]{1,2,0:T(8,128)} %param.17) | copy-start | bytes 49156
  3.0 5.2 %copy-start.6 = (bf16[20,256]{1,0:T(8,128)(2,1)S(1)}, bf16[20,256]{1,0:T(8,128)(2,1)}, u32[]{:S(2)}) copy-start(bf16[20,256]{1,0:T(8,128)(2,1)} %wf_ref.3) | copy-start | bytes 30724
  3.0 5.2 %copy-start.7 = (f32[1,128,32]{1,2,0:T(8,128)S(1)}, f32[1,128,32]{1,2,0:T(8,128)}, u32[]{:S(2)}) copy-start(f32[1,128,32]{1,2,0:T(8,128)} %param.20) | copy-start | bytes 49156
  3.1 20.9 %copy-start.4 = (bf16[1536,8]{1,0:T(8,128)(2,1)S(1)}, bf16[1536,8]{1,0:T(8,128)(2,1)}, u32[]{:S(2)}) copy-start(bf16[1536,8]{1,0:T(8,128)(2,1)} %constant.13.clone.rows_ref) | copy-start | bytes 73732
  3.1 20.8 %all-to-all-start = ((bf16[4,272,256]{2,1,0:T(8,128)(2,1)}), bf16[4,272,256]{2,1,0:T(8,128)(2,1)S(1)}, u32[]{:S(2)}, u32[]{:S(2)}) async-start(bf16[4,272,256]{2,1,0:T(8,128)(2,1)} %shard_map.181), calls=%async_computation | async-start | bytes 1114112 | tf_op jit(solution)/shard_map/all_to_all | solution.py:473
  8.2 0.7 copy-start.9
  8.2 0.7 copy-start.11
  10.4 15.1 %collective-permute-start = (bf16[64,256]{1,0:T(8,128)(2,1)S(1)}, bf16[64,256]{1,0:T(8,128)(2,1)S(1)}, u32[]{:S(2)}, u32[]{:S(2)}) collective-permute-start(bf16[64,256]{1,0:T(8,128)(2,1)S(1)} %get-tuple-element.26), channel_id=1, source_target_pairs={{3,4},{7,8},{11,12},{15,16},{19,20},{23,24},{27,28},{31,32},{35,36... | collective-permute-start | bytes 98312 | tf_op jit(solution)/shard_map/ppermute | solution.py:529
  25.5 8.3 %copy-start.2 = (bf16[256,256]{1,0:T(8,128)(2,1)S(1)}, bf16[256,256]{1,0:T(8,128)(2,1)}, u32[]{:S(2)}) copy-start(bf16[256,256]{1,0:T(8,128)(2,1)} %wm_ref.3) | copy-start | bytes 393220
  25.5 20.6 %all-to-all-start.1 = ((bf16[16,48,128]{2,1,0:T(8,128)(2,1)}), bf16[16,48,128]{2,1,0:T(8,128)(2,1)S(1)}, u32[]{:S(2)}, u32[]{:S(2)}) async-start(bf16[16,48,128]{2,1,0:T(8,128)(2,1)} %get-tuple-element.27), calls=%async_computation.1 | async-start | bytes 393216 | tf_op jit(solution)/shard_map/all_to_all | solution.py:473
  33.8 12.3 %copy-start.3 = (bf16[256,256]{1,0:T(8,128)(2,1)S(1)}, bf16[256,256]{1,0:T(8,128)(2,1)}, u32[]{:S(2)}) copy-start(bf16[256,256]{1,0:T(8,128)(2,1)} %wc_ref.1) | copy-start | bytes 393220
  33.8 12.3 %copy-start.8 = (bf16[20,256]{1,0:T(8,128)(2,1)S(1)}, bf16[20,256]{1,0:T(8,128)(2,1)}, u32[]{:S(2)}) copy-start(bf16[20,256]{1,0:T(8,128)(2,1)} %refs_4_.1) | copy-start | bytes 30724
  33.8 12.3 %copy-start.10 = (s32[3,512]{1,0:T(4,128)S(1)}, s32[3,512]{1,0:T(4,128)}, u32[]{:S(2)}) copy-start(s32[3,512]{1,0:T(4,128)} %refs_2_.1) | copy-start | bytes 18436
  100.4 16.3 %all-to-all-start.5 = ((bf16[8,4,40,128]{3,2,1,0:T(8,128)(2,1)}), bf16[8,4,40,128]{3,2,1,0:T(8,128)(2,1)S(1)}, u32[]{:S(2)}, u32[]{:S(2)}) async-start(bf16[8,4,40,128]{3,2,1,0:T(8,128)(2,1)} %shard_map.189), calls=%async_computation.5 | async-start | bytes 655360 | tf_op jit(solution)/shard_map/all_to_all | solution.py:473

commit v6 on v5

--- a/solution.py
+++ b/solution.py
@@ -402,9 +402,12 @@
     list_ref,
     wm_ref,
     wc_ref,
+    grads_ref,
     updated_ref,
     grad_ref,
+    *weight_grad_refs,
 ):
+    unpack_kernel(grads_ref, *weight_grad_refs)
     atoms, channels = feat_ref.shape
     ghosts = list_ref.shape[1]
     peers = parts_ref.shape[0]
@@ -584,11 +587,18 @@
     )[0]
     grads = exchanged(grads, ("x", "core")).reshape(GRAD_CHUNKS, CHUNK_ROWS, LANES)
 
-    updated, grad_features = on_core(
+    updated, grad_features, grad_message, grad_charge, grad_filter, grad_kspace = on_core(
         final_kernel,
-        [shape((atoms, channels), bf16), shape((atoms, channels), f32)],
+        [
+            shape((atoms, channels), bf16),
+            shape((atoms, channels), f32),
+            shape((channels, channels), f32),
+            shape((channels, channels), f32),
+            shape((bins, channels), f32),
+            shape((bins, channels), f32),
+        ],
         2,
-        12,
+        13,
     )(
         counts,
         here,
@@ -602,18 +612,8 @@
         lists,
         w_message,
         w_charge,
+        grads,
     )
-    grad_message, grad_charge, grad_filter, grad_kspace = on_core(
-        unpack_kernel,
-        [
-            shape((channels, channels), f32),
-            shape((channels, channels), f32),
-            shape((bins, channels), f32),
-            shape((bins, channels), f32),
-        ],
-        0,
-        1,
-    )(grads)
     return (updated[None], grad_features[None], grad_message, grad_charge, grad_filter, grad_kspace)
 
 

time: 118 us -> 117 us (level)
  blocking collectives: 52.5 us -> 68.5 us
  starting transfers between devices: 36.1 us -> 26.9 us
  waiting for transfers between devices: 16.2 us -> 10 us
  Pallas kernels: 10.6 us -> 9.11 us
    all_to_all x3 -> x4, blocking collectives: 52.5 us -> 68.5 us  [exchanged(): return lax.all_to_all(value, axis, 0, 0, tiled=True)]
    all_to_all x3 -> x2, starting transfers between devices: 22.6 us -> 13.4 us  [exchanged(): return lax.all_to_all(value, axis, 0, 0, tiled=True)]
    all_to_all x3 -> x2, waiting for transfers between devices: 16.2 us -> 10 us  [exchanged(): return lax.all_to_all(value, axis, 0, 0, tiled=True)]
  transfers between devices with their start and end apart: 4 -> 3, of which waited for: 2 -> 1; matrix products, arithmetic and copies ran while one was open for 0% -> 0% of each run, Pallas kernels for 5% -> 4%
where the time goes in v6:
time: 117 us
  blocking collectives  68.5 us (59%)
  starting transfers between devices  26.9 us (23%)
  waiting for transfers between devices  10 us (9%)
  Pallas kernels  9.11 us (8%)
  between operations  1.44 us (1%)
    all_to_all x4, blocking collectives, exchanged(): return lax.all_to_all(value, axis, 0, 0, tiled=True)  68.5 us
    ppermute x1, starting transfers between devices, body(): wrap = lax.ppermute(wrap, space, ends)  13.5 us
    all_to_all x2, starting transfers between devices, exchanged(): return lax.all_to_all(value, axis, 0, 0, tiled=True)  13.4 us
    all_to_all x2, waiting for transfers between devices, exchanged(): return lax.all_to_all(value, axis, 0, 0, tiled=True)  10 us
  transfers between devices with their start and end apart: 3, of which 1 were waited for; matrix products, arithmetic and copies ran while one was open for 0% of the time, Pallas kernels for 4%

profile of v6, /device:TPU:1, one launch (start us, length us, event | category | flops | bytes accessed | tf_op | source)
XLA Modules:
  0.0 116.8 jit_solution(5461067753330219675)
XLA Ops:
  1.3 1.8 %shard_map.181 = bf16[4,272,256]{2,1,0:T(8,128)(2,1)} custom-call(s32[1,1]{1,0:T(1,128)S(6)} %copy.20.count_ref, bf16[128,256]{1,0:T(8,128)(2,1)} %bitcast.16, bf16[128,256]{1,0:T(8,128)(2,1)} %bitcast.20, f32[3,1,128]{2,1,0:T(1,128)} %bitcast.29, s32[2,32]{1,0:T(2,128)} %bitcast.26), custom_call_target="tpu_custom_call" | custom-call | tf_op jit(solution)/shard_map/pallas_call | solution.py:451
  3.0 0.0 copy-start
  3.0 0.0 copy-start.1
  3.0 0.0 copy-start.5
  3.0 0.0 copy-start.6
  3.0 0.0 copy-start.7
  3.1 0.0 copy-start.4
  3.1 5.2 %all-to-all-start = ((bf16[4,272,256]{2,1,0:T(8,128)(2,1)}), bf16[4,272,256]{2,1,0:T(8,128)(2,1)S(1)}, u32[]{:S(2)}, u32[]{:S(2)}) async-start(bf16[4,272,256]{2,1,0:T(8,128)(2,1)} %shard_map.181), calls=%async_computation | async-start | bytes 1114112 | tf_op jit(solution)/shard_map/all_to_all | solution.py:476
  8.2 0.0 copy-start.9
  8.2 0.0 copy-start.11
  8.2 0.0 copy-done
  8.2 0.0 copy-done.1
  8.2 0.0 copy-done.5
  8.3 0.0 copy-done.6
  8.3 0.0 copy-done.7
  8.3 0.6 copy-done.9
  8.9 0.0 copy-done.11
  8.9 1.5 %shard_map.183 = (f32[192,256]{1,0:T(8,128)S(1)}, bf16[24,4096]{1,0:T(8,128)(2,1)S(1)}, bf16[64,256]{1,0:T(8,128)(2,1)S(1)}) custom-call(s32[1,1]{1,0:T(1,128)S(6)} %copy.20.count_ref, s32[1]{0:T(128)} %bitcast.place_ref, bf16[128,256]{1,0:T(8,128)(2,1)S(1)} %bitcast.17, s32[2,32]{1,0:T(2,128)S(1)} %bitcast.27, s32[32,128]{1,0:T(8,128)S(1)} %bitcast.23, ...), custom_call_target="tpu_custom_call" | custom-call | tf_op jit(solution)/shard_map/pallas_call | solution.py:519
  10.4 13.5 %collective-permute-start = (bf16[64,256]{1,0:T(8,128)(2,1)S(1)}, bf16[64,256]{1,0:T(8,128)(2,1)S(1)}, u32[]{:S(2)}, u32[]{:S(2)}) collective-permute-start(bf16[64,256]{1,0:T(8,128)(2,1)S(1)} %get-tuple-element.26), channel_id=1, source_target_pairs={{3,4},{7,8},{11,12},{15,16},{19,20},{23,24},{27,28},{31,32},{35,36... | collective-permute-start | bytes 98312 | tf_op jit(solution)/shard_map/ppermute | solution.py:532
  23.9 0.0 all-to-all-done.atoms_ref.shared_ref
  23.9 0.0 copy-done.4
  23.9 1.5 %shard_map.182 = (bf16[384,1024]{1,0:T(8,128)(2,1)S(1)}, bf16[16,48,128]{2,1,0:T(8,128)(2,1)}) custom-call(s32[1]{0:T(128)} %bitcast.place_ref, bf16[4,272,256]{2,1,0:T(8,128)(2,1)S(1)} %all-to-all-done.atoms_ref.shared_ref, bf16[1536,8]{1,0:T(8,128)(2,1)S(1)} %copy-done.4), custom_call_target="tpu_custom_call" | custom-call | tf_op jit(solution)/shard_map/pallas_call | solution.py:536
  25.5 0.0 collective-permute-done.wrap_ref
  25.5 0.0 copy-start.2
  25.5 8.3 %all-to-all-start.1 = ((bf16[16,48,128]{2,1,0:T(8,128)(2,1)}), bf16[16,48,128]{2,1,0:T(8,128)(2,1)S(1)}, u32[]{:S(2)}, u32[]{:S(2)}) async-start(bf16[16,48,128]{2,1,0:T(8,128)(2,1)} %get-tuple-element.27), calls=%async_computation.1 | async-start | bytes 393216 | tf_op jit(solution)/shard_map/all_to_all | solution.py:476
  33.8 0.0 copy-done.2
  33.8 0.0 copy-start.3
  33.8 0.0 copy-start.8
  33.8 0.0 copy-start.10
  33.8 2.2 %shard_map.184 = (f32[128,256]{1,0:T(8,128)S(1)}, f32[128,256]{1,0:T(8,128)S(1)}, f32[256,256]{1,0:T(8,128)S(1)}, f32[24,256]{1,0:T(8,128)S(1)}) custom-call(s32[1]{0:T(128)} %bitcast.place_ref, bf16[128,256]{1,0:T(8,128)(2,1)S(1)} %bitcast.18, bf16[64,256]{1,0:T(8,128)(2,1)S(1)} %collective-permute-done.wrap_ref, ...), custom_call_target="tpu_custom_call" | custom-call | tf_op jit(solution)/shard_map/pallas_call | solution.py:545
  36.1 10.0 %all-to-all-done.1.refs_1_ = bf16[16,48,128]{2,1,0:T(8,128)(2,1)S(1)} async-done(((bf16[16,48,128]{2,1,0:T(8,128)(2,1)}), bf16[16,48,128]{2,1,0:T(8,128)(2,1)S(1)}, u32[]{:S(2)}, u32[]{:S(2)}) %all-to-all-start.1) | async-done | bytes 196640 | tf_op jit(solution)/shard_map/all_to_all | solution.py:476
  46.1 0.0 copy-done.3
  46.1 0.0 copy-done.8
  46.1 0.0 copy-done.10
  46.1 0.4 shard_map.185
  46.6 20.2 %all_to_all.30.parts_ref = bf16[32,40,128]{2,1,0:T(8,128)(2,1)S(1)} all-to-all(bf16[32,40,128]{2,1,0:T(8,128)(2,1)S(1)} %get-tuple-element.33), channel_id=1, replica_groups=mesh['x'=4,'core'=2,'z'=16,'y'=4] {'x','core','y'}, dimensions={0} | all-to-all | bytes 655360 | tf_op jit(solution)/shard_map/all_to_all | solution.py:476
  66.7 0.1 shard_map.186
  66.8 19.7 %all_to_all.31.parts_ref = bf16[16,88,128]{2,1,0:T(8,128)(2,1)S(1)} all-to-all(bf16[16,88,128]{2,1,0:T(8,128)(2,1)S(1)} %shard_map.186), channel_id=1, replica_groups=mesh['x'=4,'core'=2,'z'=16,'y'=4] {'z'}, dimensions={0} | all-to-all | bytes 720896 | tf_op jit(solution)/shard_map/all_to_all | solution.py:476
  86.5 0.5 shard_map.187
  87.0 12.6 %all_to_all.32.parts_ref = bf16[4,616,128]{2,1,0:T(8,128)(2,1)S(1)} all-to-all(bf16[4,616,128]{2,1,0:T(8,128)(2,1)S(1)} %shard_map.187), channel_id=1, replica_groups=mesh['x'=4,'core'=2,'z'=16,'y'=4] {'y'}, dimensions={0} | all-to-all | bytes 1261568 | tf_op jit(solution)/shard_map/all_to_all | solution.py:476
  99.6 16.1 %all_to_all.33 = bf16[8,4,40,128]{3,2,1,0:T(8,128)(2,1)S(1)} all-to-all(bf16[8,4,40,128]{3,2,1,0:T(8,128)(2,1)S(1)} %shard_map.188), channel_id=1, replica_groups=mesh['x'=4,'core'=2,'z'=16,'y'=4] {'x','core'}, dimensions={0} | all-to-all | bytes 655360 | tf_op jit(solution)/shard_map/all_to_all | solution.py:476
  115.7 1.1 shard_map.189
  (1 shorter events, 0.0 us)
Async XLA Ops:
  3.0 5.2 %copy-start = (bf16[1,128,256]{2,1,0:T(8,128)(2,1)S(1)}, bf16[1,128,256]{2,1,0:T(8,128)(2,1)}, u32[]{:S(2)}) copy-start(bf16[1,128,256]{2,1,0:T(8,128)(2,1)} %param.14) | copy-start | bytes 196612
  3.0 5.2 %copy-start.1 = (bf16[1,128,256]{2,1,0:T(8,128)(2,1)S(1)}, bf16[1,128,256]{2,1,0:T(8,128)(2,1)}, u32[]{:S(2)}) copy-start(bf16[1,128,256]{2,1,0:T(8,128)(2,1)} %param.26) | copy-start | bytes 196612
  3.0 5.2 %copy-start.5 = (s32[1,128,32]{1,2,0:T(8,128)S(1)}, s32[1,128,32]{1,2,0:T(8,128)}, u32[]{:S(2)}) copy-start(s32[1,128,32]{1,2,0:T(8,128)} %param.17) | copy-start | bytes 49156
  3.0 5.2 %copy-start.6 = (bf16[20,256]{1,0:T(8,128)(2,1)S(1)}, bf16[20,256]{1,0:T(8,128)(2,1)}, u32[]{:S(2)}) copy-start(bf16[20,256]{1,0:T(8,128)(2,1)} %wf_ref.3) | copy-start | bytes 30724
  3.0 5.2 %copy-start.7 = (f32[1,128,32]{1,2,0:T(8,128)S(1)}, f32[1,128,32]{1,2,0:T(8,128)}, u32[]{:S(2)}) copy-start(f32[1,128,32]{1,2,0:T(8,128)} %param.20) | copy-start | bytes 49156
  3.1 20.9 %copy-start.4 = (bf16[1536,8]{1,0:T(8,128)(2,1)S(1)}, bf16[1536,8]{1,0:T(8,128)(2,1)}, u32[]{:S(2)}) copy-start(bf16[1536,8]{1,0:T(8,128)(2,1)} %constant.13.clone.rows_ref) | copy-start | bytes 73732
  3.1 20.8 %all-to-all-start = ((bf16[4,272,256]{2,1,0:T(8,128)(2,1)}), bf16[4,272,256]{2,1,0:T(8,128)(2,1)S(1)}, u32[]{:S(2)}, u32[]{:S(2)}) async-start(bf16[4,272,256]{2,1,0:T(8,128)(2,1)} %shard_map.181), calls=%async_computation | async-start | bytes 1114112 | tf_op jit(solution)/shard_map/all_to_all | solution.py:476
  8.2 0.7 copy-start.9
  8.2 0.7 copy-start.11
  10.4 15.1 %collective-permute-start = (bf16[64,256]{1,0:T(8,128)(2,1)S(1)}, bf16[64,256]{1,0:T(8,128)(2,1)S(1)}, u32[]{:S(2)}, u32[]{:S(2)}) collective-permute-start(bf16[64,256]{1,0:T(8,128)(2,1)S(1)} %get-tuple-element.26), channel_id=1, source_target_pairs={{3,4},{7,8},{11,12},{15,16},{19,20},{23,24},{27,28},{31,32},{35,36... | collective-permute-start | bytes 98312 | tf_op jit(solution)/shard_map/ppermute | solution.py:532
  25.5 8.3 %copy-start.2 = (bf16[256,256]{1,0:T(8,128)(2,1)S(1)}, bf16[256,256]{1,0:T(8,128)(2,1)}, u32[]{:S(2)}) copy-start(bf16[256,256]{1,0:T(8,128)(2,1)} %wm_ref.3) | copy-start | bytes 393220
  25.5 20.6 %all-to-all-start.1 = ((bf16[16,48,128]{2,1,0:T(8,128)(2,1)}), bf16[16,48,128]{2,1,0:T(8,128)(2,1)S(1)}, u32[]{:S(2)}, u32[]{:S(2)}) async-start(bf16[16,48,128]{2,1,0:T(8,128)(2,1)} %get-tuple-element.27), calls=%async_computation.1 | async-start | bytes 393216 | tf_op jit(solution)/shard_map/all_to_all | solution.py:476
  33.8 12.3 %copy-start.3 = (bf16[256,256]{1,0:T(8,128)(2,1)S(1)}, bf16[256,256]{1,0:T(8,128)(2,1)}, u32[]{:S(2)}) copy-start(bf16[256,256]{1,0:T(8,128)(2,1)} %wc_ref.1) | copy-start | bytes 393220
  33.8 12.3 %copy-start.8 = (bf16[20,256]{1,0:T(8,128)(2,1)S(1)}, bf16[20,256]{1,0:T(8,128)(2,1)}, u32[]{:S(2)}) copy-start(bf16[20,256]{1,0:T(8,128)(2,1)} %refs_4_.1) | copy-start | bytes 30724
  33.8 12.3 %copy-start.10 = (s32[3,512]{1,0:T(4,128)S(1)}, s32[3,512]{1,0:T(4,128)}, u32[]{:S(2)}) copy-start(s32[3,512]{1,0:T(4,128)} %refs_2_.1) | copy-start | bytes 18436

commit v7 on v6

--- a/solution.py
+++ b/solution.py
@@ -17,9 +17,9 @@
 f32 = jnp.float32
 
 SLOTS_OWN = 6
-ROWS_OWN = 4 * SLOTS_OWN
 LANES = 128
-PACK_ROWS = 2 * ROWS_OWN
+PACK_ROWS = 48
+BINS_ROWS = 24
 GRAD_CHUNKS = 32
 CHUNK_ROWS = 40
 
@@ -51,18 +51,33 @@
     return out
 
 
-def wave_rows(owners):
-    rows = np.zeros((owners * ROWS_OWN, 8), np.float32)
-    for owner in range(owners):
-        for place in range(ROWS_OWN):
-            v = owner * SLOTS_OWN + place % SLOTS_OWN + 1
-            nz = (v + 4) % 9 - 4
-            m = (v - nz) // 9
-            ny = (m + 4) % 9 - 4
-            nx = (m - ny) // 9
-            quarter = -0.25 if (place // SLOTS_OWN) % 2 else 0.0
-            rows[owner * ROWS_OWN + place, :4] = (nx, ny, nz, quarter)
-    return rows
+def wave_rows(size_y, size_z):
+    rows = np.zeros((size_y, size_z, 16, 8), np.float32)
+    for y in range(size_y):
+        for z in range(size_z):
+            for place in range(2 * SLOTS_OWN):
+                v = (y * size_z + z) * SLOTS_OWN + place % SLOTS_OWN + 1
+                nz = (v + 4) % 9 - 4
+                m = (v - nz) // 9
+                ny = (m + 4) % 9 - 4
+                nx = (m - ny) // 9
+                rows[y, z, place, :4] = (nx, ny, nz, -0.25 if place >= SLOTS_OWN else 0.0)
+    whole = rows[:, :, :8].reshape(size_y, 8 * size_z, 8)
+    halves = rows[:, :, 8:12].reshape(size_y, 4 * size_z, 8)
+    rows = np.concatenate([whole, halves], axis=1).reshape(-1, 8)
+    return np.concatenate([rows, rows, rows], axis=1)
+
+
+def turned(tiles):
+    return jnp.concatenate([tiles[..., 4:, :], tiles[..., :4, :]], axis=-2)
+
+
+def upper_rows(tiles):
+    return column_iota(tiles.shape, tiles.ndim - 2) < 4
+
+
+def lane_blocks(rows):
+    return [rows[..., i : i + LANES] for i in range(0, rows.shape[-1], LANES)]
 
 
 def packed(rows):
@@ -125,25 +140,29 @@
     channels = atoms_ref.shape[2]
     atoms = channels // 2
     total = table_ref.shape[0]
-    owners = total // ROWS_OWN
     rows = rows_ref[pl.ds(pl.multiple_of(place_ref[0] * total, 16), total), :]
-    sums = jnp.zeros((total, channels), f32)
-    first = column_iota((owners, ROWS_OWN, atoms), 1) < ROWS_OWN // 2
+    coords, values = [], []
     for peer in range(peers):
-        coords = atoms_ref[peer, 2 * atoms : 2 * atoms + 16, :].astype(f32)
-        high = coords[0:8, :atoms].astype(bf16)
-        middle = coords[0:8, atoms:].astype(bf16)
-        low = coords[8:16, :atoms].astype(bf16)
-        turns = dot(rows, high) + (dot(rows, middle) + dot(rows, low))
-        table = cosine_of_turns(turns).reshape(owners, ROWS_OWN, atoms)
-        nothing = jnp.zeros_like(table)
-        both = jnp.concatenate(
-            [jnp.where(first, table, nothing), jnp.where(first, nothing, table)], axis=-1
-        )
-        both = both.reshape(total, 2 * atoms).astype(bf16)
-        table_ref[:, 2 * atoms * peer : 2 * atoms * (peer + 1)] = both
-        sums = sums + dot(both, atoms_ref[peer, : 2 * atoms, :])
-    sums_ref[...] = packed(sums.reshape(owners, ROWS_OWN, channels)).astype(bf16)
+        block = atoms_ref[peer, 2 * atoms : 2 * atoms + 16, :].astype(f32)
+        thirds = [block[0:8, :atoms], block[0:8, atoms:], block[8:16, :atoms]]
+        coords.append(jnp.concatenate(thirds, axis=0))
+        features, cotangents = atoms_ref[peer, :atoms, :], atoms_ref[peer, atoms : 2 * atoms, :]
+        values.append(jnp.concatenate([features, cotangents], axis=1))
+    turns = dot(rows, jnp.concatenate(coords, axis=1).astype(bf16))
+    table = cosine_of_turns(turns).astype(bf16)
+    table_ref[...] = table
+    sums = dot(table, jnp.concatenate(values, axis=0))
+    owners = sums_ref.shape[0]
+    whole = sums[: 8 * owners].reshape(owners, 8, 2 * channels)
+    half = sums[8 * owners :].reshape(owners // 2, 8, 2 * channels)
+    half = list(zip(lane_blocks(half), lane_blocks(turned(half))))
+    parts = lane_blocks(whole)
+    for left, right in ((0, 1), (2, 3)):
+        upper = upper_rows(half[left][0])
+        even = jnp.where(upper, half[left][0], half[right][1])
+        odd = jnp.where(upper, half[left][1], half[right][0])
+        parts.append(jnp.stack([even, odd], axis=1).reshape(owners, 8, LANES))
+    sums_ref[...] = jnp.concatenate(parts, axis=1).astype(bf16)
 
 
 def paired(rows, j):
@@ -172,7 +191,7 @@
     bins = wf_ref.shape[0]
     table = ext_ref.shape[0]
     at_start = place_ref[0] == 0
-    bin_at = column_iota((ROWS_OWN, 2 * atoms), 0).astype(f32)
+    bin_at = column_iota((BINS_ROWS, 2 * atoms), 0).astype(f32)
     spacing = cutoff_radius / (bins - 1)
     wf = wf_ref[...]
     index = index_ref[...]
@@ -285,18 +304,29 @@
 
 def apply_kernel(place_ref, parts_ref, table_ref, back_ref, out_ref):
     peers, rows, lanes = out_ref.shape
-    total = table_ref.shape[0]
     parts = parts_ref[...].astype(f32)
-    weights = unpacked(parts[:, :PACK_ROWS]).reshape(total, 2 * lanes).astype(bf16)
+    owners = parts.shape[0]
+    whole = [parts[:, 8 * i : 8 * i + 8].reshape(8 * owners, lanes) for i in range(4)]
+    half = []
+    for i in (4, 5):
+        tiles = parts[:, 8 * i : 8 * i + 8].reshape(owners // 2, 2, 8, lanes)
+        even, odd = tiles[:, 0], tiles[:, 1]
+        upper = upper_rows(even)
+        half.append(jnp.where(upper, even, turned(odd)).reshape(4 * owners, lanes))
+        half.append(jnp.where(upper, turned(even), odd).reshape(4 * owners, lanes))
+    weights = jnp.concatenate(
+        [jnp.concatenate(whole, axis=1), jnp.concatenate(half, axis=1)], axis=0
+    ).astype(bf16)
     grads = jnp.sum(parts[:, PACK_ROWS:], axis=0).astype(bf16)
-    both = table_ref.shape[1] // peers
+    atoms = table_ref.shape[1] // peers
+    both = 2 * atoms
     back = back_ref[2 * (back_ref.shape[0] // 3) :]
     ghosts = back.shape[0] // 2
     lower, upper = packed(back[:ghosts]), packed(back[ghosts:])
     below = lax.rem(place_ref[0] + peers - 1, peers)
     for peer in range(peers):
-        piece = table_ref[:, both * peer : both * (peer + 1)]
-        out_ref[peer, : 2 * both, :] = packed(dot(piece, weights, TN)).astype(bf16)
+        piece = dot(table_ref[:, atoms * peer : atoms * (peer + 1)], weights, TN)
+        out_ref[peer, : 2 * both, :] = jnp.concatenate(lane_blocks(piece), axis=0).astype(bf16)
         chosen = jnp.where(below == peer, lower, upper).astype(bf16)
         out_ref[peer, 2 * both : 2 * both + 2 * ghosts, :] = chosen
         out_ref[peer, 2 * both + 2 * ghosts :, :] = grads
@@ -321,11 +351,6 @@
     spacing = kspace_limit / (bins - 1)
     scaled = (wave_vector_length(slot) - kspace_limit * bin_at / (bins - 1)) / spacing
     return jnp.where(bin_at < bins, jnp.exp(-0.5 * scaled * scaled), 0.0)
-
-
-def swapped_halves(rows):
-    half = rows.shape[0] // 2
-    return jnp.concatenate([rows[half:], rows[:half]], axis=0)
 
 
 def split_two(value):
@@ -346,7 +371,17 @@
     weights_ref,
 ):
     bins, channels = wk_ref.shape
-    sums = unpacked(total_of(sums_ref))
+    sums = total_of(sums_ref)
+    tiles = [sums[8 * i : 8 * i + 8] for i in range(6)]
+
+    def rows_of(left, right, half):
+        half = jnp.concatenate([half, turned(half)], axis=1)
+        half = jnp.where(upper_rows(half), half, 0.0)
+        return jnp.concatenate([jnp.concatenate([left, right], axis=1), half], axis=0)
+
+    features = rows_of(tiles[0], tiles[1], tiles[4])
+    cotangents = rows_of(tiles[2], tiles[3], tiles[5])
+    padded = features.shape[0]
     first_slot = (owner_ref[0] * SLOTS_OWN).astype(f32)
 
     def slot_of(shape, axis):
@@ -356,27 +391,26 @@
     waves = index_ref.shape[1]
     index = index_ref[...].astype(f32)
     codes = jnp.abs(81.0 * index[0:1] + 9.0 * index[1:2] + index[2:3])
-    same = jnp.where(slot_of((ROWS_OWN, waves), 0) + 1.0 == codes, 1.0, 0.0)
-    times = jnp.sum(same, axis=1, keepdims=True)
-    across = (ROWS_OWN, bins)
+    same = jnp.where(slot_of((padded, waves), 0) + 1.0 == codes, 1.0, 0.0)
+    times = jnp.sum(same, axis=1, keepdims=True) * scale
+    across = (padded, bins)
     basis = wave_basis(slot_of(across, 0), column_iota(across, 1).astype(f32), bins).astype(bf16)
-    wave_filter = dot(basis, wk_ref[...])
-    high, low = split_two(sums)
+    weighted = times * dot(basis, wk_ref[...])
+    high, low = split_two(features)
     factor = dot(high, wc_ref[...]) + dot(low, wc_ref[...])
-    first = column_iota((ROWS_OWN, channels), 0) < ROWS_OWN // 2
-    weights = (times * scale) * wave_filter * jnp.where(first, factor, sums)
-    weights = weights.astype(bf16)
-    weights_ref[...] = packed(weights.astype(f32)).astype(bf16)
-    filter_grad = jnp.where(first, (times * scale) * factor * swapped_halves(sums), 0.0)
-    down = (ROWS_OWN, ROWS_OWN)
+    pulled = (weighted * factor).astype(bf16).astype(f32)
+    pushed = (weighted * cotangents).astype(bf16).astype(f32)
+    parts = lane_blocks(pulled[:8]) + lane_blocks(pushed[:8])
+    for rows in (pulled, pushed):
+        left, right = lane_blocks(rows[8:])
+        parts.append(jnp.where(upper_rows(left), left, turned(right)))
+    weights_ref[...] = jnp.concatenate(parts, axis=0).astype(bf16)
+    down = (BINS_ROWS, padded)
     basis_down = wave_basis(slot_of(down, 1), column_iota(down, 0).astype(f32), bins)
     basis_down = basis_down.astype(bf16).astype(f32)
-    kspace = dot(basis_down, filter_grad, precision=lax.Precision.HIGHEST)
-    pushed = swapped_halves(weights.astype(f32)).astype(bf16)
-    none = jnp.zeros_like(sums)
-    high, low = split_two(jnp.where(first, sums, none))
+    kspace = dot(basis_down, times * factor * cotangents, precision=lax.Precision.HIGHEST)
+    pushed = pushed.astype(bf16)
     charge = dot(high, pushed, TN) + dot(low, pushed, TN)
-
     share = channels // GRAD_CHUNKS
     small = packed(jnp.concatenate([filter_ref[...], kspace], axis=0))
     spare = GRAD_CHUNKS * share - small.shape[0]
@@ -412,11 +446,12 @@
     ghosts = list_ref.shape[1]
     peers = parts_ref.shape[0]
     place = place_ref[0]
-    both = unpacked(total_of(parts_ref, slice(0, 4 * atoms)))
+    both = total_of(parts_ref, slice(0, 4 * atoms))
+    ewald, charge_grad = unpacked(both[: 2 * atoms]), unpacked(both[2 * atoms :])
     live = column_iota((atoms, channels), 0) < count_ref[0, 0]
-    added = jnp.where(live, messages_ref[...] + both[:atoms], 0.0)
+    added = jnp.where(live, messages_ref[...] + ewald, 0.0)
     updated_ref[...] = (feat_ref[...].astype(f32) + added).astype(bf16)
-    charge_grad = jnp.where(live, both[atoms:], 0.0).astype(bf16)
+    charge_grad = jnp.where(live, charge_grad, 0.0).astype(bf16)
     wrapped = wrap_ref[ghosts:].astype(f32)
     lists = list_ref[...]
     act_grad = ext_ref[:atoms]
@@ -438,10 +473,10 @@
     grads = grads_ref[...].astype(f32)
     message_ref[...] = unpacked(grads[:, 0:16]).reshape(channels, channels)
     charge_ref[...] = unpacked(grads[:, 16:32]).reshape(channels, channels)
-    small = unpacked(grads[: 4 * ROWS_OWN // 8, 32:40].reshape(4 * ROWS_OWN, LANES))
+    small = unpacked(grads[: 4 * BINS_ROWS // 8, 32:40].reshape(4 * BINS_ROWS, LANES))
     bins = filter_ref.shape[0]
     filter_ref[...] = small[:bins]
-    kspace_ref[...] = small[ROWS_OWN : ROWS_OWN + bins]
+    kspace_ref[...] = small[BINS_ROWS : BINS_ROWS + bins]
 
 
 def on_core(kernel, out_shape, in_smem, n_in, scratch=(), streamed=False):
@@ -520,7 +555,7 @@
         push_kernel,
         [
             shape((table_rows, channels), f32),
-            shape((ROWS_OWN, edges), bf16),
+            shape((BINS_ROWS, edges), bf16),
             shape((2 * ghosts, channels), bf16),
         ],
         2,
@@ -532,13 +567,13 @@
     wrap = lax.ppermute(wrap, space, ends)
     shared = exchanged(shared, "y")
 
-    total = size_z * ROWS_OWN
+    total = 2 * SLOTS_OWN * size_z
     table, sums = on_core(
         wave_kernel,
-        [shape((total, size_y * 2 * atoms), bf16), shape((size_z, PACK_ROWS, LANES), bf16)],
+        [shape((total, size_y * atoms), bf16), shape((size_z, PACK_ROWS, LANES), bf16)],
         1,
         3,
-    )(here, shared, jnp.asarray(wave_rows(domains), bf16))
+    )(here, shared, jnp.asarray(wave_rows(size_y, size_z), bf16))
     sums, wrap = lax.optimization_barrier((sums, wrap))
     sums = exchanged(sums, "z")
 
@@ -548,7 +583,7 @@
             shape((atoms, channels), f32),
             shape((atoms, channels), f32),
             shape((channels, channels), f32),
-            shape((ROWS_OWN, channels), f32),
+            shape((BINS_ROWS, channels), f32),
         ],
         1,
         9,

time: 117 us -> 117 us (level)
  transfers between devices with their start and end apart: 3 -> 3, of which waited for: 1 -> 2; matrix products, arithmetic and copies ran while one was open for 0% -> 0% of each run, Pallas kernels for 4% -> 4%
where the time goes in v7:
time: 117 us
  blocking collectives  68.6 us (59%)
  starting transfers between devices  27.2 us (23%)
  waiting for transfers between devices  10.1 us (9%)
  Pallas kernels  8.61 us (7%)
  between operations  1.44 us (1%)
    all_to_all x4, blocking collectives, exchanged(): return lax.all_to_all(value, axis, 0, 0, tiled=True)  68.6 us
    all_to_all x2, starting transfers between devices, exchanged(): return lax.all_to_all(value, axis, 0, 0, tiled=True)  13.7 us
    ppermute x1, starting transfers between devices, body(): wrap = lax.ppermute(wrap, space, ends)  13.5 us
    all_to_all x2, waiting for transfers between devices, exchanged(): return lax.all_to_all(value, axis, 0, 0, tiled=True)  10 us
  transfers between devices with their start and end apart: 3, of which 2 were waited for; matrix products, arithmetic and copies ran while one was open for 0% of the time, Pallas kernels for 4%

profile of v7, /device:TPU:1, one launch (start us, length us, event | category | flops | bytes accessed | tf_op | source)
XLA Modules:
  0.0 116.6 jit_solution(3884587060547842043)
XLA Ops:
  1.3 1.8 %shard_map.181 = bf16[4,272,256]{2,1,0:T(8,128)(2,1)} custom-call(s32[1,1]{1,0:T(1,128)S(6)} %copy.20.count_ref, bf16[128,256]{1,0:T(8,128)(2,1)} %bitcast.16, bf16[128,256]{1,0:T(8,128)(2,1)} %bitcast.20, f32[3,1,128]{2,1,0:T(1,128)} %bitcast.29, s32[2,32]{1,0:T(2,128)} %bitcast.26), custom_call_target="tpu_custom_call" | custom-call | tf_op jit(solution)/shard_map/pallas_call | solution.py:486
  3.0 0.0 copy-start
  3.0 0.0 copy-start.1
  3.0 0.0 copy-start.5
  3.0 0.0 copy-start.6
  3.0 0.0 copy-start.7
  3.1 0.0 copy-start.4
  3.1 5.2 %all-to-all-start = ((bf16[4,272,256]{2,1,0:T(8,128)(2,1)}), bf16[4,272,256]{2,1,0:T(8,128)(2,1)S(1)}, u32[]{:S(2)}, u32[]{:S(2)}) async-start(bf16[4,272,256]{2,1,0:T(8,128)(2,1)} %shard_map.181), calls=%async_computation | async-start | bytes 1114112 | tf_op jit(solution)/shard_map/all_to_all | solution.py:511
  8.2 0.0 copy-start.9
  8.2 0.0 copy-start.11
  8.2 0.0 copy-done
  8.2 0.0 copy-done.1
  8.2 0.0 copy-done.5
  8.3 0.0 copy-done.6
  8.3 0.0 copy-done.7
  8.3 0.6 copy-done.9
  8.9 0.0 copy-done.11
  8.9 1.5 %shard_map.183 = (f32[192,256]{1,0:T(8,128)S(1)}, bf16[24,4096]{1,0:T(8,128)(2,1)S(1)}, bf16[64,256]{1,0:T(8,128)(2,1)S(1)}) custom-call(s32[1,1]{1,0:T(1,128)S(6)} %copy.20.count_ref, s32[1]{0:T(128)} %bitcast.place_ref, bf16[128,256]{1,0:T(8,128)(2,1)S(1)} %bitcast.17, s32[2,32]{1,0:T(2,128)S(1)} %bitcast.27, s32[32,128]{1,0:T(8,128)S(1)} %bitcast.23, ...), custom_call_target="tpu_custom_call" | custom-call | tf_op jit(solution)/shard_map/pallas_call | solution.py:554
  10.4 13.5 %collective-permute-start = (bf16[64,256]{1,0:T(8,128)(2,1)S(1)}, bf16[64,256]{1,0:T(8,128)(2,1)S(1)}, u32[]{:S(2)}, u32[]{:S(2)}) collective-permute-start(bf16[64,256]{1,0:T(8,128)(2,1)S(1)} %get-tuple-element.26), channel_id=1, source_target_pairs={{3,4},{7,8},{11,12},{15,16},{19,20},{23,24},{27,28},{31,32},{35,36... | collective-permute-start | bytes 98312 | tf_op jit(solution)/shard_map/ppermute | solution.py:567
  23.9 0.0 all-to-all-done.atoms_ref.shared_ref
  23.9 0.0 copy-done.4
  23.9 1.2 %shard_map.182 = (bf16[192,512]{1,0:T(8,128)(2,1)S(1)}, bf16[16,48,128]{2,1,0:T(8,128)(2,1)}) custom-call(s32[1]{0:T(128)} %bitcast.place_ref, bf16[4,272,256]{2,1,0:T(8,128)(2,1)S(1)} %all-to-all-done.atoms_ref.shared_ref, bf16[768,24]{1,0:T(8,128)(2,1)S(1)} %copy-done.4), custom_call_target="tpu_custom_call" | custom-call | tf_op jit(solution)/shard_map/pallas_call | solution.py:571
  25.1 0.1 collective-permute-done.wrap_ref
  25.2 0.0 copy-start.2
  25.2 8.5 %all-to-all-start.1 = ((bf16[16,48,128]{2,1,0:T(8,128)(2,1)}), bf16[16,48,128]{2,1,0:T(8,128)(2,1)S(1)}, u32[]{:S(2)}, u32[]{:S(2)}) async-start(bf16[16,48,128]{2,1,0:T(8,128)(2,1)} %get-tuple-element.27), calls=%async_computation.1 | async-start | bytes 393216 | tf_op jit(solution)/shard_map/all_to_all | solution.py:511
  33.7 0.0 copy-done.2
  33.7 0.0 copy-start.3
  33.8 0.0 copy-start.8
  33.8 0.0 copy-start.10
  33.8 2.2 %shard_map.184 = (f32[128,256]{1,0:T(8,128)S(1)}, f32[128,256]{1,0:T(8,128)S(1)}, f32[256,256]{1,0:T(8,128)S(1)}, f32[24,256]{1,0:T(8,128)S(1)}) custom-call(s32[1]{0:T(128)} %bitcast.place_ref, bf16[128,256]{1,0:T(8,128)(2,1)S(1)} %bitcast.18, bf16[64,256]{1,0:T(8,128)(2,1)S(1)} %collective-permute-done.wrap_ref, ...), custom_call_target="tpu_custom_call" | custom-call | tf_op jit(solution)/shard_map/pallas_call | solution.py:580
  36.0 10.0 %all-to-all-done.1.refs_1_ = bf16[16,48,128]{2,1,0:T(8,128)(2,1)S(1)} async-done(((bf16[16,48,128]{2,1,0:T(8,128)(2,1)}), bf16[16,48,128]{2,1,0:T(8,128)(2,1)S(1)}, u32[]{:S(2)}, u32[]{:S(2)}) %all-to-all-start.1) | async-done | bytes 196640 | tf_op jit(solution)/shard_map/all_to_all | solution.py:511
  46.1 0.0 copy-done.3
  46.1 0.0 copy-done.8
  46.1 0.0 copy-done.10
  46.1 0.4 shard_map.185
  46.5 20.2 %all_to_all.30.parts_ref = bf16[32,40,128]{2,1,0:T(8,128)(2,1)S(1)} all-to-all(bf16[32,40,128]{2,1,0:T(8,128)(2,1)S(1)} %get-tuple-element.33), channel_id=1, replica_groups=mesh['x'=4,'core'=2,'z'=16,'y'=4] {'x','core','y'}, dimensions={0} | all-to-all | bytes 655360 | tf_op jit(solution)/shard_map/all_to_all | solution.py:511
  66.7 0.1 shard_map.186
  66.8 19.7 %all_to_all.31.parts_ref = bf16[16,88,128]{2,1,0:T(8,128)(2,1)S(1)} all-to-all(bf16[16,88,128]{2,1,0:T(8,128)(2,1)S(1)} %shard_map.186), channel_id=1, replica_groups=mesh['x'=4,'core'=2,'z'=16,'y'=4] {'z'}, dimensions={0} | all-to-all | bytes 720896 | tf_op jit(solution)/shard_map/all_to_all | solution.py:511
  86.5 0.3 shard_map.187
  86.9 12.6 %all_to_all.32.parts_ref = bf16[4,616,128]{2,1,0:T(8,128)(2,1)S(1)} all-to-all(bf16[4,616,128]{2,1,0:T(8,128)(2,1)S(1)} %shard_map.187), channel_id=1, replica_groups=mesh['x'=4,'core'=2,'z'=16,'y'=4] {'y'}, dimensions={0} | all-to-all | bytes 1261568 | tf_op jit(solution)/shard_map/all_to_all | solution.py:511
  99.5 16.1 %all_to_all.33 = bf16[8,4,40,128]{3,2,1,0:T(8,128)(2,1)S(1)} all-to-all(bf16[8,4,40,128]{3,2,1,0:T(8,128)(2,1)S(1)} %shard_map.188), channel_id=1, replica_groups=mesh['x'=4,'core'=2,'z'=16,'y'=4] {'x','core'}, dimensions={0} | all-to-all | bytes 655360 | tf_op jit(solution)/shard_map/all_to_all | solution.py:511
  115.6 1.1 shard_map.189
  (1 shorter events, 0.0 us)
Async XLA Ops:
  3.0 5.2 %copy-start = (bf16[1,128,256]{2,1,0:T(8,128)(2,1)S(1)}, bf16[1,128,256]{2,1,0:T(8,128)(2,1)}, u32[]{:S(2)}) copy-start(bf16[1,128,256]{2,1,0:T(8,128)(2,1)} %param.14) | copy-start | bytes 196612
  3.0 5.2 %copy-start.1 = (bf16[1,128,256]{2,1,0:T(8,128)(2,1)S(1)}, bf16[1,128,256]{2,1,0:T(8,128)(2,1)}, u32[]{:S(2)}) copy-start(bf16[1,128,256]{2,1,0:T(8,128)(2,1)} %param.26) | copy-start | bytes 196612
  3.0 5.2 %copy-start.5 = (s32[1,128,32]{1,2,0:T(8,128)S(1)}, s32[1,128,32]{1,2,0:T(8,128)}, u32[]{:S(2)}) copy-start(s32[1,128,32]{1,2,0:T(8,128)} %param.17) | copy-start | bytes 49156
  3.0 5.2 %copy-start.6 = (bf16[20,256]{1,0:T(8,128)(2,1)S(1)}, bf16[20,256]{1,0:T(8,128)(2,1)}, u32[]{:S(2)}) copy-start(bf16[20,256]{1,0:T(8,128)(2,1)} %wf_ref.3) | copy-start | bytes 30724
  3.0 5.2 %copy-start.7 = (f32[1,128,32]{1,2,0:T(8,128)S(1)}, f32[1,128,32]{1,2,0:T(8,128)}, u32[]{:S(2)}) copy-start(f32[1,128,32]{1,2,0:T(8,128)} %param.20) | copy-start | bytes 49156
  3.1 20.9 %copy-start.4 = (bf16[768,24]{1,0:T(8,128)(2,1)S(1)}, bf16[768,24]{1,0:T(8,128)(2,1)}, u32[]{:S(2)}) copy-start(bf16[768,24]{1,0:T(8,128)(2,1)} %constant.13.clone.rows_ref) | copy-start | bytes 110596
  3.1 20.8 %all-to-all-start = ((bf16[4,272,256]{2,1,0:T(8,128)(2,1)}), bf16[4,272,256]{2,1,0:T(8,128)(2,1)S(1)}, u32[]{:S(2)}, u32[]{:S(2)}) async-start(bf16[4,272,256]{2,1,0:T(8,128)(2,1)} %shard_map.181), calls=%async_computation | async-start | bytes 1114112 | tf_op jit(solution)/shard_map/all_to_all | solution.py:511
  8.2 0.7 copy-start.9
  8.2 0.7 copy-start.11
  10.4 14.8 %collective-permute-start = (bf16[64,256]{1,0:T(8,128)(2,1)S(1)}, bf16[64,256]{1,0:T(8,128)(2,1)S(1)}, u32[]{:S(2)}, u32[]{:S(2)}) collective-permute-start(bf16[64,256]{1,0:T(8,128)(2,1)S(1)} %get-tuple-element.26), channel_id=1, source_target_pairs={{3,4},{7,8},{11,12},{15,16},{19,20},{23,24},{27,28},{31,32},{35,36... | collective-permute-start | bytes 98312 | tf_op jit(solution)/shard_map/ppermute | solution.py:567
  25.2 8.5 %copy-start.2 = (bf16[256,256]{1,0:T(8,128)(2,1)S(1)}, bf16[256,256]{1,0:T(8,128)(2,1)}, u32[]{:S(2)}) copy-start(bf16[256,256]{1,0:T(8,128)(2,1)} %wm_ref.3) | copy-start | bytes 393220
  25.2 20.9 %all-to-all-start.1 = ((bf16[16,48,128]{2,1,0:T(8,128)(2,1)}), bf16[16,48,128]{2,1,0:T(8,128)(2,1)S(1)}, u32[]{:S(2)}, u32[]{:S(2)}) async-start(bf16[16,48,128]{2,1,0:T(8,128)(2,1)} %get-tuple-element.27), calls=%async_computation.1 | async-start | bytes 393216 | tf_op jit(solution)/shard_map/all_to_all | solution.py:511
  33.7 12.3 %copy-start.3 = (bf16[256,256]{1,0:T(8,128)(2,1)S(1)}, bf16[256,256]{1,0:T(8,128)(2,1)}, u32[]{:S(2)}) copy-start(bf16[256,256]{1,0:T(8,128)(2,1)} %wc_ref.1) | copy-start | bytes 393220
  33.8 12.3 %copy-start.8 = (bf16[20,256]{1,0:T(8,128)(2,1)S(1)}, bf16[20,256]{1,0:T(8,128)(2,1)}, u32[]{:S(2)}) copy-start(bf16[20,256]{1,0:T(8,128)(2,1)} %refs_4_.1) | copy-start | bytes 30724
  33.8 12.3 %copy-start.10 = (s32[3,512]{1,0:T(4,128)S(1)}, s32[3,512]{1,0:T(4,128)}, u32[]{:S(2)}) copy-start(s32[3,512]{1,0:T(4,128)} %refs_2_.1) | copy-start | bytes 18436

commit v8 on v7

--- a/solution.py
+++ b/solution.py
@@ -222,7 +222,9 @@
 
 
 def edge_kernel(
+    scale,
     place_ref,
+    owner_ref,
     feat_ref,
     wrap_ref,
     shared_ref,
@@ -231,13 +233,22 @@
     basis_ref,
     wf_ref,
     ext_ref,
+    wave_ref,
+    wk_ref,
+    table_ref,
     messages_ref,
     slope_ref,
     message_ref,
     filter_ref,
+    weighted_ref,
+    times_ref,
+    down_ref,
+    turned_ref,
     grad_s,
     near_s,
 ):
+    wave_terms(scale, owner_ref, wave_ref, wk_ref, weighted_ref, times_ref, down_ref)
+    turned_ref[...] = table_ref[...].astype(f32).T.astype(bf16)
     atoms, channels = feat_ref.shape
     slots = index_ref.shape[0]
     ghosts = wrap_ref.shape[0] // 2
@@ -271,7 +282,8 @@
     ext_t = (hidden * sigma).T.astype(bf16)
     slope = sigma * (1.0 + hidden * (1.0 - sigma))
     slope_ref[...] = slope[:atoms]
-    message_ref[...] = dot(feat, (ext_ref[...] * slope).astype(bf16), TN)
+    message = packed(dot(feat, (ext_ref[...] * slope).astype(bf16), TN).reshape(GRAD_CHUNKS, 8, -1))
+    message_ref[...] = message.astype(bf16)
     wf = wf_ref[...]
     index = index_ref[...]
     cot = shared_ref[place, atoms : 2 * atoms, :].astype(f32).T
@@ -318,14 +330,14 @@
         [jnp.concatenate(whole, axis=1), jnp.concatenate(half, axis=1)], axis=0
     ).astype(bf16)
     grads = jnp.sum(parts[:, PACK_ROWS:], axis=0).astype(bf16)
-    atoms = table_ref.shape[1] // peers
+    atoms = table_ref.shape[0] // peers
     both = 2 * atoms
     back = back_ref[2 * (back_ref.shape[0] // 3) :]
     ghosts = back.shape[0] // 2
     lower, upper = packed(back[:ghosts]), packed(back[ghosts:])
     below = lax.rem(place_ref[0] + peers - 1, peers)
     for peer in range(peers):
-        piece = dot(table_ref[:, atoms * peer : atoms * (peer + 1)], weights, TN)
+        piece = dot(table_ref[atoms * peer : atoms * (peer + 1), :], weights)
         out_ref[peer, : 2 * both, :] = jnp.concatenate(lane_blocks(piece), axis=0).astype(bf16)
         chosen = jnp.where(below == peer, lower, upper).astype(bf16)
         out_ref[peer, 2 * both : 2 * both + 2 * ghosts, :] = chosen
@@ -358,30 +370,9 @@
     return high, (value - high.astype(f32)).astype(bf16)
 
 
-def middle_kernel(
-    scale,
-    owner_ref,
-    sums_ref,
-    index_ref,
-    wc_ref,
-    wk_ref,
-    message_ref,
-    filter_ref,
-    grads_ref,
-    weights_ref,
-):
-    bins, channels = wk_ref.shape
-    sums = total_of(sums_ref)
-    tiles = [sums[8 * i : 8 * i + 8] for i in range(6)]
-
-    def rows_of(left, right, half):
-        half = jnp.concatenate([half, turned(half)], axis=1)
-        half = jnp.where(upper_rows(half), half, 0.0)
-        return jnp.concatenate([jnp.concatenate([left, right], axis=1), half], axis=0)
-
-    features = rows_of(tiles[0], tiles[1], tiles[4])
-    cotangents = rows_of(tiles[2], tiles[3], tiles[5])
-    padded = features.shape[0]
+def wave_terms(scale, owner_ref, index_ref, wk_ref, weighted_ref, times_ref, down_ref):
+    bins = wk_ref.shape[0]
+    padded = weighted_ref.shape[0]
     first_slot = (owner_ref[0] * SLOTS_OWN).astype(f32)
 
     def slot_of(shape, axis):
@@ -395,7 +386,36 @@
     times = jnp.sum(same, axis=1, keepdims=True) * scale
     across = (padded, bins)
     basis = wave_basis(slot_of(across, 0), column_iota(across, 1).astype(f32), bins).astype(bf16)
-    weighted = times * dot(basis, wk_ref[...])
+    weighted_ref[...] = times * dot(basis, wk_ref[...])
+    times_ref[...] = jnp.broadcast_to(times, times_ref.shape)
+    down = down_ref.shape
+    basis_down = wave_basis(slot_of(down, 1), column_iota(down, 0).astype(f32), bins)
+    down_ref[...] = basis_down.astype(bf16).astype(f32)
+
+
+def middle_kernel(
+    sums_ref,
+    wc_ref,
+    weighted_ref,
+    times_ref,
+    down_ref,
+    message_ref,
+    filter_ref,
+    grads_ref,
+    weights_ref,
+):
+    channels = wc_ref.shape[0]
+    weighted = weighted_ref[...]
+    sums = total_of(sums_ref)
+    tiles = [sums[8 * i : 8 * i + 8] for i in range(6)]
+
+    def rows_of(left, right, half):
+        half = jnp.concatenate([half, turned(half)], axis=1)
+        half = jnp.where(upper_rows(half), half, 0.0)
+        return jnp.concatenate([jnp.concatenate([left, right], axis=1), half], axis=0)
+
+    features = rows_of(tiles[0], tiles[1], tiles[4])
+    cotangents = rows_of(tiles[2], tiles[3], tiles[5])
     high, low = split_two(features)
     factor = dot(high, wc_ref[...]) + dot(low, wc_ref[...])
     pulled = (weighted * factor).astype(bf16).astype(f32)
@@ -405,10 +425,9 @@
         left, right = lane_blocks(rows[8:])
         parts.append(jnp.where(upper_rows(left), left, turned(right)))
     weights_ref[...] = jnp.concatenate(parts, axis=0).astype(bf16)
-    down = (BINS_ROWS, padded)
-    basis_down = wave_basis(slot_of(down, 1), column_iota(down, 0).astype(f32), bins)
-    basis_down = basis_down.astype(bf16).astype(f32)
-    kspace = dot(basis_down, times * factor * cotangents, precision=lax.Precision.HIGHEST)
+    kspace = dot(
+        down_ref[...], times_ref[...] * factor * cotangents, precision=lax.Precision.HIGHEST
+    )
     pushed = pushed.astype(bf16)
     charge = dot(high, pushed, TN) + dot(low, pushed, TN)
     share = channels // GRAD_CHUNKS
@@ -416,7 +435,7 @@
     spare = GRAD_CHUNKS * share - small.shape[0]
     small = jnp.concatenate([small, jnp.zeros((spare, LANES), f32)], axis=0)
     grads = [
-        packed(message_ref[...].reshape(GRAD_CHUNKS, share, channels)),
+        message_ref[...].astype(f32),
         packed(charge.reshape(GRAD_CHUNKS, share, channels)),
         small.reshape(GRAD_CHUNKS, share, LANES),
     ]
@@ -577,33 +596,51 @@
     sums, wrap = lax.optimization_barrier((sums, wrap))
     sums = exchanged(sums, "z")
 
-    messages, slope, message_term, filter_term = on_core(
-        edge_kernel,
+    owner = (place_y * size_z + place_z).reshape(1).astype(jnp.int32)
+    messages, slope, message_term, filter_term, weighted, times, down, turned_table = on_core(
+        lambda *refs: edge_kernel(scale, *refs),
         [
             shape((atoms, channels), f32),
             shape((atoms, channels), f32),
-            shape((channels, channels), f32),
+            shape((GRAD_CHUNKS, 16, LANES), bf16),
             shape((BINS_ROWS, channels), f32),
+            shape((16, channels), f32),
+            shape((16, channels), f32),
+            shape((BINS_ROWS, 16), f32),
+            shape((size_y * atoms, total), bf16),
         ],
-        1,
-        9,
+        2,
+        13,
         [pltpu.VMEM((channels, edges), bf16), pltpu.VMEM((2 * ghosts, channels), bf16)],
-    )(here, feat, wrap, shared, w_message, index, basis, w_filter, ext_grad)
-    owner = place_y * size_z + place_z
+    )(
+        here,
+        owner,
+        feat,
+        wrap,
+        shared,
+        w_message,
+        index,
+        basis,
+        w_filter,
+        ext_grad,
+        wave_index,
+        w_kspace,
+        table,
+    )
     grads, weights = on_core(
-        lambda *refs: middle_kernel(scale, *refs),
+        middle_kernel,
         [
             shape((GRAD_CHUNKS, CHUNK_ROWS, LANES), bf16),
             shape((PACK_ROWS, LANES), bf16),
         ],
-        1,
+        0,
         7,
     )(
-        owner.reshape(1).astype(jnp.int32),
         sums,
-        wave_index,
         w_charge,
-        w_kspace,
+        weighted,
+        times,
+        down,
         message_term,
         filter_term,
     )
@@ -613,7 +650,7 @@
     parts = exchanged(parts, "z")
     rows = 4 * atoms + 2 * ghosts + CHUNK_ROWS
     parts = on_core(apply_kernel, [shape((size_y, rows, LANES), bf16)], 1, 4)(
-        here, parts, table, ext_grad
+        here, parts, turned_table, ext_grad
     )[0]
     parts = exchanged(parts, "y")
     slabs = lax.axis_size("x") * lax.axis_size("core")

time: 117 us -> 117 us (level)
  no operation moved by 1% of the time
where the time goes in v8:
time: 117 us
  blocking collectives  68.6 us (59%)
  starting transfers between devices  27.2 us (23%)
  waiting for transfers between devices  9.29 us (8%)
  Pallas kernels  8.76 us (7%)
  between operations  1.43 us (1%)
  local copies, waits for them, and re-layouts  1.35 us (1%)
    all_to_all x4, blocking collectives, exchanged(): return lax.all_to_all(value, axis, 0, 0, tiled=True)  68.6 us
    all_to_all x2, starting transfers between devices, exchanged(): return lax.all_to_all(value, axis, 0, 0, tiled=True)  13.7 us
    ppermute x1, starting transfers between devices, body(): wrap = lax.ppermute(wrap, space, ends)  13.5 us
    all_to_all x2, waiting for transfers between devices, exchanged(): return lax.all_to_all(value, axis, 0, 0, tiled=True)  9.21 us
    pallas_call x1, Pallas kernels, body(): on_core(lambda *refs: edge_kernel(scale, *refs), [shape((atoms, channels)...  2.41 us
  transfers between devices with their start and end apart: 3, of which 2 were waited for; matrix products, arithmetic and copies ran while one was open for 0% of the time, Pallas kernels for 4%

profile of v8, /device:TPU:1, one launch (start us, length us, event | category | flops | bytes accessed | tf_op | source)
XLA Modules:
  0.0 116.6 jit_solution(108981070938007179)
XLA Ops:
  1.3 1.8 %shard_map.181 = bf16[4,272,256]{2,1,0:T(8,128)(2,1)} custom-call(s32[1,1]{1,0:T(1,128)S(6)} %copy.20.count_ref, bf16[128,256]{1,0:T(8,128)(2,1)} %bitcast.16, bf16[128,256]{1,0:T(8,128)(2,1)} %bitcast.20, f32[3,1,128]{2,1,0:T(1,128)} %bitcast.29, s32[2,32]{1,0:T(2,128)} %bitcast.26), custom_call_target="tpu_custom_call" | custom-call | tf_op jit(solution)/shard_map/pallas_call | solution.py:505
  3.0 0.0 copy-start
  3.0 0.0 copy-start.1
  3.0 0.0 copy-start.5
  3.0 0.0 copy-start.6
  3.0 0.0 copy-start.7
  3.1 0.0 copy-start.4
  3.1 5.2 %all-to-all-start = ((bf16[4,272,256]{2,1,0:T(8,128)(2,1)}), bf16[4,272,256]{2,1,0:T(8,128)(2,1)S(1)}, u32[]{:S(2)}, u32[]{:S(2)}) async-start(bf16[4,272,256]{2,1,0:T(8,128)(2,1)} %shard_map.181), calls=%async_computation | async-start | bytes 1114112 | tf_op jit(solution)/shard_map/all_to_all | solution.py:530
  8.2 0.0 copy-start.9
  8.2 0.0 copy-start.11
  8.2 0.0 copy-done
  8.2 0.0 copy-done.1
  8.2 0.0 copy-done.5
  8.3 0.0 copy-done.6
  8.3 0.0 copy-done.7
  8.3 0.6 copy-done.9
  8.9 0.0 copy-done.11
  8.9 1.5 %shard_map.183 = (f32[192,256]{1,0:T(8,128)S(1)}, bf16[24,4096]{1,0:T(8,128)(2,1)S(1)}, bf16[64,256]{1,0:T(8,128)(2,1)S(1)}) custom-call(s32[1,1]{1,0:T(1,128)S(6)} %copy.20.count_ref, s32[1]{0:T(128)} %bitcast.place_ref.refs_0_, bf16[128,256]{1,0:T(8,128)(2,1)S(1)} %bitcast.17, s32[2,32]{1,0:T(2,128)S(1)} %bitcast.27, s32[32,128]{1,0:T(8,128)S(1)} %bitcast.23, ...), custom_call_target="tpu_custom_call" | custom-call | tf_op jit(solution)/shard_map/pallas_call | solution.py:573
  10.4 13.5 %collective-permute-start = (bf16[64,256]{1,0:T(8,128)(2,1)S(1)}, bf16[64,256]{1,0:T(8,128)(2,1)S(1)}, u32[]{:S(2)}, u32[]{:S(2)}) collective-permute-start(bf16[64,256]{1,0:T(8,128)(2,1)S(1)} %get-tuple-element.30), channel_id=1, source_target_pairs={{3,4},{7,8},{11,12},{15,16},{19,20},{23,24},{27,28},{31,32},{35,36... | collective-permute-start | bytes 98312 | tf_op jit(solution)/shard_map/ppermute | solution.py:586
  23.9 0.0 all-to-all-done.atoms_ref.refs_4_
  23.9 0.0 copy-done.4
  23.9 1.2 %shard_map.182 = (bf16[192,512]{1,0:T(8,128)(2,1)S(1)}, bf16[16,48,128]{2,1,0:T(8,128)(2,1)}) custom-call(s32[1]{0:T(128)} %bitcast.place_ref.refs_0_, bf16[4,272,256]{2,1,0:T(8,128)(2,1)S(1)} %all-to-all-done.atoms_ref.refs_4_, bf16[768,24]{1,0:T(8,128)(2,1)S(1)} %copy-done.4), custom_call_target="tpu_custom_call" | custom-call | tf_op jit(solution)/shard_map/pallas_call | solution.py:590
  25.1 0.1 collective-permute-done.refs_3_.wrap_ref
  25.2 0.0 copy-start.2
  25.2 0.0 copy-start.10
  25.2 8.5 %all-to-all-start.1 = ((bf16[16,48,128]{2,1,0:T(8,128)(2,1)}), bf16[16,48,128]{2,1,0:T(8,128)(2,1)S(1)}, u32[]{:S(2)}, u32[]{:S(2)}) async-start(bf16[16,48,128]{2,1,0:T(8,128)(2,1)} %get-tuple-element.31), calls=%async_computation.1 | async-start | bytes 393216 | tf_op jit(solution)/shard_map/all_to_all | solution.py:530
  33.7 0.0 copy-start.8
  33.7 0.0 copy-done.2
  33.8 0.0 copy-done.10
  33.8 0.7 copy-done.8
  34.4 0.0 copy-start.3
  34.4 2.4 %shard_map.184 = (f32[128,256]{1,0:T(8,128)S(1)}, f32[128,256]{1,0:T(8,128)S(1)}, bf16[32,16,128]{2,1,0:T(8,128)(2,1)S(1)}, f32[24,256]{1,0:T(8,128)S(1)}, f32[1...) custom-call(s32[1]{0:T(128)} %bitcast.place_ref.refs_0_, ...), custom_call_target="tpu_custom_call" | custom-call | tf_op jit(solution)/shard_map/pallas_call | solution.py:600
  36.9 9.2 %all-to-all-done.1.sums_ref = bf16[16,48,128]{2,1,0:T(8,128)(2,1)S(1)} async-done(((bf16[16,48,128]{2,1,0:T(8,128)(2,1)}), bf16[16,48,128]{2,1,0:T(8,128)(2,1)S(1)}, u32[]{:S(2)}, u32[]{:S(2)}) %all-to-all-start.1) | async-done | bytes 196640 | tf_op jit(solution)/shard_map/all_to_all | solution.py:530
  46.1 0.0 copy-done.3
  46.1 0.4 shard_map.185
  46.5 20.2 %all_to_all.30.parts_ref = bf16[32,40,128]{2,1,0:T(8,128)(2,1)S(1)} all-to-all(bf16[32,40,128]{2,1,0:T(8,128)(2,1)S(1)} %get-tuple-element.41), channel_id=1, replica_groups=mesh['x'=4,'core'=2,'z'=16,'y'=4] {'x','core','y'}, dimensions={0} | all-to-all | bytes 655360 | tf_op jit(solution)/shard_map/all_to_all | solution.py:530
  66.7 0.1 shard_map.186
  66.8 19.7 %all_to_all.31.parts_ref = bf16[16,88,128]{2,1,0:T(8,128)(2,1)S(1)} all-to-all(bf16[16,88,128]{2,1,0:T(8,128)(2,1)S(1)} %shard_map.186), channel_id=1, replica_groups=mesh['x'=4,'core'=2,'z'=16,'y'=4] {'z'}, dimensions={0} | all-to-all | bytes 720896 | tf_op jit(solution)/shard_map/all_to_all | solution.py:530
  86.5 0.3 shard_map.187
  86.8 12.6 %all_to_all.32.parts_ref = bf16[4,616,128]{2,1,0:T(8,128)(2,1)S(1)} all-to-all(bf16[4,616,128]{2,1,0:T(8,128)(2,1)S(1)} %shard_map.187), channel_id=1, replica_groups=mesh['x'=4,'core'=2,'z'=16,'y'=4] {'y'}, dimensions={0} | all-to-all | bytes 1261568 | tf_op jit(solution)/shard_map/all_to_all | solution.py:530
  99.5 16.1 %all_to_all.33 = bf16[8,4,40,128]{3,2,1,0:T(8,128)(2,1)S(1)} all-to-all(bf16[8,4,40,128]{3,2,1,0:T(8,128)(2,1)S(1)} %shard_map.188), channel_id=1, replica_groups=mesh['x'=4,'core'=2,'z'=16,'y'=4] {'x','core'}, dimensions={0} | all-to-all | bytes 655360 | tf_op jit(solution)/shard_map/all_to_all | solution.py:530
  115.5 1.1 shard_map.189
  (1 shorter events, 0.0 us)
Async XLA Ops:
  3.0 5.2 %copy-start = (bf16[1,128,256]{2,1,0:T(8,128)(2,1)S(1)}, bf16[1,128,256]{2,1,0:T(8,128)(2,1)}, u32[]{:S(2)}) copy-start(bf16[1,128,256]{2,1,0:T(8,128)(2,1)} %param.14) | copy-start | bytes 196612
  3.0 5.2 %copy-start.1 = (bf16[1,128,256]{2,1,0:T(8,128)(2,1)S(1)}, bf16[1,128,256]{2,1,0:T(8,128)(2,1)}, u32[]{:S(2)}) copy-start(bf16[1,128,256]{2,1,0:T(8,128)(2,1)} %param.26) | copy-start | bytes 196612
  3.0 5.2 %copy-start.5 = (s32[1,128,32]{1,2,0:T(8,128)S(1)}, s32[1,128,32]{1,2,0:T(8,128)}, u32[]{:S(2)}) copy-start(s32[1,128,32]{1,2,0:T(8,128)} %param.17) | copy-start | bytes 49156
  3.0 5.2 %copy-start.6 = (bf16[20,256]{1,0:T(8,128)(2,1)S(1)}, bf16[20,256]{1,0:T(8,128)(2,1)}, u32[]{:S(2)}) copy-start(bf16[20,256]{1,0:T(8,128)(2,1)} %refs_8_.1) | copy-start | bytes 30724
  3.0 5.2 %copy-start.7 = (f32[1,128,32]{1,2,0:T(8,128)S(1)}, f32[1,128,32]{1,2,0:T(8,128)}, u32[]{:S(2)}) copy-start(f32[1,128,32]{1,2,0:T(8,128)} %param.20) | copy-start | bytes 49156
  3.1 20.9 %copy-start.4 = (bf16[768,24]{1,0:T(8,128)(2,1)S(1)}, bf16[768,24]{1,0:T(8,128)(2,1)}, u32[]{:S(2)}) copy-start(bf16[768,24]{1,0:T(8,128)(2,1)} %constant.13.clone.rows_ref) | copy-start | bytes 110596
  3.1 20.8 %all-to-all-start = ((bf16[4,272,256]{2,1,0:T(8,128)(2,1)}), bf16[4,272,256]{2,1,0:T(8,128)(2,1)S(1)}, u32[]{:S(2)}, u32[]{:S(2)}) async-start(bf16[4,272,256]{2,1,0:T(8,128)(2,1)} %shard_map.181), calls=%async_computation | async-start | bytes 1114112 | tf_op jit(solution)/shard_map/all_to_all | solution.py:530
  8.2 0.7 copy-start.9
  8.2 0.7 copy-start.11
  10.4 14.8 %collective-permute-start = (bf16[64,256]{1,0:T(8,128)(2,1)S(1)}, bf16[64,256]{1,0:T(8,128)(2,1)S(1)}, u32[]{:S(2)}, u32[]{:S(2)}) collective-permute-start(bf16[64,256]{1,0:T(8,128)(2,1)S(1)} %get-tuple-element.30), channel_id=1, source_target_pairs={{3,4},{7,8},{11,12},{15,16},{19,20},{23,24},{27,28},{31,32},{35,36... | collective-permute-start | bytes 98312 | tf_op jit(solution)/shard_map/ppermute | solution.py:586
  25.2 8.6 %copy-start.2 = (bf16[256,256]{1,0:T(8,128)(2,1)S(1)}, bf16[256,256]{1,0:T(8,128)(2,1)}, u32[]{:S(2)}) copy-start(bf16[256,256]{1,0:T(8,128)(2,1)} %wm_ref.1) | copy-start | bytes 393220
  25.2 8.6 %copy-start.10 = (s32[3,512]{1,0:T(4,128)S(1)}, s32[3,512]{1,0:T(4,128)}, u32[]{:S(2)}) copy-start(s32[3,512]{1,0:T(4,128)} %refs_10_.1) | copy-start | bytes 18436
  25.2 20.9 %all-to-all-start.1 = ((bf16[16,48,128]{2,1,0:T(8,128)(2,1)}), bf16[16,48,128]{2,1,0:T(8,128)(2,1)S(1)}, u32[]{:S(2)}, u32[]{:S(2)}) async-start(bf16[16,48,128]{2,1,0:T(8,128)(2,1)} %get-tuple-element.31), calls=%async_computation.1 | async-start | bytes 393216 | tf_op jit(solution)/shard_map/all_to_all | solution.py:530
  33.7 0.7 copy-start.8
  34.4 11.6 %copy-start.3 = (bf16[256,256]{1,0:T(8,128)(2,1)S(1)}, bf16[256,256]{1,0:T(8,128)(2,1)}, u32[]{:S(2)}) copy-start(bf16[256,256]{1,0:T(8,128)(2,1)} %wc_ref.3) | copy-start | bytes 393220

commit v9 on v8

--- a/solution.py
+++ b/solution.py
@@ -105,6 +105,8 @@
     list_ref,
     shared_ref,
     list_s,
+    block_s,
+    sems,
 ):
     atoms, channels = feat_ref.shape
     ghosts = list_ref.shape[1]
@@ -123,10 +125,17 @@
     left = jnp.concatenate([high, low], axis=0)
     right = jnp.concatenate([middle, list_s[...]], axis=0)
     coords = jnp.concatenate([left, right], axis=1).astype(bf16)
-    for copy in range(shared_ref.shape[0]):
-        shared_ref[copy, 0:atoms, :] = feat
-        shared_ref[copy, atoms : 2 * atoms, :] = cot
-        shared_ref[copy, 2 * atoms :, :] = coords
+    block_s[0:atoms, :] = feat
+    block_s[atoms : 2 * atoms, :] = cot
+    block_s[2 * atoms :, :] = coords
+    copies = [
+        pltpu.make_async_copy(block_s, shared_ref.at[i], sems.at[i])
+        for i in range(shared_ref.shape[0])
+    ]
+    for copy in copies:
+        copy.start()
+    for copy in copies:
+        copy.wait()
 
 
 def split_three(value):
@@ -502,14 +511,28 @@
     smem = pl.BlockSpec(memory_space=pltpu.SMEM)
     vmem = pl.BlockSpec(memory_space=pltpu.VMEM)
     if streamed:
+        n_big = n_in - in_smem
+
+        def fetching(*refs):
+            fetched, sems = refs[-n_big - 1 : -1], refs[-1]
+            copies = [
+                pltpu.make_async_copy(source, target, sems.at[i])
+                for i, (source, target) in enumerate(zip(refs[in_smem:n_in], fetched))
+            ]
+            for copy in copies:
+                copy.start()
+            for copy in copies:
+                copy.wait()
+            kernel(*refs[:in_smem], *fetched, *refs[n_in : -n_big - 1])
+
         return lambda *args: pl.pallas_call(
-            kernel,
+            fetching,
             out_shape=out_shape,
-            grid=(1,),
-            in_specs=[smem] * in_smem
-            + [pl.BlockSpec(v.shape, lambda i, n=v.ndim: (0,) * n) for v in args[in_smem:]],
-            out_specs=[vmem] * len(out_shape),
-            scratch_shapes=list(scratch),
+            in_specs=[smem] * in_smem + [pl.BlockSpec(memory_space=pl.ANY)] * n_big,
+            out_specs=[pl.BlockSpec(memory_space=pl.ANY)] * len(out_shape),
+            scratch_shapes=list(scratch)
+            + [pltpu.VMEM(v.shape, v.dtype) for v in args[in_smem:]]
+            + [pltpu.SemaphoreType.DMA((n_big,))],
             compiler_params=pltpu.CompilerParams(vmem_limit_bytes=60 * 1024 * 1024),
         )(*args)
     return pl.pallas_call(
@@ -565,7 +588,11 @@
         [shape((size_y, rows, channels), bf16)],
         1,
         5,
-        [pltpu.VMEM((8, LANES), f32)],
+        [
+            pltpu.VMEM((8, LANES), f32),
+            pltpu.VMEM((rows, channels), bf16),
+            pltpu.SemaphoreType.DMA((size_y,)),
+        ],
         streamed=True,
     )(counts, feat, cot, jnp.swapaxes(fractional, 0, 1), lists)[0]
     edges = slots * atoms

time: 117 us -> 117 us (level)
  no operation moved by 1% of the time
where the time goes in v9:
time: 117 us
  blocking collectives  68.6 us (59%)
  starting transfers between devices  27.2 us (23%)
  waiting for transfers between devices  9.29 us (8%)
  Pallas kernels  8.8 us (8%)
  between operations  1.46 us (1%)
  local copies, waits for them, and re-layouts  1.36 us (1%)
    all_to_all x4, blocking collectives, exchanged(): return lax.all_to_all(value, axis, 0, 0, tiled=True)  68.6 us
    all_to_all x2, starting transfers between devices, exchanged(): return lax.all_to_all(value, axis, 0, 0, tiled=True)  13.7 us
    ppermute x1, starting transfers between devices, body(): wrap = lax.ppermute(wrap, space, ends)  13.5 us
    all_to_all x2, waiting for transfers between devices, exchanged(): return lax.all_to_all(value, axis, 0, 0, tiled=True)  9.21 us
    pallas_call x1, Pallas kernels, body(): on_core(lambda *refs: edge_kernel(scale, *refs), [shape((atoms, channels)...  2.41 us
  transfers between devices with their start and end apart: 3, of which 2 were waited for; matrix products, arithmetic and copies ran while one was open for 0% of the time, Pallas kernels for 4%

profile of v9, /device:TPU:1, one launch (start us, length us, event | category | flops | bytes accessed | tf_op | source)
XLA Modules:
  0.0 116.7 jit_solution(4510145645153672665)
XLA Ops:
  1.3 1.8 %shard_map.181 = bf16[4,272,256]{2,1,0:T(8,128)(2,1)} custom-call(s32[1,1]{1,0:T(1,128)S(6)} %copy.20.refs_0_.count_ref, bf16[128,256]{1,0:T(8,128)(2,1)} %bitcast.16, bf16[128,256]{1,0:T(8,128)(2,1)} %bitcast.20, f32[3,1,128]{2,1,0:T(1,128)} %bitcast.29, s32[2,32]{1,0:T(2,128)} %bitcast.26), custom_call_target="tpu_custom_call" | custom-call | tf_op jit(solution)/shard_map/pallas_call | solution.py:528
  3.1 0.0 copy-start
  3.1 0.0 copy-start.1
  3.1 0.0 copy-start.5
  3.1 0.0 copy-start.6
  3.1 0.0 copy-start.7
  3.1 0.0 copy-start.4
  3.2 5.2 %all-to-all-start = ((bf16[4,272,256]{2,1,0:T(8,128)(2,1)}), bf16[4,272,256]{2,1,0:T(8,128)(2,1)S(1)}, u32[]{:S(2)}, u32[]{:S(2)}) async-start(bf16[4,272,256]{2,1,0:T(8,128)(2,1)} %shard_map.181), calls=%async_computation | async-start | bytes 1114112 | tf_op jit(solution)/shard_map/all_to_all | solution.py:553
  8.3 0.0 copy-start.9
  8.3 0.0 copy-start.11
  8.3 0.0 copy-done
  8.3 0.0 copy-done.1
  8.3 0.0 copy-done.5
  8.3 0.0 copy-done.6
  8.3 0.0 copy-done.7
  8.4 0.6 copy-done.9
  9.0 0.0 copy-done.11
  9.0 1.5 %shard_map.183 = (f32[192,256]{1,0:T(8,128)S(1)}, bf16[24,4096]{1,0:T(8,128)(2,1)S(1)}, bf16[64,256]{1,0:T(8,128)(2,1)S(1)}) custom-call(s32[1,1]{1,0:T(1,128)S(6)} %copy.20.refs_0_.count_ref, s32[1]{0:T(128)} %bitcast.place_ref.refs_0_, bf16[128,256]{1,0:T(8,128)(2,1)S(1)} %bitcast.17, s32[2,32]{1,0:T(2,128)S(1)} %bitcast.27, s32[32,128]{1,0:T(8,128)S(1)} %bitcast.23, ...), custom_call_target="tpu_custom_call" | custom-call | tf_op jit(solution)/shard_map/pallas_call | solution.py:600
  10.5 13.5 %collective-permute-start = (bf16[64,256]{1,0:T(8,128)(2,1)S(1)}, bf16[64,256]{1,0:T(8,128)(2,1)S(1)}, u32[]{:S(2)}, u32[]{:S(2)}) collective-permute-start(bf16[64,256]{1,0:T(8,128)(2,1)S(1)} %get-tuple-element.30), channel_id=1, source_target_pairs={{3,4},{7,8},{11,12},{15,16},{19,20},{23,24},{27,28},{31,32},{35,36... | collective-permute-start | bytes 98312 | tf_op jit(solution)/shard_map/ppermute | solution.py:613
  24.0 0.0 all-to-all-done.atoms_ref.refs_4_
  24.0 0.0 copy-done.4
  24.0 1.2 %shard_map.182 = (bf16[192,512]{1,0:T(8,128)(2,1)S(1)}, bf16[16,48,128]{2,1,0:T(8,128)(2,1)}) custom-call(s32[1]{0:T(128)} %bitcast.place_ref.refs_0_, bf16[4,272,256]{2,1,0:T(8,128)(2,1)S(1)} %all-to-all-done.atoms_ref.refs_4_, bf16[768,24]{1,0:T(8,128)(2,1)S(1)} %copy-done.4), custom_call_target="tpu_custom_call" | custom-call | tf_op jit(solution)/shard_map/pallas_call | solution.py:617
  25.2 0.1 collective-permute-done.refs_3_.wrap_ref
  25.3 0.0 copy-start.2
  25.3 0.0 copy-start.10
  25.3 8.5 %all-to-all-start.1 = ((bf16[16,48,128]{2,1,0:T(8,128)(2,1)}), bf16[16,48,128]{2,1,0:T(8,128)(2,1)S(1)}, u32[]{:S(2)}, u32[]{:S(2)}) async-start(bf16[16,48,128]{2,1,0:T(8,128)(2,1)} %get-tuple-element.31), calls=%async_computation.1 | async-start | bytes 393216 | tf_op jit(solution)/shard_map/all_to_all | solution.py:553
  33.8 0.0 copy-start.8
  33.8 0.0 copy-done.2
  33.8 0.0 copy-done.10
  33.9 0.7 copy-done.8
  34.5 0.0 copy-start.3
  34.5 2.4 %shard_map.184 = (f32[128,256]{1,0:T(8,128)S(1)}, f32[128,256]{1,0:T(8,128)S(1)}, bf16[32,16,128]{2,1,0:T(8,128)(2,1)S(1)}, f32[24,256]{1,0:T(8,128)S(1)}, f32[1...) custom-call(s32[1]{0:T(128)} %bitcast.place_ref.refs_0_, ...), custom_call_target="tpu_custom_call" | custom-call | tf_op jit(solution)/shard_map/pallas_call | solution.py:627
  36.9 9.2 %all-to-all-done.1.sums_ref = bf16[16,48,128]{2,1,0:T(8,128)(2,1)S(1)} async-done(((bf16[16,48,128]{2,1,0:T(8,128)(2,1)}), bf16[16,48,128]{2,1,0:T(8,128)(2,1)S(1)}, u32[]{:S(2)}, u32[]{:S(2)}) %all-to-all-start.1) | async-done | bytes 196640 | tf_op jit(solution)/shard_map/all_to_all | solution.py:553
  46.1 0.0 copy-done.3
  46.2 0.4 shard_map.185
  46.6 20.2 %all_to_all.30.parts_ref = bf16[32,40,128]{2,1,0:T(8,128)(2,1)S(1)} all-to-all(bf16[32,40,128]{2,1,0:T(8,128)(2,1)S(1)} %get-tuple-element.41), channel_id=1, replica_groups=mesh['x'=4,'core'=2,'z'=16,'y'=4] {'x','core','y'}, dimensions={0} | all-to-all | bytes 655360 | tf_op jit(solution)/shard_map/all_to_all | solution.py:553
  66.8 0.1 shard_map.186
  66.9 19.7 %all_to_all.31.parts_ref = bf16[16,88,128]{2,1,0:T(8,128)(2,1)S(1)} all-to-all(bf16[16,88,128]{2,1,0:T(8,128)(2,1)S(1)} %shard_map.186), channel_id=1, replica_groups=mesh['x'=4,'core'=2,'z'=16,'y'=4] {'z'}, dimensions={0} | all-to-all | bytes 720896 | tf_op jit(solution)/shard_map/all_to_all | solution.py:553
  86.6 0.3 shard_map.187
  86.9 12.6 %all_to_all.32.parts_ref = bf16[4,616,128]{2,1,0:T(8,128)(2,1)S(1)} all-to-all(bf16[4,616,128]{2,1,0:T(8,128)(2,1)S(1)} %shard_map.187), channel_id=1, replica_groups=mesh['x'=4,'core'=2,'z'=16,'y'=4] {'y'}, dimensions={0} | all-to-all | bytes 1261568 | tf_op jit(solution)/shard_map/all_to_all | solution.py:553
  99.5 16.1 %all_to_all.33 = bf16[8,4,40,128]{3,2,1,0:T(8,128)(2,1)S(1)} all-to-all(bf16[8,4,40,128]{3,2,1,0:T(8,128)(2,1)S(1)} %shard_map.188), channel_id=1, replica_groups=mesh['x'=4,'core'=2,'z'=16,'y'=4] {'x','core'}, dimensions={0} | all-to-all | bytes 655360 | tf_op jit(solution)/shard_map/all_to_all | solution.py:553
  115.6 1.1 shard_map.189
  (1 shorter events, 0.0 us)
Async XLA Ops:
  3.1 5.2 %copy-start = (bf16[1,128,256]{2,1,0:T(8,128)(2,1)S(1)}, bf16[1,128,256]{2,1,0:T(8,128)(2,1)}, u32[]{:S(2)}) copy-start(bf16[1,128,256]{2,1,0:T(8,128)(2,1)} %param.14) | copy-start | bytes 196612
  3.1 5.2 %copy-start.1 = (bf16[1,128,256]{2,1,0:T(8,128)(2,1)S(1)}, bf16[1,128,256]{2,1,0:T(8,128)(2,1)}, u32[]{:S(2)}) copy-start(bf16[1,128,256]{2,1,0:T(8,128)(2,1)} %param.26) | copy-start | bytes 196612
  3.1 5.2 %copy-start.5 = (s32[1,128,32]{1,2,0:T(8,128)S(1)}, s32[1,128,32]{1,2,0:T(8,128)}, u32[]{:S(2)}) copy-start(s32[1,128,32]{1,2,0:T(8,128)} %param.17) | copy-start | bytes 49156
  3.1 5.2 %copy-start.6 = (bf16[20,256]{1,0:T(8,128)(2,1)S(1)}, bf16[20,256]{1,0:T(8,128)(2,1)}, u32[]{:S(2)}) copy-start(bf16[20,256]{1,0:T(8,128)(2,1)} %refs_8_.1) | copy-start | bytes 30724
  3.1 5.2 %copy-start.7 = (f32[1,128,32]{1,2,0:T(8,128)S(1)}, f32[1,128,32]{1,2,0:T(8,128)}, u32[]{:S(2)}) copy-start(f32[1,128,32]{1,2,0:T(8,128)} %param.20) | copy-start | bytes 49156
  3.1 20.9 %copy-start.4 = (bf16[768,24]{1,0:T(8,128)(2,1)S(1)}, bf16[768,24]{1,0:T(8,128)(2,1)}, u32[]{:S(2)}) copy-start(bf16[768,24]{1,0:T(8,128)(2,1)} %constant.13.clone.rows_ref) | copy-start | bytes 110596
  3.2 20.8 %all-to-all-start = ((bf16[4,272,256]{2,1,0:T(8,128)(2,1)}), bf16[4,272,256]{2,1,0:T(8,128)(2,1)S(1)}, u32[]{:S(2)}, u32[]{:S(2)}) async-start(bf16[4,272,256]{2,1,0:T(8,128)(2,1)} %shard_map.181), calls=%async_computation | async-start | bytes 1114112 | tf_op jit(solution)/shard_map/all_to_all | solution.py:553
  8.3 0.7 copy-start.9
  8.3 0.7 copy-start.11
  10.5 14.8 %collective-permute-start = (bf16[64,256]{1,0:T(8,128)(2,1)S(1)}, bf16[64,256]{1,0:T(8,128)(2,1)S(1)}, u32[]{:S(2)}, u32[]{:S(2)}) collective-permute-start(bf16[64,256]{1,0:T(8,128)(2,1)S(1)} %get-tuple-element.30), channel_id=1, source_target_pairs={{3,4},{7,8},{11,12},{15,16},{19,20},{23,24},{27,28},{31,32},{35,36... | collective-permute-start | bytes 98312 | tf_op jit(solution)/shard_map/ppermute | solution.py:613
  25.3 8.6 %copy-start.2 = (bf16[256,256]{1,0:T(8,128)(2,1)S(1)}, bf16[256,256]{1,0:T(8,128)(2,1)}, u32[]{:S(2)}) copy-start(bf16[256,256]{1,0:T(8,128)(2,1)} %wm_ref.1) | copy-start | bytes 393220
  25.3 8.6 %copy-start.10 = (s32[3,512]{1,0:T(4,128)S(1)}, s32[3,512]{1,0:T(4,128)}, u32[]{:S(2)}) copy-start(s32[3,512]{1,0:T(4,128)} %refs_10_.1) | copy-start | bytes 18436
  25.3 20.9 %all-to-all-start.1 = ((bf16[16,48,128]{2,1,0:T(8,128)(2,1)}), bf16[16,48,128]{2,1,0:T(8,128)(2,1)S(1)}, u32[]{:S(2)}, u32[]{:S(2)}) async-start(bf16[16,48,128]{2,1,0:T(8,128)(2,1)} %get-tuple-element.31), calls=%async_computation.1 | async-start | bytes 393216 | tf_op jit(solution)/shard_map/all_to_all | solution.py:553
  33.8 0.7 copy-start.8
  34.5 11.6 %copy-start.3 = (bf16[256,256]{1,0:T(8,128)(2,1)S(1)}, bf16[256,256]{1,0:T(8,128)(2,1)}, u32[]{:S(2)}) copy-start(bf16[256,256]{1,0:T(8,128)(2,1)} %wc_ref.3) | copy-start | bytes 393220

commit v10 on v8

--- a/solution.py
+++ b/solution.py
@@ -417,7 +417,9 @@
     features = rows_of(tiles[0], tiles[1], tiles[4])
     cotangents = rows_of(tiles[2], tiles[3], tiles[5])
     high, low = split_two(features)
-    factor = dot(high, wc_ref[...]) + dot(low, wc_ref[...])
+    split = jnp.concatenate([high, low], axis=0)
+    factor = dot(split, wc_ref[...])
+    factor = factor[: high.shape[0]] + factor[high.shape[0] :]
     pulled = (weighted * factor).astype(bf16).astype(f32)
     pushed = (weighted * cotangents).astype(bf16).astype(f32)
     parts = lane_blocks(pulled[:8]) + lane_blocks(pushed[:8])
@@ -429,7 +431,7 @@
         down_ref[...], times_ref[...] * factor * cotangents, precision=lax.Precision.HIGHEST
     )
     pushed = pushed.astype(bf16)
-    charge = dot(high, pushed, TN) + dot(low, pushed, TN)
+    charge = dot(split, jnp.concatenate([pushed, pushed], axis=0), TN)
     share = channels // GRAD_CHUNKS
     small = packed(jnp.concatenate([filter_ref[...], kspace], axis=0))
     spare = GRAD_CHUNKS * share - small.shape[0]

time: 117 us -> 117 us (level)
  no operation moved by 1% of the time
where the time goes in v10:
time: 117 us
  blocking collectives  68.6 us (59%)
  starting transfers between devices  27.2 us (23%)
  waiting for transfers between devices  9.29 us (8%)
  Pallas kernels  8.69 us (7%)
  between operations  1.43 us (1%)
  local copies, waits for them, and re-layouts  1.35 us (1%)
    all_to_all x4, blocking collectives, exchanged(): return lax.all_to_all(value, axis, 0, 0, tiled=True)  68.6 us
    all_to_all x2, starting transfers between devices, exchanged(): return lax.all_to_all(value, axis, 0, 0, tiled=True)  13.7 us
    ppermute x1, starting transfers between devices, body(): wrap = lax.ppermute(wrap, space, ends)  13.5 us
    all_to_all x2, waiting for transfers between devices, exchanged(): return lax.all_to_all(value, axis, 0, 0, tiled=True)  9.21 us
    pallas_call x1, Pallas kernels, body(): on_core(lambda *refs: edge_kernel(scale, *refs), [shape((atoms, channels)...  2.41 us
  transfers between devices with their start and end apart: 3, of which 2 were waited for; matrix products, arithmetic and copies ran while one was open for 0% of the time, Pallas kernels for 4%

profile of v10, /device:TPU:1, one launch (start us, length us, event | category | flops | bytes accessed | tf_op | source)
XLA Modules:
  0.0 116.5 jit_solution(10298155702912739126)
XLA Ops:
  1.3 1.8 %shard_map.181 = bf16[4,272,256]{2,1,0:T(8,128)(2,1)} custom-call(s32[1,1]{1,0:T(1,128)S(6)} %copy.20.count_ref, bf16[128,256]{1,0:T(8,128)(2,1)} %bitcast.16, bf16[128,256]{1,0:T(8,128)(2,1)} %bitcast.20, f32[3,1,128]{2,1,0:T(1,128)} %bitcast.29, s32[2,32]{1,0:T(2,128)} %bitcast.26), custom_call_target="tpu_custom_call" | custom-call | tf_op jit(solution)/shard_map/pallas_call | solution.py:507
  3.0 0.0 copy-start
  3.0 0.0 copy-start.1
  3.0 0.0 copy-start.5
  3.0 0.0 copy-start.6
  3.0 0.0 copy-start.7
  3.1 0.0 copy-start.4
  3.1 5.2 %all-to-all-start = ((bf16[4,272,256]{2,1,0:T(8,128)(2,1)}), bf16[4,272,256]{2,1,0:T(8,128)(2,1)S(1)}, u32[]{:S(2)}, u32[]{:S(2)}) async-start(bf16[4,272,256]{2,1,0:T(8,128)(2,1)} %shard_map.181), calls=%async_computation | async-start | bytes 1114112 | tf_op jit(solution)/shard_map/all_to_all | solution.py:532
  8.2 0.0 copy-start.9
  8.2 0.0 copy-start.11
  8.2 0.0 copy-done
  8.2 0.0 copy-done.1
  8.2 0.0 copy-done.5
  8.3 0.0 copy-done.6
  8.3 0.0 copy-done.7
  8.3 0.6 copy-done.9
  8.9 0.0 copy-done.11
  8.9 1.5 %shard_map.183 = (f32[192,256]{1,0:T(8,128)S(1)}, bf16[24,4096]{1,0:T(8,128)(2,1)S(1)}, bf16[64,256]{1,0:T(8,128)(2,1)S(1)}) custom-call(s32[1,1]{1,0:T(1,128)S(6)} %copy.20.count_ref, s32[1]{0:T(128)} %bitcast.place_ref.refs_0_, bf16[128,256]{1,0:T(8,128)(2,1)S(1)} %bitcast.17, s32[2,32]{1,0:T(2,128)S(1)} %bitcast.27, s32[32,128]{1,0:T(8,128)S(1)} %bitcast.23, ...), custom_call_target="tpu_custom_call" | custom-call | tf_op jit(solution)/shard_map/pallas_call | solution.py:575
  10.4 13.5 %collective-permute-start = (bf16[64,256]{1,0:T(8,128)(2,1)S(1)}, bf16[64,256]{1,0:T(8,128)(2,1)S(1)}, u32[]{:S(2)}, u32[]{:S(2)}) collective-permute-start(bf16[64,256]{1,0:T(8,128)(2,1)S(1)} %get-tuple-element.30), channel_id=1, source_target_pairs={{3,4},{7,8},{11,12},{15,16},{19,20},{23,24},{27,28},{31,32},{35,36... | collective-permute-start | bytes 98312 | tf_op jit(solution)/shard_map/ppermute | solution.py:588
  23.9 0.0 all-to-all-done.atoms_ref.refs_4_
  23.9 0.0 copy-done.4
  23.9 1.2 %shard_map.182 = (bf16[192,512]{1,0:T(8,128)(2,1)S(1)}, bf16[16,48,128]{2,1,0:T(8,128)(2,1)}) custom-call(s32[1]{0:T(128)} %bitcast.place_ref.refs_0_, bf16[4,272,256]{2,1,0:T(8,128)(2,1)S(1)} %all-to-all-done.atoms_ref.refs_4_, bf16[768,24]{1,0:T(8,128)(2,1)S(1)} %copy-done.4), custom_call_target="tpu_custom_call" | custom-call | tf_op jit(solution)/shard_map/pallas_call | solution.py:592
  25.1 0.1 collective-permute-done.refs_3_.wrap_ref
  25.2 0.0 copy-start.2
  25.2 0.0 copy-start.10
  25.2 8.5 %all-to-all-start.1 = ((bf16[16,48,128]{2,1,0:T(8,128)(2,1)}), bf16[16,48,128]{2,1,0:T(8,128)(2,1)S(1)}, u32[]{:S(2)}, u32[]{:S(2)}) async-start(bf16[16,48,128]{2,1,0:T(8,128)(2,1)} %get-tuple-element.31), calls=%async_computation.1 | async-start | bytes 393216 | tf_op jit(solution)/shard_map/all_to_all | solution.py:532
  33.7 0.0 copy-start.8
  33.7 0.0 copy-done.2
  33.8 0.0 copy-done.10
  33.8 0.7 copy-done.8
  34.4 0.0 copy-start.3
  34.4 2.4 %shard_map.184 = (f32[128,256]{1,0:T(8,128)S(1)}, f32[128,256]{1,0:T(8,128)S(1)}, bf16[32,16,128]{2,1,0:T(8,128)(2,1)S(1)}, f32[24,256]{1,0:T(8,128)S(1)}, f32[1...) custom-call(s32[1]{0:T(128)} %bitcast.place_ref.refs_0_, ...), custom_call_target="tpu_custom_call" | custom-call | tf_op jit(solution)/shard_map/pallas_call | solution.py:602
  36.9 9.2 %all-to-all-done.1.sums_ref = bf16[16,48,128]{2,1,0:T(8,128)(2,1)S(1)} async-done(((bf16[16,48,128]{2,1,0:T(8,128)(2,1)}), bf16[16,48,128]{2,1,0:T(8,128)(2,1)S(1)}, u32[]{:S(2)}, u32[]{:S(2)}) %all-to-all-start.1) | async-done | bytes 196640 | tf_op jit(solution)/shard_map/all_to_all | solution.py:532
  46.1 0.0 copy-done.3
  46.1 0.4 shard_map.185
  46.4 20.2 %all_to_all.30.parts_ref = bf16[32,40,128]{2,1,0:T(8,128)(2,1)S(1)} all-to-all(bf16[32,40,128]{2,1,0:T(8,128)(2,1)S(1)} %get-tuple-element.41), channel_id=1, replica_groups=mesh['x'=4,'core'=2,'z'=16,'y'=4] {'x','core','y'}, dimensions={0} | all-to-all | bytes 655360 | tf_op jit(solution)/shard_map/all_to_all | solution.py:532
  66.6 0.1 shard_map.186
  66.7 19.7 %all_to_all.31.parts_ref = bf16[16,88,128]{2,1,0:T(8,128)(2,1)S(1)} all-to-all(bf16[16,88,128]{2,1,0:T(8,128)(2,1)S(1)} %shard_map.186), channel_id=1, replica_groups=mesh['x'=4,'core'=2,'z'=16,'y'=4] {'z'}, dimensions={0} | all-to-all | bytes 720896 | tf_op jit(solution)/shard_map/all_to_all | solution.py:532
  86.4 0.3 shard_map.187
  86.8 12.6 %all_to_all.32.parts_ref = bf16[4,616,128]{2,1,0:T(8,128)(2,1)S(1)} all-to-all(bf16[4,616,128]{2,1,0:T(8,128)(2,1)S(1)} %shard_map.187), channel_id=1, replica_groups=mesh['x'=4,'core'=2,'z'=16,'y'=4] {'y'}, dimensions={0} | all-to-all | bytes 1261568 | tf_op jit(solution)/shard_map/all_to_all | solution.py:532
  99.4 16.1 %all_to_all.33 = bf16[8,4,40,128]{3,2,1,0:T(8,128)(2,1)S(1)} all-to-all(bf16[8,4,40,128]{3,2,1,0:T(8,128)(2,1)S(1)} %shard_map.188), channel_id=1, replica_groups=mesh['x'=4,'core'=2,'z'=16,'y'=4] {'x','core'}, dimensions={0} | all-to-all | bytes 655360 | tf_op jit(solution)/shard_map/all_to_all | solution.py:532
  115.5 1.1 shard_map.189
  (1 shorter events, 0.0 us)
Async XLA Ops:
  3.0 5.2 %copy-start = (bf16[1,128,256]{2,1,0:T(8,128)(2,1)S(1)}, bf16[1,128,256]{2,1,0:T(8,128)(2,1)}, u32[]{:S(2)}) copy-start(bf16[1,128,256]{2,1,0:T(8,128)(2,1)} %param.14) | copy-start | bytes 196612
  3.0 5.2 %copy-start.1 = (bf16[1,128,256]{2,1,0:T(8,128)(2,1)S(1)}, bf16[1,128,256]{2,1,0:T(8,128)(2,1)}, u32[]{:S(2)}) copy-start(bf16[1,128,256]{2,1,0:T(8,128)(2,1)} %param.26) | copy-start | bytes 196612
  3.0 5.2 %copy-start.5 = (s32[1,128,32]{1,2,0:T(8,128)S(1)}, s32[1,128,32]{1,2,0:T(8,128)}, u32[]{:S(2)}) copy-start(s32[1,128,32]{1,2,0:T(8,128)} %param.17) | copy-start | bytes 49156
  3.0 5.2 %copy-start.6 = (bf16[20,256]{1,0:T(8,128)(2,1)S(1)}, bf16[20,256]{1,0:T(8,128)(2,1)}, u32[]{:S(2)}) copy-start(bf16[20,256]{1,0:T(8,128)(2,1)} %refs_8_.1) | copy-start | bytes 30724
  3.0 5.2 %copy-start.7 = (f32[1,128,32]{1,2,0:T(8,128)S(1)}, f32[1,128,32]{1,2,0:T(8,128)}, u32[]{:S(2)}) copy-start(f32[1,128,32]{1,2,0:T(8,128)} %param.20) | copy-start | bytes 49156
  3.1 20.9 %copy-start.4 = (bf16[768,24]{1,0:T(8,128)(2,1)S(1)}, bf16[768,24]{1,0:T(8,128)(2,1)}, u32[]{:S(2)}) copy-start(bf16[768,24]{1,0:T(8,128)(2,1)} %constant.13.clone.rows_ref) | copy-start | bytes 110596
  3.1 20.8 %all-to-all-start = ((bf16[4,272,256]{2,1,0:T(8,128)(2,1)}), bf16[4,272,256]{2,1,0:T(8,128)(2,1)S(1)}, u32[]{:S(2)}, u32[]{:S(2)}) async-start(bf16[4,272,256]{2,1,0:T(8,128)(2,1)} %shard_map.181), calls=%async_computation | async-start | bytes 1114112 | tf_op jit(solution)/shard_map/all_to_all | solution.py:532
  8.2 0.7 copy-start.9
  8.2 0.7 copy-start.11
  10.4 14.8 %collective-permute-start = (bf16[64,256]{1,0:T(8,128)(2,1)S(1)}, bf16[64,256]{1,0:T(8,128)(2,1)S(1)}, u32[]{:S(2)}, u32[]{:S(2)}) collective-permute-start(bf16[64,256]{1,0:T(8,128)(2,1)S(1)} %get-tuple-element.30), channel_id=1, source_target_pairs={{3,4},{7,8},{11,12},{15,16},{19,20},{23,24},{27,28},{31,32},{35,36... | collective-permute-start | bytes 98312 | tf_op jit(solution)/shard_map/ppermute | solution.py:588
  25.2 8.6 %copy-start.2 = (bf16[256,256]{1,0:T(8,128)(2,1)S(1)}, bf16[256,256]{1,0:T(8,128)(2,1)}, u32[]{:S(2)}) copy-start(bf16[256,256]{1,0:T(8,128)(2,1)} %wm_ref.1) | copy-start | bytes 393220
  25.2 8.6 %copy-start.10 = (s32[3,512]{1,0:T(4,128)S(1)}, s32[3,512]{1,0:T(4,128)}, u32[]{:S(2)}) copy-start(s32[3,512]{1,0:T(4,128)} %refs_10_.1) | copy-start | bytes 18436
  25.2 20.9 %all-to-all-start.1 = ((bf16[16,48,128]{2,1,0:T(8,128)(2,1)}), bf16[16,48,128]{2,1,0:T(8,128)(2,1)S(1)}, u32[]{:S(2)}, u32[]{:S(2)}) async-start(bf16[16,48,128]{2,1,0:T(8,128)(2,1)} %get-tuple-element.31), calls=%async_computation.1 | async-start | bytes 393216 | tf_op jit(solution)/shard_map/all_to_all | solution.py:532
  33.7 0.7 copy-start.8
  34.4 11.6 %copy-start.3 = (bf16[256,256]{1,0:T(8,128)(2,1)S(1)}, bf16[256,256]{1,0:T(8,128)(2,1)}, u32[]{:S(2)}) copy-start(bf16[256,256]{1,0:T(8,128)(2,1)} %wc_ref.3) | copy-start | bytes 393220
